TPU v7x, 32 devices: a whole 2x2x4 slice. The times are simulated.
32 devices in a mesh: fsdp: 4 (over y, x), rep: 8 (over z, core).
Axes of the slice: x: 2, y: 2, z: 4, core: 2. Of those that a mesh axis runs over, the one named last changes fastest.
Arguments:
- tokens: bfloat16 [10240, 1600], P(('rep', 'fsdp')), may hold values from -6 to 6
- lengths: int32 [8, 4], P('rep'), may hold values from 1 to 1277, as said below
- w_query: bfloat16 [2560000], P(('fsdp', 'rep')), may hold values from -0.15625 to 0.15625
- w_key: bfloat16 [512000], P(('fsdp', 'rep')), may hold values from -0.15625 to 0.15625
- w_value: bfloat16 [512000], P(('fsdp', 'rep')), may hold values from -0.15625 to 0.15625
- w_attn_out: bfloat16 [2560000], P(('fsdp', 'rep')), may hold values from -0.15625 to 0.15625
- w_inner: bfloat16 [5120000], P(('fsdp', 'rep')), may hold values from -0.15625 to 0.15625
- w_gate_z: bfloat16 [5120000], P(('fsdp', 'rep')), may hold values from -0.15625 to 0.15625
- w_bc: bfloat16 [51200], P(('fsdp', 'rep')), may hold values from -0.15625 to 0.15625
- w_step: bfloat16 [80000], P(('fsdp', 'rep')), may hold values from -0.15625 to 0.15625
- w_mamba_out: bfloat16 [5120000], P(('fsdp', 'rep')), may hold values from -0.109375 to 0.109375
- w_ffn_gate: bfloat16 [8806400], P(('fsdp', 'rep')), may hold values from -0.15625 to 0.15625
- w_ffn_up: bfloat16 [8806400], P(('fsdp', 'rep')), may hold values from -0.15625 to 0.15625
- w_ffn_down: bfloat16 [8806400], P(('fsdp', 'rep')), may hold values from -0.078125 to 0.078125
- norm_gains: float32 [4, 1600], replicated, may hold values from 0.5 to 1.5
- step_bias: float32 [50], replicated, may hold values from -2 to 1
- decay_log: float32 [50], replicated, may hold values from -9 to -3
- skip_gain: float32 [50], replicated, may hold values from 0.5 to 1.5
- cotangent: bfloat16 [10240, 1600], P(('rep', 'fsdp')), may hold values from -6 to 6
Outputs:
- output: bfloat16 [10240, 1600], P(('rep', 'fsdp'))
- grad_tokens: float32 [10240, 1600], P(('rep', 'fsdp'))
- grad_w_query: float32 [2560000], P(('fsdp', 'rep'))
- grad_w_key: float32 [512000], P(('fsdp', 'rep'))
- grad_w_value: float32 [512000], P(('fsdp', 'rep'))
- grad_w_attn_out: float32 [2560000], P(('fsdp', 'rep'))
- grad_w_inner: float32 [5120000], P(('fsdp', 'rep'))
- grad_w_gate_z: float32 [5120000], P(('fsdp', 'rep'))
- grad_w_bc: float32 [51200], P(('fsdp', 'rep'))
- grad_w_step: float32 [80000], P(('fsdp', 'rep'))
- grad_w_mamba_out: float32 [5120000], P(('fsdp', 'rep'))
- grad_w_ffn_gate: float32 [8806400], P(('fsdp', 'rep'))
- grad_w_ffn_up: float32 [8806400], P(('fsdp', 'rep'))
- grad_w_ffn_down: float32 [8806400], P(('fsdp', 'rep'))
- grad_norm_gains: float32 [4, 1600], replicated
- grad_step_bias: float32 [50], replicated
- grad_decay_log: float32 [50], replicated
- grad_skip_gain: float32 [50], replicated
Inputs may be any that keep to these rules, and one draw needn't show every extreme that they name: Each row gives the lengths of the 4 sequences of one group of 1280 tokens and sums to 1280; the first sequence is 1 to 63 long, the third and fourth 1 to 31, so the second starts on the group's first device and ends on its last.
All inputs are finite; a program needn't handle non-finite values.
Results may differ from a plain program's by a relative error of at most 0.022.
Values may be sent and summed in bfloat16 or wider, within the bound.
No kernel may reach another device: no remote copies, remote signals or barrier semaphores. Data moves between devices by JAX's collectives and lax.ppermute only.
A program may use at most 704 MiB of HBM per device.

v0:
```python
import math

import jax
import jax.numpy as jnp
from jax import lax
from jax.sharding import PartitionSpec as P

D = 1600
QUERY_HEADS = 25
KEY_VALUE_HEADS = 5
HEAD_SIZE = 64
WIN = 1024
MI = 3200
NS = 16
FF = 5504
MH = 50
STRETCH = 64


epsilon = 1e-06
masked_score = -1e30
highest = lax.Precision.HIGHEST


def shifted(value, axis, by):
    devices = lax.axis_size(axis)
    pairs = [(i, i + by) for i in range(devices) if 0 <= i + by < devices]
    return lax.ppermute(value, axis, pairs)


def prefix(part, axis, combine, identity):
    place = lax.axis_index(axis)
    gathered = jax.tree.map(lambda a: lax.all_gather(a, axis), part)
    state = jax.tree.map(lambda a, e: jnp.zeros_like(a) + jnp.asarray(e, a.dtype), part, identity)

    def one(step, state):
        return combine(
            state, jax.tree.map(lambda a: lax.dynamic_index_in_dim(a, step, 0, False), gathered)
        )

    return lax.fori_loop(0, place, one, state)


def prefix_2(value, axis, combine, identity):
    devices, mine = (lax.axis_size(axis), lax.axis_index(axis))
    everything = jax.tree.map(
        lambda part, kind: lax.all_gather(part.astype(kind), axis),
        value,
        (jnp.bfloat16, jnp.bfloat16),
    )
    start = jax.tree.map(
        lambda part, zero: jnp.broadcast_to(jnp.asarray(zero, part.dtype), part.shape),
        value,
        identity,
    )

    def step(k, before):
        at = devices - 1 - k
        reached = at > mine
        new = combine(
            before, jax.tree.map(lambda part, own: part[at].astype(own.dtype), everything, value)
        )
        return jax.tree.map(lambda a, b: jnp.where(reached, a, b), new, before)

    return lax.fori_loop(0, devices, step, start)


def rms_scale(value_rows, gain):
    return (
        value_rows
        * lax.rsqrt(jnp.mean(value_rows * value_rows, axis=-1, keepdims=True) + epsilon)
        * gain
    )


def norm_back(grad_in, value_rows, gain):
    factor = lax.rsqrt(jnp.mean(value_rows * value_rows, axis=-1, keepdims=True) + epsilon)
    weighted = grad_in * gain
    spread = jnp.mean(weighted * value_rows, axis=-1, keepdims=True)
    return (
        factor * weighted - value_rows * factor * factor * factor * spread,
        jnp.sum(grad_in * value_rows * factor, axis=0),
    )


def silu(value_rows):
    return value_rows * jax.nn.sigmoid(value_rows)


def silu_slope(value_rows):
    sigmoid_v = jax.nn.sigmoid(value_rows)
    return sigmoid_v * (1.0 + value_rows * (1.0 - sigmoid_v))


def apply_projection(value_rows, matrix):
    return jnp.dot(value_rows, matrix, preferred_element_type=jnp.float32)


def project_back(grad_in, matrix):
    return lax.dot_general(
        grad_in, matrix, (((1,), (1,)), ((), ())), preferred_element_type=jnp.float32
    )


def weight_grad(value_rows, grad_in):
    return lax.dot_general(
        value_rows, grad_in, (((0,), (0,)), ((), ())), preferred_element_type=jnp.float32
    )


def sequence_layout(seq_lengths, position):
    seq_ends = jnp.cumsum(seq_lengths, dtype=jnp.int32)
    seq_starts = seq_ends - seq_lengths
    segment = jnp.sum(
        (position[:, None] >= seq_ends[None, :]).astype(jnp.int32), axis=1, dtype=jnp.int32
    )
    labels = jnp.arange(seq_lengths.shape[0], dtype=jnp.int32)
    seq_begin = jnp.sum(
        jnp.where(segment[:, None] == labels[None, :], seq_starts[None, :], 0),
        axis=1,
        dtype=jnp.int32,
    )
    return (segment, (position - seq_begin).astype(jnp.float32))


def apply_rotary(value_rows, place, sign):
    half_width = value_rows.shape[-1] // 2
    frequency = jnp.exp(
        jnp.arange(half_width, dtype=jnp.float32)
        * (-2.0 * math.log(10000.0) / value_rows.shape[-1])
    )
    angles = place[:, None] * frequency[None, :]
    cosine = jnp.cos(angles)[:, None, :]
    sine_part = sign * jnp.sin(angles)[:, None, :]
    first_half = value_rows[..., :half_width]
    second_half = value_rows[..., half_width:]
    return jnp.concatenate(
        [
            first_half * cosine - second_half * sine_part,
            second_half * cosine + first_half * sine_part,
        ],
        axis=-1,
    )


def stretch_scan(carry, block):
    state, seg_prev = carry
    inner_q, b_q, c_q, rate_q, step_q, seg_q = block
    length = inner_q.shape[0]
    cumul = jnp.cumsum(rate_q, axis=0)
    order = jnp.arange(length, dtype=jnp.int32)
    live = (seg_q[:, None] == seg_q[None, :]) & (order[:, None] >= order[None, :])
    spread = jnp.where(live[:, :, None], cumul[:, None, :] - cumul[None, :, :], 0.0)
    decay = jnp.where(live[:, :, None], jnp.exp(spread), 0.0)
    intersection = jnp.dot(c_q, b_q.T, precision=highest, preferred_element_type=jnp.float32)
    mixing = decay * intersection[:, :, None] * step_q[None, :, :]
    result = jnp.einsum("ijh,jhp->ihp", mixing, inner_q, precision=highest)
    carried = jnp.where((seg_q == seg_prev)[:, None], jnp.exp(cumul), 0.0)
    result = result + carried[:, :, None] * jnp.einsum("in,hpn->ihp", c_q, state, precision=highest)
    tail_sum = cumul[-1]
    last_seg = seg_q[-1]
    ending = (
        jnp.where((seg_q == last_seg)[:, None], jnp.exp(tail_sum[None, :] - cumul), 0.0) * step_q
    )
    fresh = jnp.einsum("jh,jhp,jn->hpn", ending, inner_q, b_q, precision=highest)
    fresh = fresh + jnp.where(last_seg == seg_prev, jnp.exp(tail_sum), 0.0)[:, None, None] * state
    return ((fresh, last_seg), result)


def local_scan(inner_f, b_vals, c_vals, rates, step_size, segment, before_seg):
    item_count = inner_f.shape[0]
    stretches = item_count // STRETCH
    blocks = (
        inner_f.reshape(stretches, STRETCH, MH, HEAD_SIZE),
        b_vals.reshape(stretches, STRETCH, NS),
        c_vals.reshape(stretches, STRETCH, NS),
        rates.reshape(stretches, STRETCH, MH),
        step_size.reshape(stretches, STRETCH, MH),
        segment.reshape(stretches, STRETCH),
    )
    start = (jnp.zeros((MH, HEAD_SIZE, NS), jnp.float32), before_seg)
    (state_end, _), ssm_out = lax.scan(stretch_scan, start, blocks)
    carry_mult = jnp.where(segment[-1] == before_seg, jnp.exp(jnp.sum(rates, axis=0)), 0.0)
    return (ssm_out.reshape(item_count, MH, HEAD_SIZE), state_end, carry_mult)


def combine_states(earlier, later):
    return (earlier[0] * later[0], earlier[1] * later[0][:, None, None] + later[1])


def combine_back(earlier, later):
    return (earlier[0] * later[0], later[1] + later[0][:, None, None] * earlier[1])


def attend(q_group, k_block, v_block, visible, scale):
    scores = jnp.einsum("tgd,kd->gtk", q_group, k_block, preferred_element_type=jnp.float32) * scale
    scores = jnp.where(visible[None], scores, masked_score)
    top_score = jnp.max(scores, axis=-1, keepdims=True)
    exponent = jnp.exp(scores - top_score)
    row_total = jnp.sum(exponent, axis=-1, keepdims=True)
    probs_low = (exponent / row_total).astype(jnp.bfloat16)
    result = jnp.einsum("gtk,kd->tgd", probs_low, v_block, preferred_element_type=jnp.float32)
    return (result, top_score + jnp.log(row_total))


def unflatten(flats, shapes):
    return tuple((flat.reshape(shape) for flat, shape in zip(flats, shapes)))


def local(
    tokens,
    lengths,
    w_query,
    w_key,
    w_value,
    w_attn_out,
    w_inner,
    w_gate_z,
    w_bc,
    w_step,
    w_mamba_out,
    w_ffn_gate,
    w_ffn_up,
    w_ffn_down,
    norm_gains,
    step_bias,
    decay_log,
    skip_gain,
    cotangent,
):
    count_of_rows = tokens.shape[0]
    key_value_width = KEY_VALUE_HEADS * HEAD_SIZE
    heads_per_group = QUERY_HEADS // KEY_VALUE_HEADS
    scale = HEAD_SIZE ** (-0.5)
    mixer_shapes = (
        (D, D),
        (D, key_value_width),
        (D, key_value_width),
        (D, D),
        (D, MI),
        (D, MI),
        (D, 2 * NS),
        (D, MH),
        (MI, D),
    )
    ffn_shapes = ((D, FF), (D, FF), (FF, D))
    mixer_full = unflatten(
        (
            lax.all_gather(w_query, ("fsdp", "rep"), axis=0, tiled=True),
            lax.all_gather(w_key, ("fsdp", "rep"), axis=0, tiled=True),
            lax.all_gather(w_value, ("fsdp", "rep"), axis=0, tiled=True),
            lax.all_gather(w_attn_out, ("fsdp", "rep"), axis=0, tiled=True),
            lax.all_gather(w_inner, ("fsdp", "rep"), axis=0, tiled=True),
            lax.all_gather(w_gate_z, ("fsdp", "rep"), axis=0, tiled=True),
            lax.all_gather(w_bc, ("fsdp", "rep"), axis=0, tiled=True),
            lax.all_gather(w_step, ("fsdp", "rep"), axis=0, tiled=True),
            lax.all_gather(w_mamba_out, ("fsdp", "rep"), axis=0, tiled=True),
        ),
        mixer_shapes,
    )
    mat_q, key_projection, mat_v, mat_o, mat_x, mat_z, mat_bc, mat_dt, mat_om = mixer_full
    span = lax.axis_size("fsdp")
    dev_index = lax.axis_index("fsdp")
    seq_lengths = lengths[0]
    q_index = dev_index * count_of_rows + jnp.arange(count_of_rows, dtype=jnp.int32)
    q_seg, query_position = sequence_layout(seq_lengths, q_index)
    prior_index = jnp.reshape(dev_index * count_of_rows - 1, (1,))
    before_seg = jnp.where(dev_index == 0, -1, sequence_layout(seq_lengths, prior_index)[0][0])
    rim = min(span - 1, (WIN + count_of_rows - 2) // count_of_rows)
    k_index = (dev_index - rim) * count_of_rows + jnp.arange(
        (rim + 1) * count_of_rows, dtype=jnp.int32
    )
    k_seg, _ = sequence_layout(seq_lengths, k_index)
    distance = q_index[:, None] - k_index[None, :]
    visible = (
        (q_seg[:, None] == k_seg[None, :])
        & (distance >= 0)
        & (distance < WIN)
        & (k_index[None, :] >= 0)
    )
    x_float = tokens.astype(jnp.float32)
    normalized_input = rms_scale(x_float, norm_gains[0]).astype(jnp.bfloat16)
    q_raw = apply_projection(normalized_input, mat_q).reshape(count_of_rows, QUERY_HEADS, HEAD_SIZE)
    key_unrotated = apply_projection(normalized_input, key_projection).reshape(
        count_of_rows, KEY_VALUE_HEADS, HEAD_SIZE
    )
    v_raw = apply_projection(normalized_input, mat_v)
    query_rows = apply_rotary(q_raw, query_position, 1.0).astype(jnp.bfloat16)
    keys_rot = (
        apply_rotary(key_unrotated, query_position, 1.0)
        .astype(jnp.bfloat16)
        .reshape(count_of_rows, key_value_width)
    )
    pairs = jnp.concatenate([keys_rot, v_raw.astype(jnp.bfloat16)], axis=1)
    earlier = [shifted(pairs, "fsdp", offset) for offset in range(rim, 0, -1)]
    context = jnp.concatenate(earlier + [pairs], axis=0)
    head_outs = []
    log_totals = []
    for key_value_head in range(KEY_VALUE_HEADS):
        q_group = query_rows[
            :, key_value_head * heads_per_group : (key_value_head + 1) * heads_per_group, :
        ]
        k_block = context[:, key_value_head * HEAD_SIZE : (key_value_head + 1) * HEAD_SIZE]
        v_block = context[
            :,
            key_value_width
            + key_value_head * HEAD_SIZE : key_value_width
            + (key_value_head + 1) * HEAD_SIZE,
        ]
        head_out, log_total = attend(q_group, k_block, v_block, visible, scale)
        head_outs.append(head_out)
        log_totals.append(log_total)
    attn_vals = jnp.concatenate(head_outs, axis=1).reshape(count_of_rows, D).astype(jnp.bfloat16)
    attn_proj = apply_projection(attn_vals, mat_o)
    branch_attn = rms_scale(attn_proj, norm_gains[1])
    inner_vals = apply_projection(normalized_input, mat_x).astype(jnp.bfloat16)
    gate_z = apply_projection(normalized_input, mat_z)
    bc_vals = apply_projection(normalized_input, mat_bc).astype(jnp.bfloat16)
    step_raw = apply_projection(normalized_input, mat_dt)
    step_size = jax.nn.softplus(step_raw + step_bias)
    rates = -step_size * jnp.exp(decay_log)
    inner_f = inner_vals.astype(jnp.float32).reshape(count_of_rows, MH, HEAD_SIZE)
    b_vals = bc_vals[:, :NS].astype(jnp.float32)
    c_vals = bc_vals[:, NS:].astype(jnp.float32)
    y_local, state_local, carry_mult = local_scan(
        inner_f, b_vals, c_vals, rates, step_size, q_seg, before_seg
    )
    mult_in, state_in = prefix(
        (carry_mult, state_local),
        "fsdp",
        combine_states,
        (jnp.ones_like(carry_mult), jnp.zeros_like(state_local)),
    )
    reach = jnp.where((q_seg == before_seg)[:, None], jnp.exp(jnp.cumsum(rates, axis=0)), 0.0)
    y_ssm = y_local + reach[:, :, None] * jnp.einsum(
        "in,hpn->ihp", c_vals, state_in, precision=highest
    )
    y_total = (y_ssm + skip_gain[None, :, None] * inner_f).reshape(count_of_rows, MI)
    mixed_in = (y_total * silu(gate_z)).astype(jnp.bfloat16)
    mamba_proj = apply_projection(mixed_in, mat_om)
    branch_mamba = rms_scale(mamba_proj, norm_gains[2])
    mix = x_float + 0.5 * (branch_attn + branch_mamba)
    ffn_full = unflatten(
        (
            lax.all_gather(w_ffn_gate, ("fsdp", "rep"), axis=0, tiled=True),
            lax.all_gather(w_ffn_up, ("fsdp", "rep"), axis=0, tiled=True),
            lax.all_gather(w_ffn_down, ("fsdp", "rep"), axis=0, tiled=True),
        ),
        ffn_shapes,
    )
    mat_g, mat_u, mat_d = ffn_full
    normed_two = rms_scale(mix, norm_gains[3]).astype(jnp.bfloat16)
    fgate = apply_projection(normed_two, mat_g)
    fup = apply_projection(normed_two, mat_u)
    hidden = (silu(fgate) * fup).astype(jnp.bfloat16)
    output = (mix + apply_projection(hidden, mat_d)).astype(jnp.bfloat16)
    ffn_back = unflatten(
        (
            lax.all_gather(w_ffn_gate, ("fsdp", "rep"), axis=0, tiled=True),
            lax.all_gather(w_ffn_up, ("fsdp", "rep"), axis=0, tiled=True),
            lax.all_gather(w_ffn_down, ("fsdp", "rep"), axis=0, tiled=True),
        ),
        ffn_shapes,
    )
    back_g, back_u, back_d = ffn_back
    grad_down = weight_grad(hidden, cotangent)
    g_hidden = project_back(cotangent, back_d)
    g_fgate = (g_hidden * fup * silu_slope(fgate)).astype(jnp.bfloat16)
    g_fup = (g_hidden * silu(fgate)).astype(jnp.bfloat16)
    grad_gate = weight_grad(normed_two, g_fgate)
    grad_up = weight_grad(normed_two, g_fup)
    g_normed_two = project_back(g_fgate, back_g) + project_back(g_fup, back_u)
    g_mix_norm, g_gain_three = norm_back(g_normed_two, mix, norm_gains[3])
    g_mix = cotangent.astype(jnp.float32) + g_mix_norm
    ffn_grads = (
        lax.psum_scatter(grad_gate.reshape(-1), ("fsdp", "rep"), scatter_dimension=0, tiled=True),
        lax.psum_scatter(grad_up.reshape(-1), ("fsdp", "rep"), scatter_dimension=0, tiled=True),
        lax.psum_scatter(grad_down.reshape(-1), ("fsdp", "rep"), scatter_dimension=0, tiled=True),
    )
    mixer_back = unflatten(
        (
            lax.all_gather(w_query, ("fsdp", "rep"), axis=0, tiled=True),
            lax.all_gather(w_key, ("fsdp", "rep"), axis=0, tiled=True),
            lax.all_gather(w_value, ("fsdp", "rep"), axis=0, tiled=True),
            lax.all_gather(w_attn_out, ("fsdp", "rep"), axis=0, tiled=True),
            lax.all_gather(w_inner, ("fsdp", "rep"), axis=0, tiled=True),
            lax.all_gather(w_gate_z, ("fsdp", "rep"), axis=0, tiled=True),
            lax.all_gather(w_bc, ("fsdp", "rep"), axis=0, tiled=True),
            lax.all_gather(w_step, ("fsdp", "rep"), axis=0, tiled=True),
            lax.all_gather(w_mamba_out, ("fsdp", "rep"), axis=0, tiled=True),
        ),
        mixer_shapes,
    )
    back_q, back_k, back_v, back_o, back_x, back_z, back_bc, back_dt, back_om = mixer_back
    g_branch = 0.5 * g_mix
    g_attn_proj, g_gain_one = norm_back(g_branch, attn_proj, norm_gains[1])
    g_attn_proj = g_attn_proj.astype(jnp.bfloat16)
    grad_attn_out = weight_grad(attn_vals, g_attn_proj)
    g_attn_vals = (
        project_back(g_attn_proj, back_o)
        .astype(jnp.bfloat16)
        .reshape(count_of_rows, QUERY_HEADS, HEAD_SIZE)
    )
    g_mamba_proj, g_gain_two = norm_back(g_branch, mamba_proj, norm_gains[2])
    g_mamba_proj = g_mamba_proj.astype(jnp.bfloat16)
    grad_mamba_out = weight_grad(mixed_in, g_mamba_proj)
    g_gated = project_back(g_mamba_proj, back_om)
    g_y = (g_gated * silu(gate_z)).reshape(count_of_rows, MH, HEAD_SIZE)
    g_gate_z = (g_gated * y_total * silu_slope(gate_z)).astype(jnp.bfloat16)
    g_skip = jnp.sum(g_y * inner_f, axis=(0, 2))
    g_into = jnp.einsum("ih,ihp,in->hpn", reach, g_y, c_vals, precision=highest)
    mult_back, state_back = prefix_2(
        (carry_mult, g_into),
        "fsdp",
        combine_back,
        (jnp.ones_like(carry_mult), jnp.zeros_like(g_into)),
    )
    g_mult = jnp.sum(state_back * state_in, axis=(1, 2))

    def ssm_full(inner_arg, b_arg, c_arg, rate_arg, step_arg, state_arg):
        local_out, local_state, local_mult = local_scan(
            inner_arg, b_arg, c_arg, rate_arg, step_arg, q_seg, before_seg
        )
        reach_arg = jnp.where(
            (q_seg == before_seg)[:, None], jnp.exp(jnp.cumsum(rate_arg, axis=0)), 0.0
        )
        total_out = local_out + reach_arg[:, :, None] * jnp.einsum(
            "in,hpn->ihp", c_arg, state_arg, precision=highest
        )
        return (total_out, local_state, local_mult)

    _, ssm_pull = jax.vjp(ssm_full, inner_f, b_vals, c_vals, rates, step_size, state_in)
    g_inner, g_b, g_c, g_rates, g_step, _ = ssm_pull((g_y, state_back, g_mult))
    g_inner_low = (
        (g_inner + skip_gain[None, :, None] * g_y).reshape(count_of_rows, MI).astype(jnp.bfloat16)
    )
    g_bc = jnp.concatenate([g_b, g_c], axis=1).astype(jnp.bfloat16)
    g_decay = jnp.sum(g_rates * rates, axis=0)
    g_step_float = (g_step - g_rates * jnp.exp(decay_log)) * jax.nn.sigmoid(step_raw + step_bias)
    g_bias = jnp.sum(g_step_float, axis=0)
    g_step_raw = g_step_float.astype(jnp.bfloat16)
    g_query_heads = []
    g_key_heads = []
    g_value_heads = []
    for key_value_head in range(KEY_VALUE_HEADS):
        q_group = query_rows[
            :, key_value_head * heads_per_group : (key_value_head + 1) * heads_per_group, :
        ]
        k_block = context[:, key_value_head * HEAD_SIZE : (key_value_head + 1) * HEAD_SIZE]
        v_block = context[
            :,
            key_value_width
            + key_value_head * HEAD_SIZE : key_value_width
            + (key_value_head + 1) * HEAD_SIZE,
        ]
        g_out = g_attn_vals[
            :, key_value_head * heads_per_group : (key_value_head + 1) * heads_per_group, :
        ]
        scores = (
            jnp.einsum("tgd,kd->gtk", q_group, k_block, preferred_element_type=jnp.float32) * scale
        )
        probs = jnp.exp(jnp.where(visible[None], scores, masked_score) - log_totals[key_value_head])
        probs_low = probs.astype(jnp.bfloat16)
        g_probs = jnp.einsum("tgd,kd->gtk", g_out, v_block, preferred_element_type=jnp.float32)
        g_scores = (probs * (g_probs - jnp.sum(probs * g_probs, axis=-1, keepdims=True))).astype(
            jnp.bfloat16
        )
        g_value_heads.append(
            jnp.einsum("gtk,tgd->kd", probs_low, g_out, preferred_element_type=jnp.float32)
        )
        g_key_heads.append(
            jnp.einsum("gtk,tgd->kd", g_scores, q_group, preferred_element_type=jnp.float32) * scale
        )
        g_query_heads.append(
            jnp.einsum("gtk,kd->tgd", g_scores, k_block, preferred_element_type=jnp.float32) * scale
        )
    g_context = jnp.concatenate(g_key_heads + g_value_heads, axis=1)
    grad_rotated_pairs = g_context[rim * count_of_rows :]
    for offset in range(1, rim + 1):
        earlier_part = g_context[
            (rim - offset) * count_of_rows : (rim - offset + 1) * count_of_rows
        ]
        grad_rotated_pairs = grad_rotated_pairs + shifted(
            earlier_part.astype(jnp.bfloat16), "fsdp", -offset
        ).astype(earlier_part.dtype)
    g_k_raw = (
        apply_rotary(
            grad_rotated_pairs[:, :key_value_width].reshape(
                count_of_rows, KEY_VALUE_HEADS, HEAD_SIZE
            ),
            query_position,
            -1.0,
        )
        .reshape(count_of_rows, key_value_width)
        .astype(jnp.bfloat16)
    )
    g_v_raw = grad_rotated_pairs[:, key_value_width:].astype(jnp.bfloat16)
    g_q_raw = (
        apply_rotary(jnp.concatenate(g_query_heads, axis=1), query_position, -1.0)
        .reshape(count_of_rows, D)
        .astype(jnp.bfloat16)
    )
    grad_query = weight_grad(normalized_input, g_q_raw)
    grad_key = weight_grad(normalized_input, g_k_raw)
    grad_value = weight_grad(normalized_input, g_v_raw)
    grad_inner = weight_grad(normalized_input, g_inner_low)
    grad_gate_z = weight_grad(normalized_input, g_gate_z)
    grad_bc = weight_grad(normalized_input, g_bc)
    grad_step = weight_grad(normalized_input, g_step_raw)
    g_normed = (
        project_back(g_q_raw, back_q)
        + project_back(g_k_raw, back_k)
        + project_back(g_v_raw, back_v)
        + project_back(g_inner_low, back_x)
        + project_back(g_gate_z, back_z)
        + project_back(g_bc, back_bc)
        + project_back(g_step_raw, back_dt)
    )
    g_x_norm, g_gain_zero = norm_back(g_normed, x_float, norm_gains[0])
    grad_tokens = g_mix + g_x_norm
    mixer_grads = (
        lax.psum_scatter(grad_query.reshape(-1), ("fsdp", "rep"), scatter_dimension=0, tiled=True),
        lax.psum_scatter(grad_key.reshape(-1), ("fsdp", "rep"), scatter_dimension=0, tiled=True),
        lax.psum_scatter(grad_value.reshape(-1), ("fsdp", "rep"), scatter_dimension=0, tiled=True),
        lax.psum_scatter(
            grad_attn_out.reshape(-1), ("fsdp", "rep"), scatter_dimension=0, tiled=True
        ),
        lax.psum_scatter(grad_inner.reshape(-1), ("fsdp", "rep"), scatter_dimension=0, tiled=True),
        lax.psum_scatter(grad_gate_z.reshape(-1), ("fsdp", "rep"), scatter_dimension=0, tiled=True),
        lax.psum_scatter(grad_bc.reshape(-1), ("fsdp", "rep"), scatter_dimension=0, tiled=True),
        lax.psum_scatter(grad_step.reshape(-1), ("fsdp", "rep"), scatter_dimension=0, tiled=True),
        lax.psum_scatter(
            grad_mamba_out.reshape(-1), ("fsdp", "rep"), scatter_dimension=0, tiled=True
        ),
    )
    gain_grads, bias_grad, decay_grad, skip_grad = lax.psum(
        (jnp.stack([g_gain_zero, g_gain_one, g_gain_two, g_gain_three]), g_bias, g_decay, g_skip),
        ("fsdp", "rep"),
    )
    return (
        output,
        grad_tokens,
        mixer_grads[0],
        mixer_grads[1],
        mixer_grads[2],
        mixer_grads[3],
        mixer_grads[4],
        mixer_grads[5],
        mixer_grads[6],
        mixer_grads[7],
        mixer_grads[8],
        ffn_grads[0],
        ffn_grads[1],
        ffn_grads[2],
        gain_grads,
        bias_grad,
        decay_grad,
        skip_grad,
    )


def solution(mesh):
    placed = (
        P(("rep", "fsdp"), None),
        P("rep", None),
        P(("fsdp", "rep")),
        P(("fsdp", "rep")),
        P(("fsdp", "rep")),
        P(("fsdp", "rep")),
        P(("fsdp", "rep")),
        P(("fsdp", "rep")),
        P(("fsdp", "rep")),
        P(("fsdp", "rep")),
        P(("fsdp", "rep")),
        P(("fsdp", "rep")),
        P(("fsdp", "rep")),
        P(("fsdp", "rep")),
        P(),
        P(),
        P(),
        P(),
        P(("rep", "fsdp"), None),
    )
    return jax.shard_map(
        local,
        mesh=mesh,
        in_specs=placed,
        out_specs=(
            P(("rep", "fsdp"), None),
            P(("rep", "fsdp"), None),
            P(("fsdp", "rep")),
            P(("fsdp", "rep")),
            P(("fsdp", "rep")),
            P(("fsdp", "rep")),
            P(("fsdp", "rep")),
            P(("fsdp", "rep")),
            P(("fsdp", "rep")),
            P(("fsdp", "rep")),
            P(("fsdp", "rep")),
            P(("fsdp", "rep")),
            P(("fsdp", "rep")),
            P(("fsdp", "rep")),
            P(),
            P(),
            P(),
            P(),
        ),
        check_vma=False,
    )
```

profile of v0, /device:TPU:0, one launch (start us, length us, event | category | flops | bytes accessed | tf_op | source)
XLA Modules:
  0.0 5353.0 jit_solution(10562341468057484878)
XLA Ops:
  41.4 55.6 %all-gather.5 = bf16[32,1,16000]{2,1,0:T(2,128)(2,1)S(1)} all-gather(bf16[1,1,16000]{2,1,0:T(2,128)(2,1)S(1)} %reshape.1116), channel_id=1, replica_groups=mesh['fsdp'=4,'rep'=8] {'fsdp','rep'}, dimensions={0}, use_global_device_ids=true | all-gather | bytes 1056000 | tf_op jit(solution)/shard_map/all_gather | solution.py:251
  106.7 47.8 all-gather.4
  224.8 18.1 all-gather.23.cloned.1.call-done
  242.8 32.5 reduce.8
  356.2 32.6 reduce.9
  404.5 60.9 %all-gather.27.cloned.1.call-done = bf16[32,1,160000]{2,1,0:T(2,128)(2,1)} async-done(((bf16[1,1,160000]{2,1,0:T(2,128)(2,1)}), bf16[32,1,160000]{2,1,0:T(2,128)(2,1)}) %all-gather.27.cloned.1.call-update) | async-done | bytes 10240016 | tf_op jit(solution)/shard_map/all_gather | solution.py:253
  465.5 62.6 %reduce.11 = bf16[32,160000]{1,0:T(8,128)(2,1)} reduce(bf16[32,1,160000]{2,1,0:T(2,128)(2,1)} %all-gather.27.cloned.1.call-done, bf16[]{:T(256)} %constant.397), dimensions={1}, to_apply=%all-gather.8.reduce_sub_computation | reduce | bytes 20480002 | tf_op jit(solution)/shard_map/all_gather | solution.py:253
  528.1 18.9 reshape.1054
  572.9 102.7 %while.129 = (s32[]{:T(128)}, f32[50,64,16]{1,2,0:T(8,128)}, s32[]{:T(128)}, f32[5,64,50,64]{3,1,0,2:T(8,128)}, f32[5,64,50,64]{3,1,2,0:T(8,128)}, /*index=5*/f3...) while((s32[]{:T(128)}, f32[50,64,16]{1,2,0:T(8,128)}, ...), condition=%wide.region_19.20_spmd.clone, body=%wide.region_17.19_spmd.clone.sunk | while | flops 238632496 | bytes 11285638 | solution.py:182
  675.6 33.7 all-gather.1
  737.2 62.6 %reduce.13 = bf16[32,160000]{1,0:T(8,128)(2,1)} reduce(bf16[32,1,160000]{2,1,0:T(2,128)(2,1)} %all-gather.29.cloned.1.call-done, bf16[]{:T(256)} %constant.397), dimensions={1}, to_apply=%all-gather.9.reduce_sub_computation | reduce | bytes 20480002 | tf_op jit(solution)/shard_map/all_gather | solution.py:254
  799.8 18.5 reshape.1068
  818.3 63.1 %reduce.14 = bf16[32,160000]{1,0:T(8,128)(2,1)} reduce(bf16[32,1,160000]{2,1,0:T(2,128)(2,1)} %all-gather.31.cloned.1.call-done, bf16[]{:T(256)} %constant.397), dimensions={1}, to_apply=%all-gather.10.reduce_sub_computation | reduce | bytes 20480002 | tf_op jit(solution)/shard_map/all_gather | solution.py:257
  881.3 18.3 reshape.1069
  899.6 10.6 multiply_convert_fusion.4
  921.9 225.2 %while.131 = (s32[]{:T(128)}, f32[50,64,16]{1,2,0:T(8,128)S(1)}, s32[]{:T(128)}, pred[5,64,64,50]{2,1,3,0:T(32,128)(4,1)S(1)}, f32[5,64,64,50]{2,1,3,0:T(8,128)}...) while((s32[]{:T(128)}, f32[50,64,16]{1,2,0:T(8,128)S(1)}, ...), condition=%wide.region_39.40_spmd.clone, body=%wide.region_37.39_spmd.clone.sunk | while | flops 81048544 | bytes 37187364 | solution.py:182
  1147.2 343.9 %reduce.17 = bf16[32,275200]{1,0:T(8,128)(2,1)} reduce(bf16[32,1,275200]{2,1,0:T(2,128)(2,1)} %all-gather.33.cloned.1.call-done, bf16[]{:T(256)} %constant.397), dimensions={1}, to_apply=%all-gather.11.reduce_sub_computation | reduce | bytes 35225600 | tf_op jit(solution)/shard_map/all_gather | solution.py:345
  1491.2 43.7 reshape.1070
  1534.8 344.1 %reduce.18 = bf16[32,275200]{1,0:T(8,128)(2,1)} reduce(bf16[32,1,275200]{2,1,0:T(2,128)(2,1)} %all-gather.35.cloned.1.call-done, bf16[]{:T(256)} %constant.397), dimensions={1}, to_apply=%all-gather.12.reduce_sub_computation | reduce | bytes 35225600 | tf_op jit(solution)/shard_map/all_gather | solution.py:346
  1878.9 43.5 reshape.1071
  1922.4 12.3 fusion.368
  1945.2 344.0 %reduce.19 = bf16[32,275200]{1,0:T(8,128)(2,1)} reduce(bf16[32,1,275200]{2,1,0:T(2,128)(2,1)} %all-gather.37.cloned.1.call-done, bf16[]{:T(256)} %constant.397), dimensions={1}, to_apply=%all-gather.13.reduce_sub_computation | reduce | bytes 35225600 | tf_op jit(solution)/shard_map/all_gather | solution.py:347
  2289.2 43.4 reshape.1072
  2332.6 20.2 multiply_convert_fusion
  2352.8 13.2 fusion.370
  2366.1 15.7 multiply_reduce_fusion.2
  2389.8 15.4 multiply_reduce_fusion.1
  2418.5 18.4 fusion.377
  2442.4 14.2 all-gather.2
  2466.2 36.6 reshape.1093
  2502.8 19.7 fusion.378
  2522.5 41.5 reshape.1094
  2569.2 264.9 %while.128 = (s32[]{:T(128)}, f32[50,64,16]{1,2,0:T(8,128)S(1)}, f32[5,64,50,64]{3,1,2,0:T(8,128)}, bf16[5,64,16]{1,2,0:T(8,128)(2,1)S(1)}, f32[5,64,16]{1,0,2:T...) while((s32[]{:T(128)}, f32[50,64,16]{1,2,0:T(8,128)S(1)}, ...), condition=%wide.region_49.50_spmd, body=%wide.region_40.49_spmd.sunk | while | flops 477345824 | bytes 31602800 | solution.py:182
  2845.7 12.0 copy.443
  2982.8 13.5 reshape.1083
  3004.7 13.4 reshape.1086
  3023.2 10.1 fusion.343
  3033.3 21.1 reshape.1087
  3054.5 10.3 fusion.341
  3064.8 21.4 reshape.1088
  3095.2 12.6 fusion.375
  3108.0 17.0 fusion.376
  3127.3 25.0 reshape.1091
  3152.3 37.0 reshape.1092
  3222.6 14.7 fusion.191
  3243.5 44.3 all-reduce.19
  3291.8 285.8 %all-reduce.29.cloned.1.call-done = (f32[8806400]{0:T(1024)}, f32[8806400]{0:T(1024)}) async-done(((f32[8806400]{0:T(1024)}, f32[8806400]{0:T(1024)}), (f32[8806400]{0:T(1024)}, f32[8806400]{0:T(1024)})) %all-reduce.29.cloned.1.call-update) | async-done | bytes 70451216
  3582.7 1744.8 %all-reduce.27.cloned.1.call-done = (f32[2560000]{0:T(1024)}, f32[512000]{0:T(1024)}, f32[512000]{0:T(1024)}, f32[2560000]{0:T(1024)}, f32[5120000]{0:T(1024)}, ...) async-done(((f32[2560000]{0:T(1024)}, f32[512000]{0:T(1024)}, f32[512000]{0:T(1024)}, f32[2560000]{0:T(1024)}, ...) | async-done | bytes 121766416
  (1142 shorter events, 1132.1 us)
Async XLA Ops:
  7.2 188.2 %all-reduce.31.cloned.1.call-start = ((), (), s32[]{:S(2)}) async-start(), calls=%async_computation.10 | async-start | bytes 528384
  9.9 233.0 %all-gather.23.cloned.1.call-start = ((), (), s32[]{:S(2)}) async-start(), calls=%async_computation | async-start | bytes 10560000 | tf_op jit(solution)/shard_map/all_gather | solution.py:249
  11.7 344.5 %all-gather.25.cloned.1.call-start = ((), (), s32[]{:S(2)}) async-start(), calls=%async_computation.1 | async-start | bytes 10560000 | tf_op jit(solution)/shard_map/all_gather | solution.py:252
  13.7 451.8 %all-gather.27.cloned.1.call-start = ((), (), s32[]{:S(2)}) async-start(), calls=%async_computation.2 | async-start | bytes 21120000 | tf_op jit(solution)/shard_map/all_gather | solution.py:253
  18.1 719.1 %all-gather.29.cloned.1.call-start = ((), (), s32[]{:S(2)}) async-start(), calls=%async_computation.3 | async-start | bytes 21120000 | tf_op jit(solution)/shard_map/all_gather | solution.py:254
  22.6 795.7 %all-gather.31.cloned.1.call-start = ((), (), s32[]{:S(2)}) async-start(), calls=%async_computation.4 | async-start | bytes 21120000 | tf_op jit(solution)/shard_map/all_gather | solution.py:257
  27.1 1120.1 %all-gather.33.cloned.1.call-start = ((), (), s32[]{:S(2)}) async-start(), calls=%async_computation.5 | async-start | bytes 36326400 | tf_op jit(solution)/shard_map/all_gather | solution.py:345
  34.2 1500.7 %all-gather.35.cloned.1.call-start = ((), (), s32[]{:S(2)}) async-start(), calls=%async_computation.6 | async-start | bytes 36326400 | tf_op jit(solution)/shard_map/all_gather | solution.py:346
  41.3 1903.9 %all-gather.37.cloned.1.call-start = ((), (), s32[]{:S(2)}) async-start(), calls=%async_computation.7 | async-start | bytes 36326400 | tf_op jit(solution)/shard_map/all_gather | solution.py:347
  106.6 66.0 %copy-start.49 = (bf16[1600,320]{1,0:T(8,128)(2,1)}, bf16[1600,320]{1,0:T(8,128)(2,1)S(1)}, u32[]{:S(2)}) copy-start(bf16[1600,320]{1,0:T(8,128)(2,1)S(1)} %reshape.1051) | copy-start | bytes 3072004
  169.0 25.8 copy-start.127
  169.0 25.8 copy-start.129
  169.0 730.6 %copy-start.77 = (f32[1600]{0:T(1024)}, f32[1600]{0:T(1024)S(1)}, u32[]{:S(2)}) copy-start(f32[1600]{0:T(1024)S(1)} %get-tuple-element.1961) | copy-start | bytes 19204
  169.3 730.3 %copy-start.101 = (f32[320]{0:T(512)}, f32[320]{0:T(512)S(1)}, u32[]{:S(2)}) copy-start(f32[320]{0:T(512)S(1)} %add_rsqrt_fusion.3) | copy-start | bytes 3844
  173.5 21.3 copy-start.85
  173.5 20.6 copy-start.145
  174.4 47.9 collective-permute-start.2
  175.7 46.5 collective-permute-start.1
  179.8 43.3 collective-permute-start
  189.1 3388.4 %all-reduce.29.cloned.1.call-start = ((), (), s32[]{:S(2)}) async-start(), calls=%async_computation.9 | async-start | bytes 140902400
  190.5 31.1 copy-start.150
  202.8 72.5 %copy-start.86 = (f32[7,8,3,128]{3,1,2,0:T(8,128)}, f32[7,8,3,128]{3,1,2,0:T(8,128)S(1)}, u32[]{:S(2)}) copy-start(f32[7,8,3,128]{3,1,2,0:T(8,128)S(1)} %copy.582) | copy-start | bytes 258052
  224.8 128.7 %copy-start.24 = (bf16[1280,640]{1,0:T(8,128)(2,1)}, bf16[1280,640]{1,0:T(8,128)(2,1)S(1)}, u32[]{:S(2)}) copy-start(bf16[1280,640]{1,0:T(8,128)(2,1)S(1)} %maximum_maximum_fusion) | copy-start | bytes 4915204
  311.6 32.5 copy-start.2
  313.4 35.5 copy-start.1
  315.2 38.3 copy-start
  1147.1 344.1 %copy-start.58 = (f32[5,64,50]{2,1,0:T(8,128)}, f32[5,64,50]{2,1,0:T(8,128)S(1)}, u32[]{:S(2)}) copy-start(f32[5,64,50]{2,1,0:T(8,128)S(1)} %get-tuple-element.3201) | copy-start | bytes 192004
  1147.1 344.0 %copy-start.72 = (pred[5,64,64,50]{2,1,3,0:T(32,128)(4,1)}, pred[5,64,64,50]{2,1,3,0:T(32,128)(4,1)S(1)}, u32[]{:S(2)}) copy-start(pred[5,64,64,50]{2,1,3,0:T(32,128)(4,1)S(1)} %get-tuple-element.3053) | copy-start | bytes 3072004
  1147.1 344.0 %copy-start.88 = (f32[5,64,50]{2,1,0:T(8,128)}, f32[5,64,50]{2,1,0:T(8,128)S(1)}, u32[]{:S(2)}) copy-start(f32[5,64,50]{2,1,0:T(8,128)S(1)} %get-tuple-element.3052) | copy-start | bytes 192004
  1147.1 344.0 %copy-start.89 = (f32[5,64,50]{2,1,0:T(8,128)}, f32[5,64,50]{2,1,0:T(8,128)S(1)}, u32[]{:S(2)}) copy-start(f32[5,64,50]{2,1,0:T(8,128)S(1)} %get-tuple-element.3047) | copy-start | bytes 192004
  1147.1 344.0 %copy-start.90 = (f32[5,64,50]{2,1,0:T(8,128)}, f32[5,64,50]{2,1,0:T(8,128)S(1)}, u32[]{:S(2)}) copy-start(f32[5,64,50]{2,1,0:T(8,128)S(1)} %get-tuple-element.3039) | copy-start | bytes 192004
  1147.1 344.0 %copy-start.91 = (f32[5,64,50]{2,1,0:T(8,128)}, f32[5,64,50]{2,1,0:T(8,128)S(1)}, u32[]{:S(2)}) copy-start(f32[5,64,50]{2,1,0:T(8,128)S(1)} %get-tuple-element.3056) | copy-start | bytes 192004
  1147.1 344.0 %copy-start.165 = (pred[5]{0:T(512)(128)(4,1)}, pred[5]{0:T(512)(128)(4,1)S(1)}, u32[]{:S(2)}) copy-start(pred[5]{0:T(512)(128)(4,1)S(1)} %get-tuple-element.3048) | copy-start | bytes 19
  1878.9 43.5 copy-start.37
  2289.2 43.4 copy-start.56
  2410.8 26.1 slice-start.10
  2436.9 19.7 copy-start.27
  2466.2 36.6 copy-start.57
  2564.0 2763.5 %all-reduce.27.cloned.1.call-start = ((), (), s32[]{:S(2)}) async-start(), calls=%async_computation.8 | async-start | bytes 243539968
  2874.0 40.0 copy-start.42
  2957.4 231.8 %collective-permute-start.5 = (bf16[320,640]{0,1:T(8,128)(2,1)}, bf16[320,640]{0,1:T(8,128)(2,1)}, u32[]{:S(2)}, u32[]{:S(2)}) collective-permute-start(bf16[320,640]{0,1:T(8,128)(2,1)} %get-tuple-element.2201), channel_id=1, source_target_pairs={{24,0},{25,1},{26,2},{27,3},{28,4},{29,5},{30,6},{31,7}} | collective-permute-start | bytes 1228808 | tf_op jit(solution)/shard_map/ppermute | solution.py:28
  2958.7 230.5 %collective-permute-start.4 = (bf16[320,640]{0,1:T(8,128)(2,1)}, bf16[320,640]{0,1:T(8,128)(2,1)}, u32[]{:S(2)}, u32[]{:S(2)}) collective-permute-start(bf16[320,640]{0,1:T(8,128)(2,1)} %get-tuple-element.2202), channel_id=1, source_target_pairs={{16,0},{24,8},{17,1},{25,9},{18,2},{26,10},{19,3},{27,11},{20,4},{... | collective-permute-start | bytes 1228808 | tf_op jit(solution)/shard_map/ppermute | solution.py:28
  2960.0 229.2 %collective-permute-start.3 = (bf16[320,640]{0,1:T(8,128)(2,1)}, bf16[320,640]{0,1:T(8,128)(2,1)}, u32[]{:S(2)}, u32[]{:S(2)}) collective-permute-start(bf16[320,640]{0,1:T(8,128)(2,1)} %get-tuple-element.2200), channel_id=1, source_target_pairs={{8,0},{16,8},{24,16},{9,1},{17,9},{25,17},{10,2},{18,10},{26,18},{... | collective-permute-start | bytes 1228808 | tf_op jit(solution)/shard_map/ppermute | solution.py:28
  3033.3 21.2 copy-start.67
  3064.8 21.4 copy-start.23
  3064.8 21.4 copy-start.81
  3125.2 27.1 copy-start.120
  3241.1 46.8 copy-start.31
  (160 other events, 1133.1 us)
Sparse Core Ops, SparseCore 0:
  13.5 128.5 all-reduce.30
  146.0 96.7 all-gather.22
  246.8 84.1 all-gather.24
  334.7 130.7 all-gather.26
  469.2 130.1 all-gather.28
  603.2 143.5 all-gather.30
  750.9 200.9 all-gather.32
  955.9 201.0 all-gather.34
  1161.0 200.9 all-gather.36
  2564.1 1013.3 all-reduce.28
  3585.1 1742.3 all-reduce.26
where the time goes:
time: 5380 us; the launch traced here: 5350 us
  waiting for transfers between devices  2110 us (39%)
  other arithmetic  1470 us (27%)
  local copies, waits for them, and re-layouts  867 us (16%)
  matrix products  648 us (12%)
  blocking collectives  213 us (4%)
    unnamed x14, waiting for transfers between devices  2030 us
    all_gather x1, other arithmetic, local(): lax.all_gather(w_ffn_up, ('fsdp', 'rep'), axis=0, tiled=True)  344 us
    all_gather x1, other arithmetic, local(): lax.all_gather(w_ffn_down, ('fsdp', 'rep'), axis=0, tiled=True)  344 us
    all_gather x1, other arithmetic, local(): lax.all_gather(w_ffn_gate, ('fsdp', 'rep'), axis=0, tiled=True)  344 us
    reshape x12, local copies, waits for them, and re-layouts, unflatten(): return tuple((flat.reshape(shape) for flat, shape in zip(flats, shapes)))  212 us
    dynamic_update_slice x90, local copies, waits for them, and re-layouts, local_scan(): (state_end, _), ssm_out = lax.scan(stretch_scan, start, blocks)  141 us
    dot_general x12, matrix products, weight_grad(): lax.dot_general(value_rows, grad_in, (((0,), (0,)), ((), ())), preferred_...  109 us
  transfers between devices with their start and end apart: 17, of which 4 were waited for; matrix products, arithmetic and copies ran while one was open for 44% of the time, Pallas kernels for 0%

commit v1 on v0

v1 whole, which is shorter than its diff:
```python
import functools
import math

import jax
import jax.numpy as jnp
from jax import lax
from jax.experimental import pallas as pl
from jax.experimental.layout import Layout, with_layout_constraint
from jax.experimental.pallas import tpu as pltpu
from jax.sharding import PartitionSpec as P

D = 1600
QUERY_HEADS = 25
KEY_VALUE_HEADS = 5
HEAD_SIZE = 64
WIN = 1024
MI = 3200
NS = 16
FF = 5504
MH = 50
KV = KEY_VALUE_HEADS * HEAD_SIZE
HEADS_PER_GROUP = QUERY_HEADS // KEY_VALUE_HEADS
SCALE = HEAD_SIZE ** (-0.5)
CHUNK = 128
QUERY_BLOCK = 256
STEP_ROWS = 16
VMEM_BYTES = 50 * 1024 * 1024

epsilon = 1e-06
masked_score = -1e30
highest = lax.Precision.HIGHEST
f32 = jnp.float32
bf16 = jnp.bfloat16


def rms_scale(value_rows, gain):
    return (
        value_rows
        * lax.rsqrt(jnp.mean(value_rows * value_rows, axis=-1, keepdims=True) + epsilon)
        * gain
    )


def norm_back(grad_in, value_rows, gain):
    factor = lax.rsqrt(jnp.mean(value_rows * value_rows, axis=-1, keepdims=True) + epsilon)
    weighted = grad_in * gain
    spread = jnp.mean(weighted * value_rows, axis=-1, keepdims=True)
    return (
        factor * weighted - value_rows * factor * factor * factor * spread,
        jnp.sum(grad_in * value_rows * factor, axis=0),
    )


def silu(value_rows):
    return value_rows * jax.nn.sigmoid(value_rows)


def silu_slope(value_rows):
    sigmoid_v = jax.nn.sigmoid(value_rows)
    return sigmoid_v * (1.0 + value_rows * (1.0 - sigmoid_v))


def dot(a, b, ca, cb, precision=None):
    return lax.dot_general(
        a, b, (((ca,), (cb,)), ((), ())), precision=precision, preferred_element_type=f32
    )


def sequence_layout(seq_lengths, position):
    seq_ends = jnp.cumsum(seq_lengths, dtype=jnp.int32)
    seq_starts = seq_ends - seq_lengths
    segment = jnp.sum(
        (position[:, None] >= seq_ends[None, :]).astype(jnp.int32), axis=1, dtype=jnp.int32
    )
    labels = jnp.arange(seq_lengths.shape[0], dtype=jnp.int32)
    seq_begin = jnp.sum(
        jnp.where(segment[:, None] == labels[None, :], seq_starts[None, :], 0),
        axis=1,
        dtype=jnp.int32,
    )
    return (segment, (position - seq_begin).astype(f32))


def key_range(i):
    low = max(0, i * QUERY_BLOCK - (WIN - 1)) // QUERY_BLOCK * QUERY_BLOCK
    return low, (i + 1) * QUERY_BLOCK


def fill_mask(seg_col, seg_row, mask, blocks):
    for i in range(blocks):
        low, high = key_range(i)
        cols = slice(i * QUERY_BLOCK, (i + 1) * QUERY_BLOCK)
        shape = (high - low, QUERY_BLOCK)
        key = lax.broadcasted_iota(jnp.int32, shape, 0) + low
        query = lax.broadcasted_iota(jnp.int32, shape, 1) + i * QUERY_BLOCK
        gap = query - key
        visible = (seg_col[low:high, :] == seg_row[:, cols]) & (gap >= 0) & (gap < WIN)
        mask[low:high, cols] = jnp.where(visible, 0.0, masked_score)


def rotate(value, cosine, sine):
    half = HEAD_SIZE // 2
    a, b = value[:half], value[half:]
    return jnp.concatenate([a * cosine - b * sine, b * cosine + a * sine], axis=0)


def attn_fwd_kernel(
    kvmap, kv_ref, q_ref, cosine, sine, seg_row, seg_col, o_ref, qt_ref, kt_ref, kn_ref, vn_ref, mask, vt, *, blocks
):
    h = pl.program_id(0)

    @pl.when(h == 0)
    def _():
        fill_mask(seg_col, seg_row, mask, blocks)
        for c in range(KEY_VALUE_HEADS):
            k = rotate(kv_ref[c], cosine[...], sine[...])
            kt_ref[c] = k.astype(bf16)
            kn_ref[c] = k.T.astype(bf16)
            v = kv_ref[KEY_VALUE_HEADS + c]
            vt[c] = v.astype(bf16)
            vn_ref[c] = v.T.astype(bf16)

    kv = kvmap[h]
    tokens = o_ref.shape[3]
    for i in range(blocks):
        low, high = key_range(i)
        start, stop = i * QUERY_BLOCK, (i + 1) * QUERY_BLOCK
        cols = slice(start, stop)
        q = (rotate(q_ref[0, :, cols], cosine[:, cols], sine[:, cols]) * SCALE).astype(bf16)
        qt_ref[0, :, cols] = q
        s = dot(kn_ref[kv, low:high, :], q, 1, 0) + mask[low:high, cols]
        p = jnp.exp(s - jnp.max(s, axis=0, keepdims=True))
        total = jnp.sum(p, axis=0, keepdims=True)
        o = dot(vt[kv, :, low:high], p.astype(bf16), 1, 0)
        o = (o / total).astype(bf16)
        for d in range(o_ref.shape[0]):
            first, last = max(start, d * tokens), min(stop, (d + 1) * tokens)
            if first < last:
                part = o[:, first - start : last - start]
                o_ref[d, 0, :, first - d * tokens : last - d * tokens] = part


def attn_fwd(kvmap, proj, cosine, sine, seg_row, seg_col, devices):
    heads = proj.shape[0] - 2 * KEY_VALUE_HEADS
    group = proj.shape[2]
    tokens = group // devices
    per_head = pl.BlockSpec((1, HEAD_SIZE, group), lambda h, m: (h, 0, 0))
    angle = pl.BlockSpec((HEAD_SIZE // 2, group), lambda h, m: (0, 0))
    kv_t = (KEY_VALUE_HEADS, HEAD_SIZE, group)
    kv_n = (KEY_VALUE_HEADS, group, HEAD_SIZE)
    whole_t = pl.BlockSpec(kv_t, lambda h, m: (0, 0, 0))
    whole_n = pl.BlockSpec(kv_n, lambda h, m: (0, 0, 0))
    return pl.pallas_call(
        functools.partial(attn_fwd_kernel, blocks=group // QUERY_BLOCK),
        out_shape=(
            jax.ShapeDtypeStruct((devices, heads, HEAD_SIZE, tokens), bf16),
            jax.ShapeDtypeStruct((heads, HEAD_SIZE, group), bf16),
            jax.ShapeDtypeStruct(kv_t, bf16),
            jax.ShapeDtypeStruct(kv_n, bf16),
            jax.ShapeDtypeStruct(kv_n, bf16),
        ),
        grid_spec=pltpu.PrefetchScalarGridSpec(
            num_scalar_prefetch=1,
            grid=(heads,),
            in_specs=[
                pl.BlockSpec((2 * KEY_VALUE_HEADS, HEAD_SIZE, group), lambda h, m: (0, 0, 0)),
                pl.BlockSpec((1, HEAD_SIZE, group), lambda h, m: (h + 2 * KEY_VALUE_HEADS, 0, 0)),
                angle,
                angle,
                pl.BlockSpec((1, group), lambda h, m: (0, 0)),
                pl.BlockSpec((group, 1), lambda h, m: (0, 0)),
            ],
            out_specs=(
                pl.BlockSpec((devices, 1, HEAD_SIZE, tokens), lambda h, m: (0, h, 0, 0)),
                per_head,
                whole_t,
                whole_n,
                whole_n,
            ),
            scratch_shapes=[pltpu.VMEM((group, group), f32), pltpu.VMEM(kv_t, bf16)],
        ),
        compiler_params=pltpu.CompilerParams(vmem_limit_bytes=VMEM_BYTES),
        cost_estimate=pl.CostEstimate(
            flops=group * group, bytes_accessed=group * HEAD_SIZE, transcendentals=group,
        ),
        name="attn_fwd",
    )(kvmap, proj, proj, cosine, sine, seg_row, seg_col)


def attn_bwd_kernel(kvmap, *refs, blocks, devices):
    do_parts = refs[:devices]
    q_ref, kn_ref, kt_ref, vn_ref, cosine, sine, seg_row, seg_col = refs[devices : devices + 8]
    g_ref, mask, dk, dv, do_all = refs[devices + 8 :]
    h = pl.program_id(0)

    @pl.when(h == 0)
    def _():
        fill_mask(seg_col, seg_row, mask, blocks)
        dk[...] = jnp.zeros(dk.shape, f32)
        dv[...] = jnp.zeros(dv.shape, f32)

    kv = kvmap[h]
    tokens = do_parts[0].shape[3]
    for d in range(devices):
        do_all[:, d * tokens : (d + 1) * tokens] = do_parts[d][0, 0]
    for i in range(blocks):
        low, high = key_range(i)
        cols = slice(i * QUERY_BLOCK, (i + 1) * QUERY_BLOCK)
        q = q_ref[0, :, cols]
        do = do_all[:, cols]
        s = dot(kn_ref[kv, low:high, :], q, 1, 0) + mask[low:high, cols]
        p = jnp.exp(s - jnp.max(s, axis=0, keepdims=True))
        p = p * (1.0 / jnp.sum(p, axis=0, keepdims=True))
        dp = dot(vn_ref[kv, low:high, :], do, 1, 0)
        delta = jnp.sum(p * dp, axis=0, keepdims=True)
        ds = (p * (dp - delta)).astype(bf16)
        dv[kv, low:high, :] += dot(p.astype(bf16), do, 1, 1)
        dk[kv, low:high, :] += dot(ds, q, 1, 1)
        dq = dot(kt_ref[kv, :, low:high], ds, 1, 0) * SCALE
        dq = rotate(dq, cosine[:, cols], -sine[:, cols])
        g_ref[2 * KEY_VALUE_HEADS + h, :, cols] = dq.astype(bf16)

    @pl.when(h == pl.num_programs(0) - 1)
    def _():
        for c in range(KEY_VALUE_HEADS):
            g_ref[c] = rotate(dk[c].T, cosine[...], -sine[...]).astype(bf16)
            g_ref[KEY_VALUE_HEADS + c] = dv[c].T.astype(bf16)


def attn_bwd(kvmap, do_blocks, q_t, k_n, k_t, v_n, cosine, sine, seg_row, seg_col):
    devices, heads, _, tokens = do_blocks.shape
    group = q_t.shape[2]
    angle = pl.BlockSpec((HEAD_SIZE // 2, group), lambda h, m: (0, 0))
    kv_t = (KEY_VALUE_HEADS, HEAD_SIZE, group)
    kv_n = (KEY_VALUE_HEADS, group, HEAD_SIZE)
    whole_n = pl.BlockSpec(kv_n, lambda h, m: (0, 0, 0))
    out = (2 * KEY_VALUE_HEADS + heads, HEAD_SIZE, group)

    def block_spec(d):
        return pl.BlockSpec((1, 1, HEAD_SIZE, tokens), lambda h, m: (m[heads + d], h, 0, 0))

    return pl.pallas_call(
        functools.partial(attn_bwd_kernel, blocks=group // QUERY_BLOCK, devices=devices),
        out_shape=jax.ShapeDtypeStruct(out, bf16),
        grid_spec=pltpu.PrefetchScalarGridSpec(
            num_scalar_prefetch=1,
            grid=(heads,),
            in_specs=[block_spec(d) for d in range(devices)]
            + [
                pl.BlockSpec((1, HEAD_SIZE, group), lambda h, m: (h, 0, 0)),
                whole_n,
                pl.BlockSpec(kv_t, lambda h, m: (0, 0, 0)),
                whole_n,
                angle,
                angle,
                pl.BlockSpec((1, group), lambda h, m: (0, 0)),
                pl.BlockSpec((group, 1), lambda h, m: (0, 0)),
            ],
            out_specs=pl.BlockSpec(out, lambda h, m: (0, 0, 0)),
            scratch_shapes=[
                pltpu.VMEM((group, group), f32),
                pltpu.VMEM(kv_n, f32),
                pltpu.VMEM(kv_n, f32),
                pltpu.VMEM((HEAD_SIZE, group), bf16),
            ],
        ),
        compiler_params=pltpu.CompilerParams(vmem_limit_bytes=VMEM_BYTES),
        cost_estimate=pl.CostEstimate(
            flops=group * group, bytes_accessed=group * HEAD_SIZE, transcendentals=group,
        ),
        name="attn_bwd",
    )(kvmap, *([do_blocks] * devices), q_t, k_n, k_t, v_n, cosine, sine, seg_row, seg_col)


def block_setup(p_ref, bias, decay, marks, seg_col, channels):
    at = 2 * channels
    b_t = p_ref[at : at + NS].astype(bf16)
    c_t = p_ref[at + NS : at + 2 * NS].astype(bf16)
    raw = p_ref[at + 2 * NS : at + 2 * NS + STEP_ROWS] + bias[...]
    step = jnp.maximum(raw, 0.0) + jnp.log1p(jnp.exp(-jnp.abs(raw)))
    rate = -step * decay[...]
    rows = lax.broadcasted_iota(jnp.int32, (CHUNK, CHUNK), 0)
    cols = lax.broadcasted_iota(jnp.int32, (CHUNK, CHUNK), 1)
    a_t = dot(rate, (rows <= cols).astype(f32), 1, 0, highest)
    a_n = a_t.T
    visible = (seg_col[...] == marks[0:1]) & (rows <= cols)
    hidden = jnp.where(visible, 0.0, masked_score)
    return b_t, c_t, raw, step, rate, a_t, a_n, rows, cols, hidden


def ssm_fwd_kernel(p_ref, bias, decay, marks, seg_col, skip, y_ref, mixed_ref, states, state, *, heads):
    channels = heads * HEAD_SIZE

    @pl.when(pl.program_id(0) == 0)
    def _():
        state[...] = jnp.zeros(state.shape, f32)

    states[0] = state[...]
    b_t, c_t, _, step, _, a_t, a_n, _, _, hidden = block_setup(
        p_ref, bias, decay, marks, seg_col, channels
    )
    block = dot(b_t, c_t, 0, 0)
    enter, leave, through = marks[1:2], marks[2:3], marks[3:4, 0:1]
    for h in range(heads):
        at = slice(h * HEAD_SIZE, (h + 1) * HEAD_SIZE)
        a_row = a_t[h : h + 1]
        a_end = a_t[h : h + 1, CHUNK - 1 :]
        x = p_ref[at].astype(bf16).astype(f32)
        z = p_ref[channels + h * HEAD_SIZE : channels + (h + 1) * HEAD_SIZE]
        mixing = (jnp.exp(a_row - a_n[:, h : h + 1] + hidden) * block).astype(bf16)
        xs = x * step[h : h + 1]
        y = dot(xs.astype(bf16), mixing, 1, 0)
        s = state[at]
        y = y + dot(s.astype(bf16), c_t, 1, 0) * (enter * jnp.exp(a_row)) + skip[h] * x
        y_ref[at] = y
        mixed_ref[at] = (y * silu(z)).astype(bf16)
        xw = (xs * (leave * jnp.exp(a_end - a_row))).astype(bf16)
        state[at] = through * jnp.exp(a_end) * s + dot(xw, b_t, 1, 1)


def ssm_specs(height, order):
    column = pl.BlockSpec((STEP_ROWS, 1), lambda c: (0, 0))
    return [
        pl.BlockSpec((height, CHUNK), lambda c: (0, order(c))),
        column,
        column,
        pl.BlockSpec((8, CHUNK), lambda c: (0, order(c))),
        pl.BlockSpec((CHUNK, 1), lambda c: (order(c), 0)),
        pl.BlockSpec(memory_space=pltpu.SMEM),
    ]


def ssm_fwd(heads, proj, bias, decay, marks, seg_col, skip):
    height, group = proj.shape
    channels = heads * HEAD_SIZE
    count = group // CHUNK
    by_block = pl.BlockSpec((channels, CHUNK), lambda c: (0, c))
    return pl.pallas_call(
        functools.partial(ssm_fwd_kernel, heads=heads),
        out_shape=(
            jax.ShapeDtypeStruct((channels, group), f32),
            jax.ShapeDtypeStruct((channels, group), bf16),
            jax.ShapeDtypeStruct((count, channels, NS), f32),
        ),
        grid=(count,),
        in_specs=ssm_specs(height, lambda c: c),
        out_specs=(by_block, by_block, pl.BlockSpec((1, channels, NS), lambda c: (c, 0, 0))),
        scratch_shapes=[pltpu.VMEM((channels, NS), f32)],
        compiler_params=pltpu.CompilerParams(vmem_limit_bytes=VMEM_BYTES),
        cost_estimate=pl.CostEstimate(
            flops=group * group, bytes_accessed=group * HEAD_SIZE, transcendentals=group,
        ),
        name="ssm_fwd",
    )(proj, bias, decay, marks, seg_col, skip)


def ssm_bwd_kernel(
    p_ref,
    bias,
    decay,
    marks,
    seg_col,
    skip,
    up_ref,
    y_ref,
    states,
    g_ref,
    sums,
    adjoint,
    after,
    before,
    gstep,
    grate,
    *,
    heads,
):
    channels = heads * HEAD_SIZE

    @pl.when(pl.program_id(0) == 0)
    def _():
        for ref in (adjoint, sums, after, before, gstep, grate):
            ref[...] = jnp.zeros(ref.shape, f32)

    b_t, c_t, raw, step_all, rate_all, a_t, a_n, rows, cols, hidden = block_setup(
        p_ref, bias, decay, marks, seg_col, channels
    )
    block = dot(b_t, c_t, 0, 0)
    enter, leave, through = marks[1:2], marks[2:3], marks[3:4, 0:1]
    from_here = (rows >= cols).astype(f32)
    from_here_low = from_here.astype(bf16)
    strictly = (rows < cols).astype(f32)
    pair_sum = jnp.zeros((CHUNK, CHUNK), f32)
    gc = jnp.zeros((NS, CHUNK), f32)
    gb = jnp.zeros((NS, CHUNK), f32)
    at_skip = 2 * STEP_ROWS
    for h in range(heads):
        at = slice(h * HEAD_SIZE, (h + 1) * HEAD_SIZE)
        at_gate = slice(channels + h * HEAD_SIZE, channels + (h + 1) * HEAD_SIZE)
        one = slice(h, h + 1)
        a_row = a_t[one]
        a_end = a_t[one, CHUNK - 1 :]
        step = step_all[one]
        x = p_ref[at].astype(bf16).astype(f32)
        z = p_ref[at_gate]
        g = up_ref[at]
        sigmoid_z = jax.nn.sigmoid(z)
        gy = g * z * sigmoid_z
        gz = g * y_ref[at] * sigmoid_z * (1.0 + z * (1.0 - sigmoid_z))
        g_ref[at_gate] = gz.astype(bf16)
        sums[at_skip + h : at_skip + h + 1] += jnp.sum(gy * x, axis=0, keepdims=True)
        reach = jnp.exp(a_row - a_n[:, one] + hidden)
        gy_low = gy.astype(bf16)
        xs = x * step
        u = dot(gy_low, (reach * block).astype(bf16), 1, 1)
        lam = adjoint[at]
        lam_low = lam.astype(bf16)
        out_weight = leave * jnp.exp(a_end - a_row)
        u_state = dot(lam_low, b_t, 1, 0) * out_weight
        u = u + u_state
        g_ref[at] = (step * u + skip[h] * gy).astype(bf16)
        gstep[one] = jnp.sum(x * u, axis=0, keepdims=True)
        before[one] = jnp.sum(xs * u_state, axis=0, keepdims=True)
        pairs = dot(xs.astype(bf16), gy_low, 0, 0) * reach
        pair_sum = pair_sum + pairs
        crossing = dot((pairs * block).astype(bf16), from_here_low, 1, 0)
        crossed = jnp.sum(crossing * strictly, axis=0, keepdims=True)
        gyw = gy * (enter * jnp.exp(a_row))
        gyw_low = gyw.astype(bf16)
        s = states[0, at]
        s_low = s.astype(bf16)
        after[one] = jnp.sum(gyw * dot(s_low, c_t, 1, 0), axis=0, keepdims=True)
        gc = gc + dot(s_low, gyw_low, 0, 0)
        gb = gb + dot(lam_low, (xs * out_weight).astype(bf16), 0, 0)
        passing = through * jnp.exp(a_end)
        product = jnp.sum(jnp.sum(lam * s, axis=1, keepdims=True), axis=0, keepdims=True)
        grate[one] = crossed + passing * product
        adjoint[at] = passing * lam + dot(gyw_low, c_t, 1, 1)
    grate_all = (
        grate[...]
        + dot(after[...], from_here, 1, 0, highest)
        + dot(before[...], strictly, 1, 0, highest)
    )
    pair_low = pair_sum.astype(bf16)
    small = 2 * channels
    g_ref[small : small + NS] = (gb + dot(c_t, pair_low, 1, 1)).astype(bf16)
    g_ref[small + NS : small + 2 * NS] = (gc + dot(b_t, pair_low, 1, 0)).astype(bf16)
    graw = (gstep[...] - grate_all * decay[...]) * jax.nn.sigmoid(raw)
    at_step = small + 2 * NS
    g_ref[at_step : at_step + STEP_ROWS] = graw.astype(bf16)
    rest = g_ref.shape[0] - at_step - STEP_ROWS
    g_ref[at_step + STEP_ROWS :] = jnp.zeros((rest, CHUNK), bf16)
    sums[:STEP_ROWS] += graw
    sums[STEP_ROWS:at_skip] += grate_all * rate_all


def ssm_bwd(heads, proj, bias, decay, marks, seg_col, skip, up_t, y_t, states):
    height, group = proj.shape
    channels = heads * HEAD_SIZE
    count = group // CHUNK

    def order(c):
        return count - 1 - c

    by_block = pl.BlockSpec((channels, CHUNK), lambda c: (0, order(c)))
    small = pltpu.VMEM((STEP_ROWS, CHUNK), f32)
    return pl.pallas_call(
        functools.partial(ssm_bwd_kernel, heads=heads),
        out_shape=(
            jax.ShapeDtypeStruct((height, group), bf16),
            jax.ShapeDtypeStruct((3 * STEP_ROWS, CHUNK), f32),
        ),
        grid=(count,),
        in_specs=ssm_specs(height, order)
        + [by_block, by_block, pl.BlockSpec((1, channels, NS), lambda c: (order(c), 0, 0))],
        out_specs=(
            pl.BlockSpec((height, CHUNK), lambda c: (0, order(c))),
            pl.BlockSpec((3 * STEP_ROWS, CHUNK), lambda c: (0, 0)),
        ),
        scratch_shapes=[pltpu.VMEM((channels, NS), f32), small, small, small, small],
        compiler_params=pltpu.CompilerParams(vmem_limit_bytes=VMEM_BYTES),
        cost_estimate=pl.CostEstimate(
            flops=group * group, bytes_accessed=group * HEAD_SIZE, transcendentals=group,
        ),
        name="ssm_bwd",
    )(proj, bias, decay, marks, seg_col, skip, up_t, y_t, states)


def pad_to(value, multiple):
    return -(-value // multiple) * multiple


def place_columns(block, start, width):
    return jnp.pad(block, ((0, 0), (start, width - start - block.shape[1])))


def peers(devices, k):
    return [(i, i ^ k) for i in range(devices)]


def one_hot(rows, cols, wanted):
    row = wanted(jnp.arange(rows, dtype=jnp.int32))
    return (row[:, None] == jnp.arange(cols, dtype=jnp.int32)[None, :]).astype(bf16)


def tie(*values):
    return lax.optimization_barrier(values)


def row_major(value):
    return with_layout_constraint(value, Layout(tuple(range(value.ndim))))


def send_to_peers(parts):
    devices = lax.axis_size("fsdp")
    return [lax.ppermute(parts[k - 1], "fsdp", peers(devices, k)) for k in range(1, devices)]


def place_blocks(own, received):
    devices, mine = lax.axis_size("fsdp"), lax.axis_index("fsdp")
    result = jnp.broadcast_to(own[None], (devices,) + own.shape)
    for k in range(1, devices):
        result = lax.dynamic_update_index_in_dim(result, received[k - 1], mine ^ k, 0)
    return result


def take_blocks(blocks):
    devices, mine = lax.axis_size("fsdp"), lax.axis_index("fsdp")
    return [lax.dynamic_index_in_dim(blocks, mine ^ k, 0, False) for k in range(devices)]


def exchange(blocks):
    parts = take_blocks(blocks)
    return place_blocks(parts[0], send_to_peers(parts[1:]))


def gather_rows(part, hold=lambda received: received):
    devices = lax.axis_size("fsdp")
    received = hold(send_to_peers([part] * (devices - 1)))
    return place_blocks(part, received).reshape((devices * part.shape[0],) + part.shape[1:])


def add_up(own, received):
    total = own.astype(f32)
    for part in received:
        total = total + part.astype(f32)
    return total


def row_blocks(partial):
    devices = lax.axis_size("fsdp")
    return partial.reshape((devices, partial.shape[0] // devices) + partial.shape[1:])


def scatter_rows(partial):
    parts = take_blocks(row_blocks(partial))
    return add_up(parts[0], send_to_peers(parts[1:]))


def all_sum(value):
    for axis in ("fsdp", "rep"):
        devices, k = lax.axis_size(axis), 1
        while k < devices:
            value = value + lax.ppermute(value, axis, peers(devices, k))
            k *= 2
    return value


def local(
    tokens,
    lengths,
    w_query,
    w_key,
    w_value,
    w_attn_out,
    w_inner,
    w_gate_z,
    w_bc,
    w_step,
    w_mamba_out,
    w_ffn_gate,
    w_ffn_up,
    w_ffn_down,
    norm_gains,
    step_bias,
    decay_log,
    skip_gain,
    cotangent,
):
    F, R = lax.axis_size("fsdp"), lax.axis_size("rep")
    mine = lax.axis_index("fsdp")
    rows = tokens.shape[0]
    group = rows * F
    aligned = D % (F * R) == 0 and FF % (F * R) == 0
    depth = D // (F * R) if aligned else D // F

    heads_q = -(-QUERY_HEADS // F)
    width_q = heads_q * HEAD_SIZE
    per_dev = MI // F
    first_head = [per_dev * d // HEAD_SIZE for d in range(F)]
    shift = [per_dev * d % HEAD_SIZE for d in range(F)]
    heads_s = max(-(-(s + per_dev) // HEAD_SIZE) for s in shift)
    channels = heads_s * HEAD_SIZE
    at_small = 2 * channels
    at_step = at_small + 2 * NS
    width_att = 2 * KV + width_q
    width_ssm = at_small + 64
    hidden_dev = FF // F
    blocks = R if aligned else 1
    rows_o, rows_m, rows_f = (D // F // blocks, per_dev // blocks, hidden_dev // blocks)
    pad_o, pad_m, pad_f = (pad_to(n, 8) for n in (rows_o, rows_m, rows_f))
    width_f = blocks * pad_f

    if aligned:

        def old_place(n):
            return (n // depth % F) * (R * depth) + n // (F * depth) * depth + n % depth

        order = one_hot(D, D, old_place)

        def permute(v):
            return dot(v, order, 1, 1).astype(v.dtype)

        def restore(v):
            return dot(v, order, 1, 0).astype(v.dtype)

        gains = norm_gains.reshape(4, F, R, depth).transpose(0, 2, 1, 3).reshape(4, D)
    else:

        def permute(v):
            return v

        restore = permute
        gains = norm_gains

    def pad_rows(matrix, height):
        return jnp.pad(matrix, ((0, height - matrix.shape[0]), (0, 0)))

    def rep_gather(flat, width):
        return lax.all_gather(flat, "rep", axis=0, tiled=True).reshape(-1, width)

    def read(flat, width):
        return flat.reshape(depth, width) if aligned else rep_gather(flat, width)

    def collect(part):
        if aligned:
            part = part.reshape(F * depth, part.shape[2])
            return lax.all_gather(part, "rep", axis=0, tiled=True)
        return part.reshape(D, part.shape[2])

    index = jnp.arange(group, dtype=jnp.int32)
    segment, place = sequence_layout(lengths[0], index)
    frequency = jnp.exp(
        jnp.arange(HEAD_SIZE // 2, dtype=f32) * (-2.0 * math.log(10000.0) / HEAD_SIZE)
    )
    angles = frequency[:, None] * place[None, :]
    cosine, sine = jnp.cos(angles), jnp.sin(angles)
    seg_row, seg_col = segment[None, :], segment[:, None]
    by_chunk = segment.reshape(group // CHUNK, CHUNK)
    last = by_chunk[:, -1:]
    prior = jnp.concatenate([jnp.full((1, 1), -1, jnp.int32), last[:-1]], axis=0)
    marks = jnp.stack(
        [
            by_chunk,
            (by_chunk == prior).astype(jnp.int32),
            (by_chunk == last).astype(jnp.int32),
            jnp.broadcast_to((last == prior).astype(jnp.int32), by_chunk.shape),
        ]
    ).reshape(4, group)
    marks = jnp.concatenate([marks, jnp.zeros((4, group), jnp.int32)], axis=0).astype(f32)
    seg_col_f = seg_col.astype(f32)
    distance = jnp.arange(F, dtype=jnp.int32) ^ mine
    kvmap = jnp.minimum(mine * heads_q + jnp.arange(heads_q), QUERY_HEADS - 1) // HEADS_PER_GROUP
    kvmap = jnp.concatenate([kvmap.astype(jnp.int32), distance.astype(jnp.int32)])

    both = permute(jnp.concatenate([tokens, cotangent], axis=0))
    x_float = both[:rows].astype(f32)
    cot = both[rows:]
    normed_own = rms_scale(x_float, gains[0]).astype(bf16)

    if aligned:
        down_shards = jnp.concatenate(
            [
                pad_rows(w_attn_out.reshape(rows_o, D), pad_o),
                pad_rows(w_mamba_out.reshape(rows_m, D), pad_m),
                pad_rows(w_ffn_down.reshape(rows_f, D), pad_f),
            ],
            axis=0,
        )
        down_shards = permute(down_shards)
        down_shards, w_inner, w_gate_z, w_query = tie(down_shards, w_inner, w_gate_z, w_query)
        out_both = lax.all_gather(down_shards[: pad_o + pad_m], "rep", axis=0)
        w_o_part = out_both[:, :rows_o].reshape(R * rows_o, D)
        w_m_part = out_both[:, pad_o:].reshape(R * pad_m, D)
        down_late = down_shards[pad_o + pad_m :]
    else:
        w_o_part, w_m_part = rep_gather(w_attn_out, D), rep_gather(w_mamba_out, D)
        down_late = w_ffn_down

    wq, wk, wv = read(w_query, D), read(w_key, KV), read(w_value, KV)
    wx, wz = read(w_inner, MI), read(w_gate_z, MI)
    wbc, wdt = read(w_bc, 2 * NS), read(w_step, MH)
    wq = place_columns(wq, 0, F * width_q)
    column_blocks = []
    for d in range(F):
        cols = slice(per_dev * d, per_dev * (d + 1))
        column_blocks.append(
            jnp.concatenate(
                [
                    wk,
                    wv,
                    wq[:, width_q * d : width_q * (d + 1)],
                    place_columns(wx[:, cols], shift[d], channels),
                    place_columns(wz[:, cols], shift[d], channels),
                    wbc,
                    place_columns(
                        wdt[:, first_head[d] : first_head[d] + heads_s], 0, width_ssm - at_step
                    ),
                ],
                axis=1,
            )
        )
    in_sent = take_blocks(jnp.stack(column_blocks))
    in_got = send_to_peers(in_sent[1:])
    normed_own, in_sent[0] = tie(normed_own, in_sent[0])
    normed_got = tie(*send_to_peers([normed_own] * (F - 1)))
    in_got, w_ffn_gate, w_ffn_up = tie(in_got, w_ffn_gate, w_ffn_up)
    in_part = place_blocks(in_sent[0], in_got)
    spread_f = one_hot(
        width_f,
        hidden_dev,
        lambda c: jnp.where(c % pad_f < rows_f, c // pad_f * rows_f + c % pad_f, -1),
    )
    gate_up = jnp.stack([read(w_ffn_gate, FF), read(w_ffn_up, FF)])
    gate_up = gate_up.reshape(2, depth, F, hidden_dev).transpose(2, 1, 0, 3)
    if width_f != hidden_dev:
        gate_up = dot(gate_up.reshape(-1, hidden_dev), spread_f, 1, 1).astype(bf16)
    gate_up = gate_up.reshape(F, depth, 2 * width_f)
    normed = place_blocks(normed_own, normed_got).reshape(group, D)
    w_o_sent, normed = tie(w_o_part, normed)
    w_o_got = send_to_peers([w_o_sent] * (F - 1))
    w_att = collect(in_part[:, :, :width_att])
    w_ssm = collect(in_part[:, :, width_att:])

    proj_att = dot(w_att, normed, 0, 1)
    attn_args = (cosine, sine, seg_row, seg_col)
    attn_t, q_t, k_t, k_n, v_n = attn_fwd(
        kvmap, proj_att.reshape(-1, HEAD_SIZE, group), *attn_args, F
    )
    attn_t, w_o_got = tie(attn_t, w_o_got)
    attn_parts = take_blocks(attn_t.reshape(F, width_q, rows))
    attn_got = send_to_peers(attn_parts[1:])
    attn_parts[0], cot_sent = tie(attn_parts[0], cot)
    cot_parts = send_to_peers([cot_sent] * (F - 1))
    own_shift = (mine * per_dev) % HEAD_SIZE
    own_head = (mine * per_dev) // HEAD_SIZE

    def channel_source(c):
        c = c - own_shift
        return jnp.where((c >= 0) & (c < per_dev), c // rows_m * pad_m + c % rows_m, -1)

    spread_m = one_hot(channels, blocks * pad_m, channel_source)
    w_m = dot(spread_m, w_m_part, 1, 0).astype(bf16)

    proj_ssm = dot(w_ssm, normed, 0, 1)

    attn_got, gate_up, proj_ssm = tie(attn_got, gate_up, proj_ssm)
    gate_up = take_blocks(gate_up)
    gate_up_got = send_to_peers(gate_up[1:])
    w_gu = collect(place_blocks(gate_up[0], gate_up_got))
    if aligned:
        w_down = lax.all_gather(down_late, "rep", axis=0, tiled=True)
    else:
        w_down = rep_gather(down_late, D)

    def own_heads(v):
        v = jnp.pad(v, (0, STEP_ROWS))
        return lax.dynamic_slice_in_dim(v, own_head, STEP_ROWS, 0)

    ssm_args = (
        proj_ssm,
        own_heads(step_bias)[:, None],
        jnp.exp(own_heads(decay_log))[:, None],
        marks,
        seg_col_f,
        own_heads(skip_gain),
    )
    y_t, mixed_t, states = ssm_fwd(heads_s, *ssm_args)
    mixed_t, cot_parts = tie(mixed_t, cot_parts)
    mamba_parts = take_blocks(row_blocks(row_major(dot(mixed_t, w_m, 0, 0).astype(bf16))))
    mamba_got = send_to_peers(mamba_parts[1:])

    w_o_got, attn_got, mamba_parts[0] = tie(w_o_got, attn_got, mamba_parts[0])
    w_o = row_major(place_blocks(w_o_sent, w_o_got)).reshape(D, D)
    attn_tok = row_major(place_blocks(attn_parts[0], attn_got)).reshape(F * width_q, rows)[:D]
    attn_proj = dot(attn_tok, w_o, 0, 0)
    branch_attn = rms_scale(attn_proj, gains[1])
    mamba_got, branch_attn = tie(mamba_got, branch_attn)
    mamba_proj = add_up(mamba_parts[0], mamba_got)
    branch_mamba = rms_scale(mamba_proj, gains[2])
    mix = x_float + 0.5 * (branch_attn + branch_mamba)

    def by_distance(own, received):
        return jnp.concatenate([own] + list(received), axis=0)

    def scatter_start(partial):
        parts = [partial[rows * k : rows * (k + 1)] for k in range(F)]
        return parts[0], send_to_peers(parts[1:])

    normed_two = rms_scale(mix, gains[3]).astype(bf16)
    normed_two = by_distance(normed_two, send_to_peers([normed_two] * (F - 1)))
    cot_all = by_distance(cot, cot_parts)
    gate_and_up = dot(normed_two, w_gu, 1, 0)
    fgate, fup = gate_and_up[:, :width_f], gate_and_up[:, width_f:]
    hidden = (silu(fgate) * fup).astype(bf16)
    g_hidden = dot(cot_all, w_down, 1, 1)
    g_fgate = (g_hidden * fup * silu_slope(fgate)).astype(bf16)
    g_fup = (g_hidden * silu(fgate)).astype(bf16)
    g_gu = jnp.concatenate([g_fgate, g_fup], axis=1)
    g_gu, hidden = tie(g_gu, hidden)
    g_two_partial = row_major(dot(g_gu, w_gu, 1, 1).astype(bf16))
    g_two_own, g_two_got = scatter_start(g_two_partial)
    g_gu, hidden, g_two_own = tie(g_gu, hidden, g_two_own)
    grad_gu = dot(normed_two, g_gu, 0, 0).astype(bf16)
    grad_down = row_major(dot(hidden, cot_all, 0, 0).astype(bf16))
    g_two_got, grad_gu, grad_down = tie(g_two_got, grad_gu, grad_down)
    g_mix_norm, g_gain_three = norm_back(add_up(g_two_own, g_two_got), mix, gains[3])
    g_mix = cot.astype(f32) + g_mix_norm

    def over_rep(grad):
        if aligned:
            return lax.psum_scatter(grad, "rep", scatter_dimension=0, tiled=True)
        return grad

    def to_owners(part):
        return exchange(part.reshape(F, depth, part.shape[1]))

    def finish(matrix):
        flat = matrix.reshape(-1)
        if aligned:
            return flat.astype(f32)
        return lax.psum_scatter(flat, "rep", scatter_dimension=0, tiled=True).astype(f32)

    gu_part, down_part = over_rep(grad_gu), over_rep(grad_down)

    g_branch = 0.5 * g_mix
    g_attn_proj, g_gain_one = norm_back(g_branch, attn_proj, gains[1])
    g_attn_proj = g_attn_proj.astype(bf16)
    g_mamba_proj, g_gain_two = norm_back(g_branch, mamba_proj, gains[2])
    g_mamba_proj = g_mamba_proj.astype(bf16)
    g_attn_tok = row_major(dot(w_o, g_attn_proj, 1, 1).astype(bf16))
    g_attn_tok, attn_late, hidden = tie(g_attn_tok, attn_tok, hidden)
    g_attn_parts = jnp.pad(g_attn_tok, ((0, F * width_q - D), (0, 0)))
    g_attn_parts = take_blocks(g_attn_parts.reshape(F, heads_q, HEAD_SIZE, rows))
    g_attn_got = send_to_peers(g_attn_parts[1:])
    grad_o = row_major(dot(attn_late, g_attn_proj, 1, 0).astype(bf16))
    grad_o = take_blocks(row_blocks(grad_o))
    out_partial = row_major(dot(hidden, w_down, 1, 0).astype(bf16))
    g_attn_got, grad_o, out_partial = tie(g_attn_got, grad_o, out_partial)
    g_mamba_sent, g_attn_got = tie(g_mamba_proj, g_attn_got)
    g_mamba_got = send_to_peers([g_mamba_sent] * (F - 1))
    g_attn_blocks = jnp.stack([g_attn_parts[0]] + g_attn_got)
    g_att = attn_bwd(kvmap, g_attn_blocks, q_t, k_n, k_t, v_n, *attn_args)
    g_att = g_att.reshape(width_att, group)
    g_mamba_got, g_att, out_partial = tie(g_mamba_got, g_att, out_partial)
    out_own, out_got = scatter_start(out_partial)
    g_mamba_all = place_blocks(g_mamba_sent, g_mamba_got).reshape(group, D)
    g_gated = dot(w_m, g_mamba_all, 1, 1)
    grad_m = row_major(dot(mixed_t, g_mamba_all, 1, 0).astype(bf16))
    grad_m = row_major(dot(spread_m, grad_m, 0, 0).astype(bf16))
    g_gated, grad_m = tie(g_gated, grad_m)
    g_ssm, sums = ssm_bwd(heads_s, *ssm_args, g_gated, y_t, states)

    out_got, g_ssm, gu_part, down_part, grad_o = tie(out_got, g_ssm, gu_part, down_part, grad_o)
    grad_o_got = send_to_peers(grad_o[1:])
    g_in = jnp.concatenate([g_att, g_ssm], axis=0)
    grad_in = dot(normed, g_in, 0, 1).astype(bf16)
    g_att, g_ssm, grad_in = tie(g_att, g_ssm, grad_in)
    in_part = over_rep(grad_in)
    g_normed = dot(g_att, w_att, 0, 1) + dot(g_ssm, w_ssm, 0, 1)
    g_normed, grad_o_got = tie(row_major(g_normed.astype(bf16)), grad_o_got)
    g_normed = take_blocks(row_blocks(g_normed))
    g_normed_got = send_to_peers(g_normed[1:])
    grad_o = add_up(grad_o[0], grad_o_got).astype(bf16)
    if aligned:
        grad_o = jnp.pad(grad_o.reshape(R, rows_o, D), ((0, 0), (0, pad_o - rows_o), (0, 0)))
        joined = jnp.concatenate([grad_o, grad_m.reshape(R, pad_m, D)], axis=1)
        g_normed_got, gu_part, in_part, joined = tie(g_normed_got, gu_part, in_part, joined)
        joined = over_rep(joined.reshape(R * (pad_o + pad_m), D))
    g_normed = add_up(g_normed[0], g_normed_got)
    gu_back = to_owners(gu_part).reshape(F, depth, 2, width_f)
    if width_f != hidden_dev:
        gu_back = dot(gu_back.reshape(-1, width_f), spread_f, 1, 0).astype(bf16)
    gu_back = gu_back.reshape(F, depth, 2, hidden_dev).transpose(2, 1, 0, 3)
    grad_gate = finish(gu_back[0].reshape(depth, FF))
    grad_up = finish(gu_back[1].reshape(depth, FF))
    grad_down = finish(restore(down_part)[:rows_f])
    if aligned:
        joined = restore(joined)
        grad_attn_out = finish(joined[:rows_o])
        grad_mamba_out = finish(joined[pad_o : pad_o + rows_m])
    else:
        grad_attn_out, grad_mamba_out = finish(grad_o), finish(grad_m)
    g_x_norm, g_gain_zero = norm_back(g_normed, x_float, gains[0])
    grad_tokens = g_mix + g_x_norm
    output = restore((mix + add_up(out_own, out_got)).astype(bf16))
    if aligned:
        grad_tokens = dot(grad_tokens, order.astype(f32), 1, 0, lax.Precision.HIGH)

    head_sums = jnp.sum(sums, axis=1).reshape(3, STEP_ROWS)
    head_sums = lax.dynamic_update_slice(
        jnp.zeros((3, MH + STEP_ROWS), f32), head_sums, (0, own_head)
    )[:, :MH]
    small = jnp.concatenate(
        [g_gain_zero, g_gain_one, g_gain_two, g_gain_three, head_sums.reshape(-1)]
    )
    in_back = to_owners(in_part)
    att_back, ssm_back = in_back[:, :, :width_att], in_back[:, :, width_att:]
    wide_att = att_back[:, :, : 2 * KV].astype(f32)
    grad_query = jnp.concatenate([att_back[d][:, 2 * KV :] for d in range(F)], axis=1)
    grad_query = finish(grad_query[:, :D])
    grad_key = finish(jnp.sum(wide_att[:, :, :KV], axis=0))
    grad_value = finish(jnp.sum(wide_att[:, :, KV:], axis=0))

    wide_ssm = ssm_back[:, :, at_small:].astype(f32)

    def channel_columns(start):
        return finish(
            jnp.concatenate(
                [
                    ssm_back[d][:, start + shift[d] : start + shift[d] + per_dev]
                    for d in range(F)
                ],
                axis=1,
            )
        )

    grad_inner = channel_columns(0)
    grad_gate_z = channel_columns(channels)
    grad_bc = finish(jnp.sum(wide_ssm[:, :, : 2 * NS], axis=0))
    grad_step = finish(
        sum(
            place_columns(wide_ssm[d][:, 2 * NS : 2 * NS + heads_s], first_head[d], MH)
            for d in range(F)
        )
    )

    small_rows = pad_to(small.shape[0], 1024) // 128
    small = jnp.pad(small, (0, small_rows * 128 - small.shape[0])).reshape(small_rows, 128)
    small = all_sum(small).reshape(-1)
    gain_grads = small[: 4 * D].reshape(4, D)
    bias_grad, decay_grad, skip_grad = (
        small[4 * D + MH * i : 4 * D + MH * (i + 1)] for i in range(3)
    )
    if aligned:
        gain_grads = gain_grads.reshape(4, R, F, depth).transpose(0, 2, 1, 3).reshape(4, D)
    return (
        output,
        grad_tokens,
        grad_query,
        grad_key,
        grad_value,
        grad_attn_out,
        grad_inner,
        grad_gate_z,
        grad_bc,
        grad_step,
        grad_mamba_out,
        grad_gate,
        grad_up,
        grad_down,
        gain_grads,
        bias_grad,
        decay_grad,
        skip_grad,
    )


def solution(mesh):
    split_tokens = P(("rep", "fsdp"), None)
    flat = P(("fsdp", "rep"))
    placed = (split_tokens, P("rep", None)) + (flat,) * 12 + (P(),) * 4 + (split_tokens,)
    return jax.shard_map(
        local,
        mesh=mesh,
        in_specs=placed,
        out_specs=(split_tokens, split_tokens) + (flat,) * 12 + (P(),) * 4,
        check_vma=False,
    )
```

time: 5380 us -> 851 us (0.16)
  waiting for transfers between devices: 2110 us -> 263 us
  other arithmetic: 1470 us -> 36 us
  local copies, waits for them, and re-layouts: 867 us -> 110 us
  matrix products: 648 us -> 245 us
  blocking collectives: 213 us -> 0 us
  Pallas kernels: 0 us -> 107 us
  starting transfers between devices: 12.3 us -> 70 us
    unnamed x14 -> x9, waiting for transfers between devices: 2030 us -> 0.83 us
    all_gather x10 -> x0, other arithmetic: 1300 us -> none  [the longest x1 344 us: local(): lax.all_gather(w_ffn_up, ('fsdp', 'rep'), axis=0, tiled=True)]
    reshape x34 -> x31, local copies, waits for them, and re-layouts: 454 us -> 25.8 us  [the longest x3 4.76 us: collect(): part = part.reshape(F * depth, part.shape[2])]
    dot_general x144 -> x26, matrix products: 648 us -> 245 us  [dot(): lax.dot_general(a, b, (((ca,), (cb,)), ((), ())), precision=precision, pr...]
    ppermute x6 -> x53, waiting for transfers between devices: 0.02 us -> 254 us  [the longest x48 253 us: send_to_peers(): lax.ppermute(parts[k - 1], 'fsdp', peers(devices, k))]
    all_gather x4 -> x0, blocking collectives: 151 us -> none  [the longest x1 55.6 us: local(): lax.all_gather(w_value, ('fsdp', 'rep'), axis=0, tiled=True)]
    dynamic_update_slice x90 -> x25, local copies, waits for them, and re-layouts: 141 us -> 25.1 us  [the longest x24 24.8 us: place_blocks(): lax.dynamic_update_index_in_dim(result, received[k - 1], mine ^ k, 0)]
    pallas_call x0 -> x4, Pallas kernels: none -> 107 us  [the longest x1 39.7 us: attn_bwd(): pl.pallas_call(functools.partial(attn_bwd_kernel, blocks=group // QUERY_B...]
  transfers between devices with their start and end apart: 17 -> 62, of which waited for: 4 -> 28; matrix products, arithmetic and copies ran while one was open for 44% -> 35% of each run, Pallas kernels for 0% -> 13%
where the time goes in v1:
time: 851 us; the launch traced here: 846 us
  waiting for transfers between devices  263 us (31%)
  matrix products  245 us (29%)
  local copies, waits for them, and re-layouts  110 us (13%)
  Pallas kernels  107 us (13%)
  starting transfers between devices  70 us (8%)
  other arithmetic  36 us (4%)
  between operations  15.8 us (2%)
    ppermute x48, waiting for transfers between devices, send_to_peers(): lax.ppermute(parts[k - 1], 'fsdp', peers(devices, k))  253 us
    dot_general x26, matrix products, dot(): lax.dot_general(a, b, (((ca,), (cb,)), ((), ())), precision=precision, pr...  245 us
    ppermute x48, starting transfers between devices, send_to_peers(): lax.ppermute(parts[k - 1], 'fsdp', peers(devices, k))  58 us
    pallas_call x1, Pallas kernels, attn_bwd(): pl.pallas_call(functools.partial(attn_bwd_kernel, blocks=group // QUERY_B...  39.7 us
    pallas_call x1, Pallas kernels, ssm_bwd(): pl.pallas_call(functools.partial(ssm_bwd_kernel, heads=heads), out_shape=...  26.7 us
    pallas_call x1, Pallas kernels, attn_fwd(): pl.pallas_call(functools.partial(attn_fwd_kernel, blocks=group // QUERY_B...  25.9 us
    dynamic_update_slice x24, local copies, waits for them, and re-layouts, place_blocks(): lax.dynamic_update_index_in_dim(result, received[k - 1], mine ^ k, 0)  24.8 us
  transfers between devices with their start and end apart: 62, of which 28 were waited for; matrix products, arithmetic and copies ran while one was open for 35% of the time, Pallas kernels for 13%

profile of v1, /device:TPU:0, one launch (start us, length us, event | category | flops | bytes accessed | tf_op | source)
XLA Modules:
  0.0 845.6 jit_solution(5388166398614048122)
XLA Ops:
  19.6 4.0 collective-permute-start.2
  25.1 6.1 fusion.23
  32.9 4.8 collective-permute-done.1
  50.2 3.5 reshape.460
  53.7 15.3 %collective-permute-done.5 = bf16[320,1600]{1,0:T(8,128)(2,1)} collective-permute-done((bf16[320,1600]{1,0:T(8,128)(2,1)}, bf16[320,1600]{1,0:T(8,128)(2,1)}, u32[]{:S(2)}, u32[]{:S(2)}) %collective-permute-start.5) | collective-permute-done | bytes 1024032 | tf_op jit(solution)/shard_map/ppermute | solution.py:515
  69.1 21.6 %collective-permute-done.4 = bf16[320,1600]{1,0:T(8,128)(2,1)} collective-permute-done((bf16[320,1600]{1,0:T(8,128)(2,1)}, bf16[320,1600]{1,0:T(8,128)(2,1)}, u32[]{:S(2)}, u32[]{:S(2)}) %collective-permute-start.4) | collective-permute-done | bytes 1024032 | tf_op jit(solution)/shard_map/ppermute | solution.py:515
  108.0 3.5 fusion.24
  112.8 11.2 %fusion.137 = f32[1088,1280]{1,0:T(8,128)} fusion(bf16[1600,1088]{1,0:T(8,128)(2,1)} %all-gather.7.cloned.1.call-done, bf16[1280,1600]{1,0:T(8,128)(2,1)} %bitcast.16), kind=kOutput, calls=%fused_computation.331 | convolution fusion | flops 4456448000 | bytes 13148160 | tf_op jit(solution)/shard_map/dot_general | solution.py:64
  123.9 25.9 %attn_fwd.1 = (bf16[4,7,64,320]{3,2,1,0:T(8,128)(2,1)}, bf16[7,64,1280]{2,1,0:T(8,128)(2,1)S(1)}, bf16[5,64,1280]{2,1,0:T(8,128)(2,1)S(1)}, bf16[5,1280,64]{2,1,0:T(8,128)(2,1)}, bf16[5,1280,64]{2,1,0:T(8,128)(2,1)}) custom-call(s32[11]{0:T(128)S(1)} %pad_add_fusion.3.kvmap, f32[17,64,1280]{2,1,0:T(8,128)} %bitcast.252, f32[17,64,1280]{2,1,0:T(8,128)} %bitcast.253, ...), custom_call_target="tpu_custom_call" | custom-call | flops 1638400 | bytes 81920 | tf_op jit(solution)/shard_map/attn_fwd/pallas_call | solution.py:153
  149.9 15.3 %collective-permute-done.7 = bf16[400,1600]{1,0:T(8,128)(2,1)} collective-permute-done((bf16[400,1600]{1,0:T(8,128)(2,1)}, bf16[400,1600]{1,0:T(8,128)(2,1)}, u32[]{:S(2)}, u32[]{:S(2)}) %collective-permute-start.7) | collective-permute-done | bytes 1280032 | tf_op jit(solution)/shard_map/ppermute | solution.py:515
  171.5 13.9 %fusion.138.p_ref = f32[1728,1280]{1,0:T(8,128)} fusion(bf16[1600,1728]{1,0:T(8,128)(2,1)} %all-gather.9.cloned.1.call-done, bf16[1280,1600]{1,0:T(8,128)(2,1)} %bitcast.16), kind=kOutput, calls=%fused_computation.332 | convolution fusion | flops 7077888000 | bytes 18472960 | tf_op jit(solution)/shard_map/dot_general | solution.py:64
  189.9 6.8 collective-permute-done.21
  198.6 6.2 collective-permute-done.22
  221.0 5.0 convolution_convert_fusion.9
  226.0 14.1 %ssm_fwd.1 = (f32[832,1280]{1,0:T(8,128)}, bf16[832,1280]{1,0:T(8,128)(2,1)S(1)}, f32[10,832,16]{2,1,0:T(8,128)}) custom-call(f32[1728,1280]{1,0:T(8,128)} %fusion.138.p_ref, f32[16,1]{1,0:T(8,128)S(1)} %copy.83.bias, f32[16,1]{1,0:T(8,128)S(1)} %copy.84.decay, f32[8,1280]{1,0:T(8,128)S(1)} %pad_convert_fusion.marks, ...), custom_call_target="tpu_custom_call" | custom-call | flops 1638400 | bytes 81920 | tf_op jit(solution)/shard_map/ssm_fwd/pallas_call | solution.py:338
  242.3 18.8 %collective-permute-done.13 = bf16[320,1600]{1,0:T(8,128)(2,1)S(1)} collective-permute-done((bf16[320,1600]{1,0:T(8,128)(2,1)}, bf16[320,1600]{1,0:T(8,128)(2,1)S(1)}, u32[]{:S(2)}, u32[]{:S(2)}) %collective-permute-start.13) | collective-permute-done | bytes 1024032 | tf_op jit(solution)/shard_map/ppermute | solution.py:515
  261.2 7.6 convolution_convert_fusion.6
  285.1 11.3 %collective-permute-done.17 = bf16[320,1600]{1,0:T(8,128)(2,1)S(1)} collective-permute-done((bf16[320,1600]{1,0:T(8,128)(2,1)S(1)}, bf16[320,1600]{1,0:T(8,128)(2,1)S(1)}, u32[]{:S(2)}, u32[]{:S(2)}) %collective-permute-start.17) | collective-permute-done | bytes 1024032 | tf_op jit(solution)/shard_map/ppermute | solution.py:515
  296.5 22.0 %collective-permute-done.16 = bf16[320,1600]{1,0:T(8,128)(2,1)S(1)} collective-permute-done((bf16[320,1600]{1,0:T(8,128)(2,1)S(1)}, bf16[320,1600]{1,0:T(8,128)(2,1)S(1)}, u32[]{:S(2)}, u32[]{:S(2)}) %collective-permute-start.16) | collective-permute-done | bytes 1024032 | tf_op jit(solution)/shard_map/ppermute | solution.py:515
  326.0 23.8 %collective-permute-done.20 = bf16[320,1600]{1,0:T(8,128)(2,1)S(1)} collective-permute-done((bf16[320,1600]{1,0:T(8,128)(2,1)S(1)}, bf16[320,1600]{1,0:T(8,128)(2,1)S(1)}, u32[]{:S(2)}, u32[]{:S(2)}) %collective-permute-start.20) | collective-permute-done | bytes 1024032 | tf_op jit(solution)/shard_map/ppermute | solution.py:515
  349.8 21.8 %collective-permute-done.19 = bf16[320,1600]{1,0:T(8,128)(2,1)S(1)} collective-permute-done((bf16[320,1600]{1,0:T(8,128)(2,1)S(1)}, bf16[320,1600]{1,0:T(8,128)(2,1)S(1)}, u32[]{:S(2)}, u32[]{:S(2)}) %collective-permute-start.19) | collective-permute-done | bytes 1024032 | tf_op jit(solution)/shard_map/ppermute | solution.py:515
  372.6 22.7 %fusion.68 = f32[1280,2816]{1,0:T(8,128)} fusion(bf16[1600,2816]{1,0:T(8,128)(2,1)} %all-gather.13.cloned.1.call-done, bf16[320,1600]{1,0:T(8,128)(2,1)} %copy-done.63, bf16[320,1600]{1,0:T(8,128)(2,1)} %copy-done.65, bf16[320,1600]{1,0:T(8,128)(2,1)} %collective-permute-done.18, bf16[320,1600]{1,0:T(8,128)(2,1)} %copy-done.32), kind=kOutput, calls=%fused_computation.140 | convolution fusion | flops 11550720000 | bytes 27525120 | tf_op jit(solution)/shard_map/dot_general | solution.py:64
  395.3 17.8 %multiply_convert_fusion.2 = (bf16[1280,1408]{1,0:T(8,128)(2,1)}, bf16[1280,1408]{1,0:T(8,128)(2,1)}, bf16[1280,1408]{1,0:T(8,128)(2,1)}) fusion(f32[1280,2816]{1,0:T(8,128)} %fusion.68, bf16[1408,1600]{1,0:T(8,128)(2,1)} %all-gather.11.cloned.1.call-done, bf16[320,1600]{1,0:T(8,128)(2,1)} %copy-done.60, bf16[320,1600]{1,0:T(8,128)(2,1)} %copy-done.61, ...), kind=kOutput, calls=%fused_computation.27 | convolution fusion | flops 5810585600 | bytes 33832960 | tf_op jit(solution)/shard_map/dot_general | solution.py:64
  413.2 6.6 pad_maximum_fusion
  419.7 18.3 %convolution_convert_fusion.5 = bf16[1280,1600]{1,0:T(8,128)(2,1)S(1)} fusion(bf16[1280,2816]{1,0:T(8,128)(2,1)} %pad_maximum_fusion, bf16[1600,2816]{1,0:T(8,128)(2,1)} %all-gather.13.cloned.1.call-done), kind=kOutput, calls=%fused_computation.19 | convolution fusion | flops 11536384000 | bytes 20316160 | tf_op jit(solution)/shard_map/dot_general | solution.py:64
  443.8 16.6 %convolution_convert_fusion.1 = bf16[1600,2816]{1,0:T(8,128)(2,1)} fusion(bf16[1280,2816]{1,0:T(8,128)(2,1)S(1)} %copy-done.22, bf16[320,1600]{1,0:T(8,128)(2,1)S(1)} %copy-done.64, bf16[320,1600]{1,0:T(8,128)(2,1)S(1)} %copy-done.66, bf16[320,1600]{1,0:T(8,128)(2,1)} %collective-permute-done.18, bf16[320,1600]{1,0:T(8,128)(2,1)S(1)} %copy-done.33), kind=kOutput, calls=%fused_computation.1 | convolution fusion | flops 11555225600 | bytes 20316160 | tf_op jit(solution)/shard_map/dot_general | solution.py:64
  460.4 12.2 %convolution_convert_fusion.4 = bf16[1408,1600]{1,0:T(8,128)(2,1)} fusion(bf16[1280,1408]{1,0:T(8,128)(2,1)} %get-tuple-element.179, bf16[320,1600]{1,0:T(8,128)(2,1)} %copy-done.60, bf16[320,1600]{1,0:T(8,128)(2,1)} %copy-done.61, bf16[320,1600]{1,0:T(8,128)(2,1)} %copy-done.62, bf16[320,1600]{1,0:T(8,128)(2,1)} %slice.397), kind=kOutput, calls=%fused_computation.18 | convolution fusion | flops 5785804800 | bytes 12206080 | tf_op jit(solution)/shard_map/dot_general | solution.py:64
  472.7 17.4 %collective-permute-done.26 = bf16[320,1600]{1,0:T(8,128)(2,1)} collective-permute-done((bf16[320,1600]{1,0:T(8,128)(2,1)}, bf16[320,1600]{1,0:T(8,128)(2,1)}, u32[]{:S(2)}, u32[]{:S(2)}) %collective-permute-start.26) | collective-permute-done | bytes 1024032 | tf_op jit(solution)/shard_map/ppermute | solution.py:515
  496.6 5.9 multiply_reduce_fusion.1
  510.7 3.6 convolution_convert_fusion.3
  514.4 7.4 convolution_convert_fusion.2
  529.8 39.7 %attn_bwd.1 = bf16[17,64,1280]{2,1,0:T(8,128)(2,1)} custom-call(s32[11]{0:T(128)S(1)} %copy-done.5, bf16[4,7,64,320]{3,2,1,0:T(8,128)(2,1)} %pad_maximum_fusion.3.refs_0_.refs_1_.refs_2_.refs_3_, bf16[4,7,64,320]{3,2,1,0:T(8,128)(2,1)} %pad_maximum_fusion.3.refs_0_.refs_1_.refs_2_.refs_3_, ...), custom_call_target="tpu_custom_call" | custom-call | flops 1638400 | bytes 81920 | tf_op jit(solution)/shard_map/attn_bwd/pallas_call | solution.py:242
  569.5 4.5 collective-permute-done.31
  584.8 13.7 %convolution_convert_fusion.7 = bf16[832,1600]{1,0:T(8,128)(2,1)} fusion(s32[832]{0:T(1024)S(1)} %copy-done.54, bf16[832,1280]{1,0:T(8,128)(2,1)S(1)} %copy-done.7, bf16[1280,1600]{1,0:T(8,128)(2,1)} %bitcast.68), kind=kOutput, calls=%fused_computation.46 | convolution fusion | flops 5626343424 | bytes 8891648 | tf_op jit(solution)/shard_map/dot_general | solution.py:64
  598.5 9.4 %fusion.139.up_ref = f32[832,1280]{1,0:T(8,128)} fusion(bf16[832,1600]{1,0:T(8,128)(2,1)} %convolution_convert_fusion.9, bf16[1280,1600]{1,0:T(8,128)(2,1)} %bitcast.68), kind=kOutput, calls=%fused_computation.333 | convolution fusion | flops 3407872000 | bytes 11018240 | tf_op jit(solution)/shard_map/dot_general | solution.py:64
  607.9 26.7 %ssm_bwd.1 = (bf16[1728,1280]{1,0:T(8,128)(2,1)}, f32[48,128]{1,0:T(8,128)S(1)}) custom-call(f32[1728,1280]{1,0:T(8,128)} %fusion.138.p_ref, f32[16,1]{1,0:T(8,128)S(1)} %copy.83.bias, f32[16,1]{1,0:T(8,128)S(1)} %copy.84.decay, f32[8,1280]{1,0:T(8,128)S(1)} %copy-done.3, f32[1280,1]{1,0:T(8,128)S(1)} %copy-done.1, f32[16]{0:T(128)S(1)} %pad_dynamic-slice_fusion.skip, ...), custom_call_target="tpu_custom_call" | custom-call | flops 1638400 | bytes 81920 | tf_op jit(solution)/shard_map/ssm_bwd/pallas_call | solution.py:466
  634.7 7.1 reduce-scatter.5.cloned.1.call-done
  641.8 19.3 %convolution_convert_fusion = bf16[1600,2816]{1,0:T(8,128)(2,1)} fusion(bf16[1280,1600]{1,0:T(8,128)(2,1)} %bitcast.16, bf16[1728,1280]{1,0:T(8,128)(2,1)} %get-tuple-element.212, bf16[1088,1280]{1,0:T(8,128)(2,1)} %bitcast.265), kind=kOutput, calls=%fused_computation | convolution fusion | flops 11553259520 | bytes 20316160 | tf_op jit(solution)/shard_map/dot_general | solution.py:64
  665.3 10.9 %fusion.140 = f32[1280,1600]{1,0:T(8,128)} fusion(bf16[1088,1280]{1,0:T(8,128)(2,1)S(1)} %bitcast.266, bf16[1600,1088]{1,0:T(8,128)(2,1)} %all-gather.7.cloned.1.call-done), kind=kOutput, calls=%fused_computation.334 | convolution fusion | flops 4456448000 | bytes 14458880 | tf_op jit(solution)/shard_map/dot_general | solution.py:64
  676.2 14.1 %fusion.9 = bf16[1280,1600]{1,0:T(8,128)(2,1)S(1)} fusion(f32[1280,1600]{1,0:T(8,128)} %fusion.140, bf16[1728,1280]{1,0:T(8,128)(2,1)} %get-tuple-element.212, bf16[1600,1728]{1,0:T(8,128)(2,1)} %all-gather.9.cloned.1.call-done), kind=kOutput, calls=%fused_computation.15 | convolution fusion | flops 7081984000 | bytes 22241280 | tf_op jit(solution)/shard_map/dot_general | solution.py:64
  693.5 6.4 fusion.27
  699.9 20.8 %collective-permute-done.37 = bf16[400,1600]{1,0:T(8,128)(2,1)S(1)} collective-permute-done((bf16[400,1600]{1,0:T(8,128)(2,1)}, bf16[400,1600]{1,0:T(8,128)(2,1)S(1)}, u32[]{:S(2)}, u32[]{:S(2)}) %collective-permute-start.37) | collective-permute-done | bytes 1280032 | tf_op jit(solution)/shard_map/ppermute | solution.py:515
  728.0 4.1 fusion.20
  732.1 17.9 %collective-permute-done.41 = bf16[320,1600]{1,0:T(8,128)(2,1)S(1)} collective-permute-done((bf16[320,1600]{1,0:T(8,128)(2,1)}, bf16[320,1600]{1,0:T(8,128)(2,1)S(1)}, u32[]{:S(2)}, u32[]{:S(2)}) %collective-permute-start.41) | collective-permute-done | bytes 1024032 | tf_op jit(solution)/shard_map/ppermute | solution.py:515
  750.0 18.5 %collective-permute-done.40 = bf16[320,1600]{1,0:T(8,128)(2,1)} collective-permute-done((bf16[320,1600]{1,0:T(8,128)(2,1)}, bf16[320,1600]{1,0:T(8,128)(2,1)}, u32[]{:S(2)}, u32[]{:S(2)}) %collective-permute-start.40) | collective-permute-done | bytes 1024032 | tf_op jit(solution)/shard_map/ppermute | solution.py:515
  768.5 4.2 fusion.44
  787.3 5.7 collective-permute-start.51
  798.6 8.3 fusion.2
  (479 shorter events, 207.0 us)
Async XLA Ops:
  7.2 94.3 %all-gather.15.cloned.1.call-start = ((), (), s32[]{:S(2)}) async-start(), calls=%async_computation.12 | async-start | bytes 4792320 | tf_op jit(solution)/shard_map/all_gather | solution.py:691
  15.8 97.0 %all-gather.7.cloned.1.call-start = ((), (), s32[]{:S(2)}) async-start(), calls=%async_computation.4 | async-start | bytes 4147200 | tf_op jit(solution)/shard_map/all_gather | solution.py:647
  39.3 132.1 %all-gather.9.cloned.1.call-start = ((), (), s32[]{:S(2)}) async-start(), calls=%async_computation.5 | async-start | bytes 6451200 | tf_op jit(solution)/shard_map/all_gather | solution.py:647
  40.9 331.7 %all-gather.13.cloned.1.call-start = ((), (), s32[]{:S(2)}) async-start(), calls=%async_computation.7 | async-start | bytes 10137600 | tf_op jit(solution)/shard_map/all_gather | solution.py:647
  41.4 27.7 %collective-permute-start.5 = (bf16[320,1600]{1,0:T(8,128)(2,1)}, bf16[320,1600]{1,0:T(8,128)(2,1)}, u32[]{:S(2)}, u32[]{:S(2)}) collective-permute-start(bf16[320,1600]{1,0:T(8,128)(2,1)} %fusion.35), channel_id=1, source_target_pairs={{0,24},{8,16},{16,8},{24,0},{1,25},{9,17},{17,9},{25,1},{2,26},{10... | collective-permute-start | bytes 3072008 | tf_op jit(solution)/shard_map/ppermute | solution.py:515
  43.0 47.8 %collective-permute-start.4 = (bf16[320,1600]{1,0:T(8,128)(2,1)}, bf16[320,1600]{1,0:T(8,128)(2,1)}, u32[]{:S(2)}, u32[]{:S(2)}) collective-permute-start(bf16[320,1600]{1,0:T(8,128)(2,1)} %fusion.35), channel_id=1, source_target_pairs={{0,16},{8,24},{16,0},{24,8},{1,17},{9,25},{17,1},{25,9},{2,18},{10... | collective-permute-start | bytes 3072008 | tf_op jit(solution)/shard_map/ppermute | solution.py:515
  44.4 46.6 %collective-permute-start.3 = (bf16[320,1600]{1,0:T(8,128)(2,1)}, bf16[320,1600]{1,0:T(8,128)(2,1)}, u32[]{:S(2)}, u32[]{:S(2)}) collective-permute-start(bf16[320,1600]{1,0:T(8,128)(2,1)} %fusion.35), channel_id=1, source_target_pairs={{0,8},{8,0},{16,24},{24,16},{1,9},{9,1},{17,25},{25,17},{2,10},{10... | collective-permute-start | bytes 3072008 | tf_op jit(solution)/shard_map/ppermute | solution.py:515
  104.5 45.4 %collective-permute-start.8 = (bf16[400,1600]{1,0:T(8,128)(2,1)}, bf16[400,1600]{1,0:T(8,128)(2,1)}, u32[]{:S(2)}, u32[]{:S(2)}) collective-permute-start(bf16[400,1600]{1,0:T(8,128)(2,1)} %reshape.454), channel_id=1, source_target_pairs={{0,24},{8,16},{16,8},{24,0},{1,25},{9,17},{17,9},{25,1},{2,26},{10... | collective-permute-start | bytes 3840008 | tf_op jit(solution)/shard_map/ppermute | solution.py:515
  105.9 59.3 %collective-permute-start.7 = (bf16[400,1600]{1,0:T(8,128)(2,1)}, bf16[400,1600]{1,0:T(8,128)(2,1)}, u32[]{:S(2)}, u32[]{:S(2)}) collective-permute-start(bf16[400,1600]{1,0:T(8,128)(2,1)} %reshape.454), channel_id=1, source_target_pairs={{0,16},{8,24},{16,0},{24,8},{1,17},{9,25},{17,1},{25,9},{2,18},{10... | collective-permute-start | bytes 3840008 | tf_op jit(solution)/shard_map/ppermute | solution.py:515
  107.3 58.1 %collective-permute-start.6 = (bf16[400,1600]{1,0:T(8,128)(2,1)}, bf16[400,1600]{1,0:T(8,128)(2,1)}, u32[]{:S(2)}, u32[]{:S(2)}) collective-permute-start(bf16[400,1600]{1,0:T(8,128)(2,1)} %reshape.454), channel_id=1, source_target_pairs={{0,8},{8,0},{16,24},{24,16},{1,9},{9,1},{17,25},{25,17},{2,10},{10... | collective-permute-start | bytes 3840008 | tf_op jit(solution)/shard_map/ppermute | solution.py:515
  167.7 17.7 %collective-permute-start.11 = (bf16[448,320]{1,0:T(8,128)(2,1)}, bf16[448,320]{1,0:T(8,128)(2,1)}, u32[]{:S(2)}, u32[]{:S(2)}) collective-permute-start(bf16[448,320]{1,0:T(8,128)(2,1)} %get-tuple-element.281), channel_id=1, source_target_pairs={{0,24},{8,16},{16,8},{24,0},{1,25},{9,17},{17,9},{25,1},{2,26},{10... | collective-permute-start | bytes 860168 | tf_op jit(solution)/shard_map/ppermute | solution.py:515
  169.1 16.9 %collective-permute-start.10 = (bf16[448,320]{1,0:T(8,128)(2,1)}, bf16[448,320]{1,0:T(8,128)(2,1)}, u32[]{:S(2)}, u32[]{:S(2)}) collective-permute-start(bf16[448,320]{1,0:T(8,128)(2,1)} %get-tuple-element.282), channel_id=1, source_target_pairs={{0,16},{8,24},{16,0},{24,8},{1,17},{9,25},{17,1},{25,9},{2,18},{10... | collective-permute-start | bytes 860168 | tf_op jit(solution)/shard_map/ppermute | solution.py:515
  170.5 15.8 %collective-permute-start.9 = (bf16[448,320]{1,0:T(8,128)(2,1)}, bf16[448,320]{1,0:T(8,128)(2,1)}, u32[]{:S(2)}, u32[]{:S(2)}) collective-permute-start(bf16[448,320]{1,0:T(8,128)(2,1)} %get-tuple-element.283), channel_id=1, source_target_pairs={{0,8},{8,0},{16,24},{24,16},{1,9},{9,1},{17,25},{25,17},{2,10},{10... | collective-permute-start | bytes 860168 | tf_op jit(solution)/shard_map/ppermute | solution.py:515
  187.8 17.9 %collective-permute-start.23 = (bf16[50,2816]{1,0:T(8,128)(2,1)S(1)}, bf16[50,2816]{1,0:T(8,128)(2,1)S(1)}, u32[]{:S(2)}, u32[]{:S(2)}) collective-permute-start(bf16[50,2816]{1,0:T(8,128)(2,1)S(1)} %get-tuple-element.300), channel_id=1, source_target_pairs={{0,24},{8,16},{16,8},{24,0},{1,25},{9,17},{17,9},{25,1},{2,26},{10... | collective-permute-start | bytes 844808 | tf_op jit(solution)/shard_map/ppermute | solution.py:515
  209.1 186.2 %all-gather.11.cloned.1.call-start = ((), (), s32[]{:S(2)}) async-start(), calls=%async_computation.6 | async-start | bytes 5271552 | tf_op jit(solution)/shard_map/all_gather | solution.py:771
  211.1 423.6 %reduce-scatter.7.cloned.1.call-start = ((), (), s32[]{:S(2)}) async-start(), calls=%async_computation.9 | async-start | bytes 5271552 | tf_op jit(solution)/shard_map/reduce_scatter | solution.py:831
  214.6 27.6 %collective-permute-start.14 = (bf16[320,1600]{1,0:T(8,128)(2,1)}, bf16[320,1600]{1,0:T(8,128)(2,1)S(1)}, u32[]{:S(2)}, u32[]{:S(2)}) collective-permute-start(bf16[320,1600]{1,0:T(8,128)(2,1)} %slice.397), channel_id=1, source_target_pairs={{0,24},{8,16},{16,8},{24,0},{1,25},{9,17},{17,9},{25,1},{2,26},{10... | collective-permute-start | bytes 3072008 | tf_op jit(solution)/shard_map/ppermute | solution.py:515
  216.1 44.9 %collective-permute-start.13 = (bf16[320,1600]{1,0:T(8,128)(2,1)}, bf16[320,1600]{1,0:T(8,128)(2,1)S(1)}, u32[]{:S(2)}, u32[]{:S(2)}) collective-permute-start(bf16[320,1600]{1,0:T(8,128)(2,1)} %slice.397), channel_id=1, source_target_pairs={{0,16},{8,24},{16,0},{24,8},{1,17},{9,25},{17,1},{25,9},{2,18},{10... | collective-permute-start | bytes 3072008 | tf_op jit(solution)/shard_map/ppermute | solution.py:515
  217.1 44.1 %collective-permute-start.12 = (bf16[320,1600]{1,0:T(8,128)(2,1)}, bf16[320,1600]{1,0:T(8,128)(2,1)S(1)}, u32[]{:S(2)}, u32[]{:S(2)}) collective-permute-start(bf16[320,1600]{1,0:T(8,128)(2,1)} %slice.397), channel_id=1, source_target_pairs={{0,8},{8,0},{16,24},{24,16},{1,9},{9,1},{17,25},{25,17},{2,10},{10... | collective-permute-start | bytes 3072008 | tf_op jit(solution)/shard_map/ppermute | solution.py:515
  269.1 27.4 %collective-permute-start.17 = (bf16[320,1600]{1,0:T(8,128)(2,1)S(1)}, bf16[320,1600]{1,0:T(8,128)(2,1)S(1)}, u32[]{:S(2)}, u32[]{:S(2)}) collective-permute-start(bf16[320,1600]{1,0:T(8,128)(2,1)S(1)} %get-tuple-element.271), channel_id=1, source_target_pairs={{0,24},{8,16},{16,8},{24,0},{1,25},{9,17},{17,9},{25,1},{2,26},{10... | collective-permute-start | bytes 3072008 | tf_op jit(solution)/shard_map/ppermute | solution.py:515
  271.6 46.9 %collective-permute-start.16 = (bf16[320,1600]{1,0:T(8,128)(2,1)S(1)}, bf16[320,1600]{1,0:T(8,128)(2,1)S(1)}, u32[]{:S(2)}, u32[]{:S(2)}) collective-permute-start(bf16[320,1600]{1,0:T(8,128)(2,1)S(1)} %get-tuple-element.272), channel_id=1, source_target_pairs={{0,16},{8,24},{16,0},{24,8},{1,17},{9,25},{17,1},{25,9},{2,18},{10... | collective-permute-start | bytes 3072008 | tf_op jit(solution)/shard_map/ppermute | solution.py:515
  272.6 46.0 %collective-permute-start.15 = (bf16[320,1600]{1,0:T(8,128)(2,1)S(1)}, bf16[320,1600]{1,0:T(8,128)(2,1)S(1)}, u32[]{:S(2)}, u32[]{:S(2)}) collective-permute-start(bf16[320,1600]{1,0:T(8,128)(2,1)S(1)} %get-tuple-element.273), channel_id=1, source_target_pairs={{0,8},{8,0},{16,24},{24,16},{1,9},{9,1},{17,25},{25,17},{2,10},{10... | collective-permute-start | bytes 3072008 | tf_op jit(solution)/shard_map/ppermute | solution.py:515
  322.4 27.4 %collective-permute-start.20 = (bf16[320,1600]{1,0:T(8,128)(2,1)S(1)}, bf16[320,1600]{1,0:T(8,128)(2,1)S(1)}, u32[]{:S(2)}, u32[]{:S(2)}) collective-permute-start(bf16[320,1600]{1,0:T(8,128)(2,1)S(1)} %multiply_convert_fusion.3), channel_id=1, source_target_pairs={{0,24},{8,16},{16,8},{24,0},{1,25},{9,17},{17,9},{25,1},{2,26},{10... | collective-permute-start | bytes 3072008 | tf_op jit(solution)/shard_map/ppermute | solution.py:515
  323.8 47.8 %collective-permute-start.19 = (bf16[320,1600]{1,0:T(8,128)(2,1)S(1)}, bf16[320,1600]{1,0:T(8,128)(2,1)S(1)}, u32[]{:S(2)}, u32[]{:S(2)}) collective-permute-start(bf16[320,1600]{1,0:T(8,128)(2,1)S(1)} %multiply_convert_fusion.3), channel_id=1, source_target_pairs={{0,16},{8,24},{16,0},{24,8},{1,17},{9,25},{17,1},{25,9},{2,18},{10... | collective-permute-start | bytes 3072008 | tf_op jit(solution)/shard_map/ppermute | solution.py:515
  324.8 47.7 %collective-permute-start.18 = (bf16[320,1600]{1,0:T(8,128)(2,1)S(1)}, bf16[320,1600]{1,0:T(8,128)(2,1)}, u32[]{:S(2)}, u32[]{:S(2)}) collective-permute-start(bf16[320,1600]{1,0:T(8,128)(2,1)S(1)} %multiply_convert_fusion.3), channel_id=1, source_target_pairs={{0,8},{8,0},{16,24},{24,16},{1,9},{9,1},{17,25},{25,17},{2,10},{10... | collective-permute-start | bytes 3072008 | tf_op jit(solution)/shard_map/ppermute | solution.py:515
  440.3 32.3 %collective-permute-start.25 = (bf16[320,1600]{1,0:T(8,128)(2,1)}, bf16[320,1600]{1,0:T(8,128)(2,1)}, u32[]{:S(2)}, u32[]{:S(2)}) collective-permute-start(bf16[320,1600]{1,0:T(8,128)(2,1)} %get-tuple-element.267), channel_id=1, source_target_pairs={{0,16},{8,24},{16,0},{24,8},{1,17},{9,25},{17,1},{25,9},{2,18},{10... | collective-permute-start | bytes 3072008 | tf_op jit(solution)/shard_map/ppermute | solution.py:515
  441.3 31.3 %collective-permute-start.24 = (bf16[320,1600]{1,0:T(8,128)(2,1)}, bf16[320,1600]{1,0:T(8,128)(2,1)}, u32[]{:S(2)}, u32[]{:S(2)}) collective-permute-start(bf16[320,1600]{1,0:T(8,128)(2,1)} %get-tuple-element.268), channel_id=1, source_target_pairs={{0,8},{8,0},{16,24},{24,16},{1,9},{9,1},{17,25},{25,17},{2,10},{10... | collective-permute-start | bytes 3072008 | tf_op jit(solution)/shard_map/ppermute | solution.py:515
  442.3 47.8 %collective-permute-start.26 = (bf16[320,1600]{1,0:T(8,128)(2,1)}, bf16[320,1600]{1,0:T(8,128)(2,1)}, u32[]{:S(2)}, u32[]{:S(2)}) collective-permute-start(bf16[320,1600]{1,0:T(8,128)(2,1)} %get-tuple-element.269), channel_id=1, source_target_pairs={{0,24},{8,16},{16,8},{24,0},{1,25},{9,17},{17,9},{25,1},{2,26},{10... | collective-permute-start | bytes 3072008 | tf_op jit(solution)/shard_map/ppermute | solution.py:515
  490.1 151.7 %reduce-scatter.5.cloned.1.call-start = ((), (), s32[]{:S(2)}) async-start(), calls=%async_computation.8 | async-start | bytes 10137600 | tf_op jit(solution)/shard_map/reduce_scatter | solution.py:831
  490.9 277.6 %reduce-scatter.9.cloned.1.call-start = ((), (), s32[]{:S(2)}) async-start(), calls=%async_computation.10 | async-start | bytes 10137600 | tf_op jit(solution)/shard_map/reduce_scatter | solution.py:831
  507.2 17.6 %collective-permute-start.29 = (bf16[7,64,320]{2,1,0:T(8,128)(2,1)S(1)}, bf16[7,64,320]{2,1,0:T(8,128)(2,1)S(1)}, u32[]{:S(2)}, u32[]{:S(2)}) collective-permute-start(bf16[7,64,320]{2,1,0:T(8,128)(2,1)S(1)} %get-tuple-element.277), channel_id=1, source_target_pairs={{0,24},{8,16},{16,8},{24,0},{1,25},{9,17},{17,9},{25,1},{2,26},{10... | collective-permute-start | bytes 860168 | tf_op jit(solution)/shard_map/ppermute | solution.py:515
  524.8 44.7 %collective-permute-start.32 = (bf16[320,1600]{1,0:T(8,128)(2,1)S(1)}, bf16[320,1600]{1,0:T(8,128)(2,1)S(1)}, u32[]{:S(2)}, u32[]{:S(2)}) collective-permute-start(bf16[320,1600]{1,0:T(8,128)(2,1)S(1)} %get-tuple-element.183), channel_id=1, source_target_pairs={{0,24},{8,16},{16,8},{24,0},{1,25},{9,17},{17,9},{25,1},{2,26},{10... | collective-permute-start | bytes 3072008 | tf_op jit(solution)/shard_map/ppermute | solution.py:515
  526.7 47.3 %collective-permute-start.31 = (bf16[320,1600]{1,0:T(8,128)(2,1)S(1)}, bf16[320,1600]{1,0:T(8,128)(2,1)S(1)}, u32[]{:S(2)}, u32[]{:S(2)}) collective-permute-start(bf16[320,1600]{1,0:T(8,128)(2,1)S(1)} %get-tuple-element.183), channel_id=1, source_target_pairs={{0,16},{8,24},{16,0},{24,8},{1,17},{9,25},{17,1},{25,9},{2,18},{10... | collective-permute-start | bytes 3072008 | tf_op jit(solution)/shard_map/ppermute | solution.py:515
  527.5 46.5 %collective-permute-start.30 = (bf16[320,1600]{1,0:T(8,128)(2,1)S(1)}, bf16[320,1600]{1,0:T(8,128)(2,1)S(1)}, u32[]{:S(2)}, u32[]{:S(2)}) collective-permute-start(bf16[320,1600]{1,0:T(8,128)(2,1)S(1)} %get-tuple-element.183), channel_id=1, source_target_pairs={{0,8},{8,0},{16,24},{24,16},{1,9},{9,1},{17,25},{25,17},{2,10},{10... | collective-permute-start | bytes 3072008 | tf_op jit(solution)/shard_map/ppermute | solution.py:515
  575.8 58.9 %collective-permute-start.35 = (bf16[320,1600]{1,0:T(8,128)(2,1)}, bf16[320,1600]{1,0:T(8,128)(2,1)}, u32[]{:S(2)}, u32[]{:S(2)}) collective-permute-start(bf16[320,1600]{1,0:T(8,128)(2,1)} %get-tuple-element.263), channel_id=1, source_target_pairs={{0,24},{8,16},{16,8},{24,0},{1,25},{9,17},{17,9},{25,1},{2,26},{10... | collective-permute-start | bytes 3072008 | tf_op jit(solution)/shard_map/ppermute | solution.py:515
  577.2 57.5 %collective-permute-start.34 = (bf16[320,1600]{1,0:T(8,128)(2,1)}, bf16[320,1600]{1,0:T(8,128)(2,1)}, u32[]{:S(2)}, u32[]{:S(2)}) collective-permute-start(bf16[320,1600]{1,0:T(8,128)(2,1)} %get-tuple-element.264), channel_id=1, source_target_pairs={{0,16},{8,24},{16,0},{24,8},{1,17},{9,25},{17,1},{25,9},{2,18},{10... | collective-permute-start | bytes 3072008 | tf_op jit(solution)/shard_map/ppermute | solution.py:515
  578.2 56.4 %collective-permute-start.33 = (bf16[320,1600]{1,0:T(8,128)(2,1)}, bf16[320,1600]{1,0:T(8,128)(2,1)}, u32[]{:S(2)}, u32[]{:S(2)}) collective-permute-start(bf16[320,1600]{1,0:T(8,128)(2,1)} %get-tuple-element.265), channel_id=1, source_target_pairs={{0,8},{8,0},{16,24},{24,16},{1,9},{9,1},{17,25},{25,17},{2,10},{10... | collective-permute-start | bytes 3072008 | tf_op jit(solution)/shard_map/ppermute | solution.py:515
  661.1 172.3 %reduce-scatter.11.cloned.1.call-start = ((), (), s32[]{:S(2)}) async-start(), calls=%async_computation.11 | async-start | bytes 4792320 | tf_op jit(solution)/shard_map/reduce_scatter | solution.py:831
  661.8 38.1 %collective-permute-start.36 = (bf16[400,1600]{1,0:T(8,128)(2,1)}, bf16[400,1600]{1,0:T(8,128)(2,1)S(1)}, u32[]{:S(2)}, u32[]{:S(2)}) collective-permute-start(bf16[400,1600]{1,0:T(8,128)(2,1)} %get-tuple-element.213), channel_id=1, source_target_pairs={{0,8},{8,0},{16,24},{24,16},{1,9},{9,1},{17,25},{25,17},{2,10},{10... | collective-permute-start | bytes 3840008 | tf_op jit(solution)/shard_map/ppermute | solution.py:515
  663.4 57.3 %collective-permute-start.37 = (bf16[400,1600]{1,0:T(8,128)(2,1)}, bf16[400,1600]{1,0:T(8,128)(2,1)S(1)}, u32[]{:S(2)}, u32[]{:S(2)}) collective-permute-start(bf16[400,1600]{1,0:T(8,128)(2,1)} %get-tuple-element.214), channel_id=1, source_target_pairs={{0,16},{8,24},{16,0},{24,8},{1,17},{9,25},{17,1},{25,9},{2,18},{10... | collective-permute-start | bytes 3840008 | tf_op jit(solution)/shard_map/ppermute | solution.py:515
  664.9 55.8 %collective-permute-start.38 = (bf16[400,1600]{1,0:T(8,128)(2,1)}, bf16[400,1600]{1,0:T(8,128)(2,1)S(1)}, u32[]{:S(2)}, u32[]{:S(2)}) collective-permute-start(bf16[400,1600]{1,0:T(8,128)(2,1)} %get-tuple-element.215), channel_id=1, source_target_pairs={{0,24},{8,16},{16,8},{24,0},{1,25},{9,17},{17,9},{25,1},{2,26},{10... | collective-permute-start | bytes 3840008 | tf_op jit(solution)/shard_map/ppermute | solution.py:515
  722.5 27.6 %collective-permute-start.41 = (bf16[320,1600]{1,0:T(8,128)(2,1)}, bf16[320,1600]{1,0:T(8,128)(2,1)S(1)}, u32[]{:S(2)}, u32[]{:S(2)}) collective-permute-start(bf16[320,1600]{1,0:T(8,128)(2,1)} %get-tuple-element.260), channel_id=1, source_target_pairs={{0,24},{8,16},{16,8},{24,0},{1,25},{9,17},{17,9},{25,1},{2,26},{10... | collective-permute-start | bytes 3072008 | tf_op jit(solution)/shard_map/ppermute | solution.py:515
  723.9 44.6 %collective-permute-start.40 = (bf16[320,1600]{1,0:T(8,128)(2,1)}, bf16[320,1600]{1,0:T(8,128)(2,1)}, u32[]{:S(2)}, u32[]{:S(2)}) collective-permute-start(bf16[320,1600]{1,0:T(8,128)(2,1)} %get-tuple-element.261), channel_id=1, source_target_pairs={{0,16},{8,24},{16,0},{24,8},{1,17},{9,25},{17,1},{25,9},{2,18},{10... | collective-permute-start | bytes 3072008 | tf_op jit(solution)/shard_map/ppermute | solution.py:515
  725.1 43.4 %collective-permute-start.39 = (bf16[320,1600]{1,0:T(8,128)(2,1)}, bf16[320,1600]{1,0:T(8,128)(2,1)}, u32[]{:S(2)}, u32[]{:S(2)}) collective-permute-start(bf16[320,1600]{1,0:T(8,128)(2,1)} %get-tuple-element.262), channel_id=1, source_target_pairs={{0,8},{8,0},{16,24},{24,16},{1,9},{9,1},{17,25},{25,17},{2,10},{10... | collective-permute-start | bytes 3072008 | tf_op jit(solution)/shard_map/ppermute | solution.py:515
  782.0 30.8 %collective-permute-start.44 = (bf16[50,2816]{1,0:T(8,128)(2,1)}, bf16[50,2816]{1,0:T(8,128)(2,1)}, u32[]{:S(2)}, u32[]{:S(2)}) collective-permute-start(bf16[50,2816]{1,0:T(8,128)(2,1)} %get-tuple-element.296), channel_id=1, source_target_pairs={{0,24},{8,16},{16,8},{24,0},{1,25},{9,17},{17,9},{25,1},{2,26},{10... | collective-permute-start | bytes 844808 | tf_op jit(solution)/shard_map/ppermute | solution.py:515
  783.4 28.5 %collective-permute-start.43 = (bf16[50,2816]{1,0:T(8,128)(2,1)}, bf16[50,2816]{1,0:T(8,128)(2,1)}, u32[]{:S(2)}, u32[]{:S(2)}) collective-permute-start(bf16[50,2816]{1,0:T(8,128)(2,1)} %get-tuple-element.297), channel_id=1, source_target_pairs={{0,16},{8,24},{16,0},{24,8},{1,17},{9,25},{17,1},{25,9},{2,18},{10... | collective-permute-start | bytes 844808 | tf_op jit(solution)/shard_map/ppermute | solution.py:515
  784.8 24.1 %collective-permute-start.42 = (bf16[50,2816]{1,0:T(8,128)(2,1)}, bf16[50,2816]{1,0:T(8,128)(2,1)}, u32[]{:S(2)}, u32[]{:S(2)}) collective-permute-start(bf16[50,2816]{1,0:T(8,128)(2,1)} %get-tuple-element.298), channel_id=1, source_target_pairs={{0,8},{8,0},{16,24},{24,16},{1,9},{9,1},{17,25},{25,17},{2,10},{10... | collective-permute-start | bytes 844808 | tf_op jit(solution)/shard_map/ppermute | solution.py:515
  794.1 31.4 %collective-permute-start.47 = (bf16[50,2816]{1,0:T(8,128)(2,1)}, bf16[50,2816]{1,0:T(8,128)(2,1)S(1)}, u32[]{:S(2)}, u32[]{:S(2)}) collective-permute-start(bf16[50,2816]{1,0:T(8,128)(2,1)} %get-tuple-element.284), channel_id=1, source_target_pairs={{0,24},{8,16},{16,8},{24,0},{1,25},{9,17},{17,9},{25,1},{2,26},{10... | collective-permute-start | bytes 844808 | tf_op jit(solution)/shard_map/ppermute | solution.py:515
  (89 other events, 991.8 us)
Sparse Core Ops, SparseCore 0:
  16.0 50.4 all-gather.14
  68.7 41.4 all-gather.6
  112.4 59.0 all-gather.8
  209.1 87.3 all-gather.12
  298.6 49.9 all-gather.10
  490.2 55.0 reduce-scatter.6
  547.7 94.0 reduce-scatter.4
  661.2 94.0 reduce-scatter.8
  776.5 55.4 reduce-scatter.10

commit v2 on v1

--- a/solution.py
+++ b/solution.py
@@ -485,6 +485,91 @@
     )(proj, bias, decay, marks, seg_col, skip, up_t, y_t, states)
 
 
+def ffn_middle_kernel(gate_up_ref, g_ref, hidden_ref, g_gu_ref):
+    width = g_ref.shape[1]
+    gate = gate_up_ref[:, :width].astype(f32)
+    up = gate_up_ref[:, width:].astype(f32)
+    g = g_ref[...].astype(f32)
+    sigmoid_v = jax.nn.sigmoid(gate)
+    passed = gate * sigmoid_v
+    hidden_ref[...] = (passed * up).astype(bf16)
+    slope = sigmoid_v * (1.0 + gate * (1.0 - sigmoid_v))
+    g_gu_ref[:, :width] = (g * up * slope).astype(bf16)
+    g_gu_ref[:, width:] = (g * passed).astype(bf16)
+
+
+def ffn_middle(gate_up, g_hidden):
+    group, width = g_hidden.shape
+    height = 128
+    narrow = pl.BlockSpec((height, width), lambda i: (i, 0))
+    wide = pl.BlockSpec((height, 2 * width), lambda i: (i, 0))
+    return pl.pallas_call(
+        ffn_middle_kernel,
+        out_shape=(
+            jax.ShapeDtypeStruct((group, width), bf16),
+            jax.ShapeDtypeStruct((group, 2 * width), bf16),
+        ),
+        grid=(group // height,),
+        in_specs=[wide, narrow],
+        out_specs=(narrow, wide),
+        compiler_params=pltpu.CompilerParams(vmem_limit_bytes=VMEM_BYTES),
+        name="ffn_middle",
+    )(gate_up, g_hidden)
+
+
+def weight_grads_kernel(rows_ref, g_ref, hidden_ref, cot_ref, wide_ref, down_ref, *, wide_steps):
+    i = pl.program_id(0)
+
+    @pl.when(i < wide_steps)
+    def _():
+        wide_ref[...] = dot(rows_ref[...], g_ref[...], 0, 0).astype(bf16)
+
+    @pl.when(i >= wide_steps)
+    def _():
+        down_ref[...] = dot(hidden_ref[...], cot_ref[...], 0, 0).astype(bf16)
+
+
+def ffn_weight_grads(rows, g_wide, hidden, cot):
+    group, depth = rows.shape
+    wide, width = g_wide.shape[1], hidden.shape[1]
+    columns, height = 256, 128
+    if wide % columns or width % height:
+        return (
+            dot(rows, g_wide, 0, 0).astype(bf16),
+            row_major(dot(hidden, cot, 0, 0).astype(bf16)),
+        )
+    wide_steps, down_steps = wide // columns, width // height
+
+    def first(i):
+        return jnp.minimum(i, wide_steps - 1)
+
+    def second(i):
+        return jnp.maximum(i - wide_steps, 0)
+
+    whole = pl.BlockSpec((group, depth), lambda i: (0, 0))
+    return pl.pallas_call(
+        functools.partial(weight_grads_kernel, wide_steps=wide_steps),
+        out_shape=(
+            jax.ShapeDtypeStruct((depth, wide), bf16),
+            jax.ShapeDtypeStruct((width, depth), bf16),
+        ),
+        grid=(wide_steps + down_steps,),
+        in_specs=[
+            whole,
+            pl.BlockSpec((group, columns), lambda i: (0, first(i))),
+            pl.BlockSpec((group, height), lambda i: (0, second(i))),
+            whole,
+        ],
+        out_specs=(
+            pl.BlockSpec((depth, columns), lambda i: (0, first(i))),
+            pl.BlockSpec((height, depth), lambda i: (second(i), 0)),
+        ),
+        compiler_params=pltpu.CompilerParams(vmem_limit_bytes=VMEM_BYTES),
+        cost_estimate=pl.CostEstimate(flops=group * group, bytes_accessed=group, transcendentals=0),
+        name="ffn_weight_grads",
+    )(rows, g_wide, hidden, cot)
+
+
 def pad_to(value, multiple):
     return -(-value // multiple) * multiple
 
@@ -513,6 +598,17 @@
 def send_to_peers(parts):
     devices = lax.axis_size("fsdp")
     return [lax.ppermute(parts[k - 1], "fsdp", peers(devices, k)) for k in range(1, devices)]
+
+
+def gather_start(part):
+    devices = lax.axis_size("fsdp")
+    if devices != 4:
+        return send_to_peers([part] * (devices - 1))
+    half = part.shape[0] // 2
+    one, two = (lax.ppermute(part, "fsdp", peers(devices, k)) for k in (1, 2))
+    upper = lax.ppermute(two[:half], "fsdp", peers(devices, 1))
+    lower = lax.ppermute(one[half:], "fsdp", peers(devices, 2))
+    return [one, two, jnp.concatenate([upper, lower], axis=0)]
 
 
 def place_blocks(own, received):
@@ -722,7 +818,7 @@
     in_sent = take_blocks(jnp.stack(column_blocks))
     in_got = send_to_peers(in_sent[1:])
     normed_own, in_sent[0] = tie(normed_own, in_sent[0])
-    normed_got = tie(*send_to_peers([normed_own] * (F - 1)))
+    normed_got = tie(*gather_start(normed_own))
     in_got, w_ffn_gate, w_ffn_up = tie(in_got, w_ffn_gate, w_ffn_up)
     in_part = place_blocks(in_sent[0], in_got)
     spread_f = one_hot(
@@ -736,7 +832,7 @@
         gate_up = dot(gate_up.reshape(-1, hidden_dev), spread_f, 1, 1).astype(bf16)
     gate_up = gate_up.reshape(F, depth, 2 * width_f)
     normed = place_blocks(normed_own, normed_got).reshape(group, D)
-    w_o_sent, normed = tie(w_o_part, normed)
+    w_o_sent, normed_late = tie(w_o_part, normed)
     w_o_got = send_to_peers([w_o_sent] * (F - 1))
     w_att = collect(in_part[:, :, :width_att])
     w_ssm = collect(in_part[:, :, width_att:])
@@ -763,7 +859,20 @@
 
     proj_ssm = dot(w_ssm, normed, 0, 1)
 
-    attn_got, gate_up, proj_ssm = tie(attn_got, gate_up, proj_ssm)
+    def own_heads(v):
+        v = jnp.pad(v, (0, STEP_ROWS))
+        return lax.dynamic_slice_in_dim(v, own_head, STEP_ROWS, 0)
+
+    ssm_args = (
+        proj_ssm,
+        own_heads(step_bias)[:, None],
+        jnp.exp(own_heads(decay_log))[:, None],
+        marks,
+        seg_col_f,
+        own_heads(skip_gain),
+    )
+    y_t, mixed_t, states = ssm_fwd(heads_s, *ssm_args)
+    attn_got, gate_up, mixed_t = tie(attn_got, gate_up, mixed_t)
     gate_up = take_blocks(gate_up)
     gate_up_got = send_to_peers(gate_up[1:])
     w_gu = collect(place_blocks(gate_up[0], gate_up_got))
@@ -772,56 +881,36 @@
     else:
         w_down = rep_gather(down_late, D)
 
-    def own_heads(v):
-        v = jnp.pad(v, (0, STEP_ROWS))
-        return lax.dynamic_slice_in_dim(v, own_head, STEP_ROWS, 0)
-
-    ssm_args = (
-        proj_ssm,
-        own_heads(step_bias)[:, None],
-        jnp.exp(own_heads(decay_log))[:, None],
-        marks,
-        seg_col_f,
-        own_heads(skip_gain),
-    )
-    y_t, mixed_t, states = ssm_fwd(heads_s, *ssm_args)
-    mixed_t, cot_parts = tie(mixed_t, cot_parts)
     mamba_parts = take_blocks(row_blocks(row_major(dot(mixed_t, w_m, 0, 0).astype(bf16))))
     mamba_got = send_to_peers(mamba_parts[1:])
 
-    w_o_got, attn_got, mamba_parts[0] = tie(w_o_got, attn_got, mamba_parts[0])
+    cot_parts, w_o_got, attn_got, mamba_parts[0] = tie(cot_parts, w_o_got, attn_got, mamba_parts[0])
     w_o = row_major(place_blocks(w_o_sent, w_o_got)).reshape(D, D)
     attn_tok = row_major(place_blocks(attn_parts[0], attn_got)).reshape(F * width_q, rows)[:D]
     attn_proj = dot(attn_tok, w_o, 0, 0)
     branch_attn = rms_scale(attn_proj, gains[1])
-    mamba_got, branch_attn = tie(mamba_got, branch_attn)
+    def by_distance(own, received):
+        return jnp.concatenate([own] + list(received), axis=0)
+
+    cot_all = by_distance(cot, cot_parts)
+    g_hidden = row_major(dot(cot_all, w_down, 1, 1).astype(bf16))
+    mamba_got, branch_attn, g_hidden = tie(mamba_got, branch_attn, g_hidden)
     mamba_proj = add_up(mamba_parts[0], mamba_got)
     branch_mamba = rms_scale(mamba_proj, gains[2])
     mix = x_float + 0.5 * (branch_attn + branch_mamba)
 
-    def by_distance(own, received):
-        return jnp.concatenate([own] + list(received), axis=0)
-
     def scatter_start(partial):
         parts = [partial[rows * k : rows * (k + 1)] for k in range(F)]
         return parts[0], send_to_peers(parts[1:])
 
     normed_two = rms_scale(mix, gains[3]).astype(bf16)
-    normed_two = by_distance(normed_two, send_to_peers([normed_two] * (F - 1)))
-    cot_all = by_distance(cot, cot_parts)
-    gate_and_up = dot(normed_two, w_gu, 1, 0)
-    fgate, fup = gate_and_up[:, :width_f], gate_and_up[:, width_f:]
-    hidden = (silu(fgate) * fup).astype(bf16)
-    g_hidden = dot(cot_all, w_down, 1, 1)
-    g_fgate = (g_hidden * fup * silu_slope(fgate)).astype(bf16)
-    g_fup = (g_hidden * silu(fgate)).astype(bf16)
-    g_gu = jnp.concatenate([g_fgate, g_fup], axis=1)
-    g_gu, hidden = tie(g_gu, hidden)
+    normed_two = by_distance(normed_two, gather_start(normed_two))
+    gate_and_up = row_major(dot(normed_two, w_gu, 1, 0).astype(bf16))
+    hidden, g_gu = ffn_middle(gate_and_up, g_hidden)
     g_two_partial = row_major(dot(g_gu, w_gu, 1, 1).astype(bf16))
     g_two_own, g_two_got = scatter_start(g_two_partial)
     g_gu, hidden, g_two_own = tie(g_gu, hidden, g_two_own)
-    grad_gu = dot(normed_two, g_gu, 0, 0).astype(bf16)
-    grad_down = row_major(dot(hidden, cot_all, 0, 0).astype(bf16))
+    grad_gu, grad_down = ffn_weight_grads(normed_two, g_gu, hidden, cot_all)
     g_two_got, grad_gu, grad_down = tie(g_two_got, grad_gu, grad_down)
     g_mix_norm, g_gain_three = norm_back(add_up(g_two_own, g_two_got), mix, gains[3])
     g_mix = cot.astype(f32) + g_mix_norm
@@ -873,7 +962,7 @@
     out_got, g_ssm, gu_part, down_part, grad_o = tie(out_got, g_ssm, gu_part, down_part, grad_o)
     grad_o_got = send_to_peers(grad_o[1:])
     g_in = jnp.concatenate([g_att, g_ssm], axis=0)
-    grad_in = dot(normed, g_in, 0, 1).astype(bf16)
+    grad_in = dot(normed_late, g_in, 0, 1).astype(bf16)
     g_att, g_ssm, grad_in = tie(g_att, g_ssm, grad_in)
     in_part = over_rep(grad_in)
     g_normed = dot(g_att, w_att, 0, 1) + dot(g_ssm, w_ssm, 0, 1)
@@ -884,7 +973,7 @@
     if aligned:
         grad_o = jnp.pad(grad_o.reshape(R, rows_o, D), ((0, 0), (0, pad_o - rows_o), (0, 0)))
         joined = jnp.concatenate([grad_o, grad_m.reshape(R, pad_m, D)], axis=1)
-        g_normed_got, gu_part, in_part, joined = tie(g_normed_got, gu_part, in_part, joined)
+        g_normed_got[0], gu_part, in_part, joined = tie(g_normed_got[0], gu_part, in_part, joined)
         joined = over_rep(joined.reshape(R * (pad_o + pad_m), D))
     g_normed = add_up(g_normed[0], g_normed_got)
     gu_back = to_owners(gu_part).reshape(F, depth, 2, width_f)
@@ -894,12 +983,6 @@
     grad_gate = finish(gu_back[0].reshape(depth, FF))
     grad_up = finish(gu_back[1].reshape(depth, FF))
     grad_down = finish(restore(down_part)[:rows_f])
-    if aligned:
-        joined = restore(joined)
-        grad_attn_out = finish(joined[:rows_o])
-        grad_mamba_out = finish(joined[pad_o : pad_o + rows_m])
-    else:
-        grad_attn_out, grad_mamba_out = finish(grad_o), finish(grad_m)
     g_x_norm, g_gain_zero = norm_back(g_normed, x_float, gains[0])
     grad_tokens = g_mix + g_x_norm
     output = restore((mix + add_up(out_own, out_got)).astype(bf16))
@@ -947,6 +1030,13 @@
     small_rows = pad_to(small.shape[0], 1024) // 128
     small = jnp.pad(small, (0, small_rows * 128 - small.shape[0])).reshape(small_rows, 128)
     small = all_sum(small).reshape(-1)
+    if aligned:
+        joined, small = tie(joined, small)
+        joined = restore(joined)
+        grad_attn_out = finish(joined[:rows_o])
+        grad_mamba_out = finish(joined[pad_o : pad_o + rows_m])
+    else:
+        grad_attn_out, grad_mamba_out = finish(grad_o), finish(grad_m)
     gain_grads = small[: 4 * D].reshape(4, D)
     bias_grad, decay_grad, skip_grad = (
         small[4 * D + MH * i : 4 * D + MH * (i + 1)] for i in range(3)

time: 851 us -> 836 us (0.982)
  waiting for transfers between devices: 263 us -> 215 us
  Pallas kernels: 107 us -> 148 us
  matrix products: 245 us -> 210 us
  local copies, waits for them, and re-layouts: 110 us -> 130 us
    ppermute x48 -> x42, waiting for transfers between devices: 253 us -> 134 us  [send_to_peers(): lax.ppermute(parts[k - 1], 'fsdp', peers(devices, k))]
    ppermute x0 -> x8, waiting for transfers between devices: none -> 57.5 us  [the longest x4 42.3 us: gather_start(): one, two = (lax.ppermute(part, 'fsdp', peers(devices, k)) for k in (1, 2))]
    pallas_call x0 -> x2, Pallas kernels: none -> 41.3 us  [the longest x1 29.8 us: ffn_weight_grads(): pl.pallas_call(functools.partial(weight_grads_kernel, wide_steps=wide_ste...]
    dot_general x26 -> x24, matrix products: 245 us -> 210 us  [dot(): lax.dot_general(a, b, (((ca,), (cb,)), ((), ())), precision=precision, pr...]
    ppermute x48 -> x42, starting transfers between devices: 58 us -> 50.2 us  [send_to_peers(): lax.ppermute(parts[k - 1], 'fsdp', peers(devices, k))]
  transfers between devices with their start and end apart: 62 -> 64, of which waited for: 28 -> 26; matrix products, arithmetic and copies ran while one was open for 35% -> 36% of each run, Pallas kernels for 13% -> 16%
where the time goes in v2:
time: 836 us; the launch traced here: 830 us
  waiting for transfers between devices  215 us (26%)
  matrix products  210 us (25%)
  Pallas kernels  148 us (18%)
  local copies, waits for them, and re-layouts  130 us (16%)
  starting transfers between devices  70.2 us (8%)
  other arithmetic  40.7 us (5%)
  between operations  15.8 us (2%)
    dot_general x24, matrix products, dot(): lax.dot_general(a, b, (((ca,), (cb,)), ((), ())), precision=precision, pr...  210 us
    ppermute x42, waiting for transfers between devices, send_to_peers(): lax.ppermute(parts[k - 1], 'fsdp', peers(devices, k))  134 us
    ppermute x42, starting transfers between devices, send_to_peers(): lax.ppermute(parts[k - 1], 'fsdp', peers(devices, k))  50.2 us
    ppermute x4, waiting for transfers between devices, gather_start(): one, two = (lax.ppermute(part, 'fsdp', peers(devices, k)) for k in (1, 2))  42.3 us
    pallas_call x1, Pallas kernels, attn_bwd(): pl.pallas_call(functools.partial(attn_bwd_kernel, blocks=group // QUERY_B...  40 us
    pallas_call x1, Pallas kernels, ffn_weight_grads(): pl.pallas_call(functools.partial(weight_grads_kernel, wide_steps=wide_ste...  29.8 us
    dynamic_update_slice x24, local copies, waits for them, and re-layouts, place_blocks(): lax.dynamic_update_index_in_dim(result, received[k - 1], mine ^ k, 0)  29.1 us
    pallas_call x1, Pallas kernels, ssm_bwd(): pl.pallas_call(functools.partial(ssm_bwd_kernel, heads=heads), out_shape=...  26.6 us
  transfers between devices with their start and end apart: 64, of which 26 were waited for; matrix products, arithmetic and copies ran while one was open for 36% of the time, Pallas kernels for 16%

profile of v2, /device:TPU:0, one launch (start us, length us, event | category | flops | bytes accessed | tf_op | source)
XLA Modules:
  0.0 829.9 jit_solution(8303988890284898570)
XLA Ops:
  19.6 4.0 collective-permute-start.2
  25.1 6.1 fusion.22
  31.9 5.8 collective-permute-done.1
  50.4 18.9 %collective-permute-done.4 = bf16[320,1600]{1,0:T(8,128)(2,1)} collective-permute-done((bf16[320,1600]{1,0:T(8,128)(2,1)S(1)}, bf16[320,1600]{1,0:T(8,128)(2,1)}, u32[]{:S(2)}, u32[]{:S(2)}) %collective-permute-start.4) | collective-permute-done | bytes 1024032 | tf_op jit(solution)/shard_map/ppermute | solution.py:608
  110.2 6.3 copy.89
  116.5 10.2 %fusion.130.kv_ref.q_ref = f32[17,64,1280]{2,1,0:T(8,128)} fusion(bf16[17,64,1600]{2,1,0:T(8,128)(2,1)} %bitcast.261, bf16[1280,1600,1]{1,0,2:T(8,128)(2,1)} %bitcast.18), kind=kOutput, calls=%fused_computation.325 | convolution fusion | flops 4456448000 | bytes 13148160 | tf_op jit(solution)/shard_map/dot_general | solution.py:64
  126.7 26.2 %attn_fwd.1 = (bf16[4,7,64,320]{3,2,1,0:T(8,128)(2,1)}, bf16[7,64,1280]{2,1,0:T(8,128)(2,1)S(1)}, bf16[5,64,1280]{2,1,0:T(8,128)(2,1)S(1)}, bf16[5,1280,64]{2,1,0:T(8,128)(2,1)}, bf16[5,1280,64]{2,1,0:T(8,128)(2,1)}) custom-call(s32[11]{0:T(128)S(1)} %pad_add_fusion.3.kvmap, f32[17,64,1280]{2,1,0:T(8,128)} %fusion.130.kv_ref.q_ref, ...), custom_call_target="tpu_custom_call" | custom-call | flops 1638400 | bytes 81920 | tf_op jit(solution)/shard_map/attn_fwd/pallas_call | solution.py:153
  153.9 5.0 collective-permute-done.8
  164.7 6.8 all-gather.9.cloned.1.call-done
  171.5 13.9 %fusion.131.p_ref = f32[1728,1280]{1,0:T(8,128)} fusion(bf16[1600,1728]{1,0:T(8,128)(2,1)} %all-gather.9.cloned.1.call-done, bf16[1280,1600]{1,0:T(8,128)(2,1)} %bitcast.17), kind=kOutput, calls=%fused_computation.326 | convolution fusion | flops 7077888000 | bytes 18472960 | tf_op jit(solution)/shard_map/dot_general | solution.py:64
  185.3 14.3 %ssm_fwd.1 = (f32[832,1280]{1,0:T(8,128)}, bf16[832,1280]{1,0:T(8,128)(2,1)S(1)}, f32[10,832,16]{2,1,0:T(8,128)}) custom-call(f32[1728,1280]{1,0:T(8,128)} %fusion.131.p_ref, f32[16,1]{1,0:T(8,128)S(1)} %copy.94.bias, f32[16,1]{1,0:T(8,128)S(1)} %copy.95.decay, f32[8,1280]{1,0:T(8,128)S(1)} %pad_convert_fusion.marks, ...), custom_call_target="tpu_custom_call" | custom-call | flops 1638400 | bytes 81920 | tf_op jit(solution)/shard_map/ssm_fwd/pallas_call | solution.py:338
  203.3 6.8 collective-permute-done.23
  212.0 6.6 collective-permute-done.24
  227.5 3.8 convolution_convert_fusion.9
  234.8 5.2 convolution_convert_fusion.6
  242.2 16.5 %collective-permute-done.18 = bf16[320,1600]{1,0:T(8,128)(2,1)S(1)} collective-permute-done((bf16[320,1600]{1,0:T(8,128)(2,1)S(1)}, bf16[320,1600]{1,0:T(8,128)(2,1)S(1)}, u32[]{:S(2)}, u32[]{:S(2)}) %collective-permute-start.18) | collective-permute-done | bytes 1024032 | tf_op jit(solution)/shard_map/ppermute | solution.py:600
  258.7 20.7 %collective-permute-done.17 = bf16[320,1600]{1,0:T(8,128)(2,1)S(1)} collective-permute-done((bf16[320,1600]{1,0:T(8,128)(2,1)S(1)}, bf16[320,1600]{1,0:T(8,128)(2,1)S(1)}, u32[]{:S(2)}, u32[]{:S(2)}) %collective-permute-start.17) | collective-permute-done | bytes 1024032 | tf_op jit(solution)/shard_map/ppermute | solution.py:600
  299.6 12.4 %convolution_convert_fusion.5.g_ref = bf16[1280,1408]{1,0:T(8,128)(2,1)} fusion(bf16[1408,1600]{1,0:T(8,128)(2,1)} %all-gather.11.cloned.1.call-done, bf16[320,1600]{1,0:T(8,128)(2,1)} %copy-done.34, bf16[320,1600]{1,0:T(8,128)(2,1)} %copy-done.36, bf16[320,1600]{1,0:T(8,128)(2,1)} %copy-done.38, bf16[320,1600]{1,0:T(8,128)(2,1)} %slice.407), kind=kOutput, calls=%fused_computation.19 | convolution fusion | flops 5785354240 | bytes 12206080 | tf_op jit(solution)/shard_map/dot_general | solution.py:64
  312.1 5.3 multiply_reduce_fusion.8
  318.7 10.4 %collective-permute-done.14 = bf16[320,1600]{1,0:T(8,128)(2,1)} collective-permute-done((bf16[320,1600]{1,0:T(8,128)(2,1)}, bf16[320,1600]{1,0:T(8,128)(2,1)}, u32[]{:S(2)}, u32[]{:S(2)}) %collective-permute-start.14) | collective-permute-done | bytes 1024032 | tf_op jit(solution)/shard_map/ppermute | solution.py:600
  336.8 23.4 %collective-permute-done.20 = bf16[320,1600]{1,0:T(8,128)(2,1)S(1)} collective-permute-done((bf16[320,1600]{1,0:T(8,128)(2,1)S(1)}, bf16[320,1600]{1,0:T(8,128)(2,1)S(1)}, u32[]{:S(2)}, u32[]{:S(2)}) %collective-permute-start.20) | collective-permute-done | bytes 1024032 | tf_op jit(solution)/shard_map/ppermute | solution.py:608
  364.7 8.9 %collective-permute-done.21 = bf16[160,1600]{1,0:T(8,128)(2,1)S(1)} collective-permute-done((bf16[160,1600]{1,0:T(8,128)(2,1)S(1)}, bf16[160,1600]{1,0:T(8,128)(2,1)S(1)}, u32[]{:S(2)}, u32[]{:S(2)}) %collective-permute-start.21) | collective-permute-done | bytes 512032 | tf_op jit(solution)/shard_map/ppermute | solution.py:609
  375.2 19.2 %convolution_convert_fusion.1.gate_up_ref = bf16[1280,2816]{1,0:T(8,128)(2,1)} fusion(bf16[1280,1600]{1,0:T(8,128)(2,1)} %constant_dynamic-update-slice_fusion.rows_ref, bf16[1600,2816]{1,0:T(8,128)(2,1)} %all-gather.13.cloned.1.call-done), kind=kOutput, calls=%fused_computation.1 | convolution fusion | flops 11537940480 | bytes 20316160 | tf_op jit(solution)/shard_map/dot_general | solution.py:64
  394.4 11.5 %ffn_middle.1 = (bf16[1280,1408]{1,0:T(8,128)(2,1)S(1)}, bf16[1280,2816]{1,0:T(8,128)(2,1)}) custom-call(bf16[1280,2816]{1,0:T(8,128)(2,1)} %convolution_convert_fusion.1.gate_up_ref, bf16[1280,1408]{1,0:T(8,128)(2,1)} %convolution_convert_fusion.5.g_ref), custom_call_target="tpu_custom_call" | custom-call | tf_op jit(solution)/shard_map/ffn_middle/pallas_call | solution.py:506
  405.9 19.8 %convolution_convert_fusion.4 = bf16[1280,1600]{1,0:T(8,128)(2,1)S(1)} fusion(bf16[1280,2816]{1,0:T(8,128)(2,1)} %get-tuple-element.173.g_ref, bf16[1600,2816]{1,0:T(8,128)(2,1)} %all-gather.13.cloned.1.call-done), kind=kOutput, calls=%fused_computation.18 | convolution fusion | flops 11536384000 | bytes 20316160 | tf_op jit(solution)/shard_map/dot_general | solution.py:64
  430.5 8.1 pad_maximum_fusion.cot_ref
  438.7 29.8 %ffn_weight_grads.1 = (bf16[1600,2816]{1,0:T(8,128)(2,1)}, bf16[1408,1600]{1,0:T(8,128)(2,1)}) custom-call(bf16[1280,1600]{1,0:T(8,128)(2,1)} %constant_dynamic-update-slice_fusion.rows_ref, bf16[1280,2816]{1,0:T(8,128)(2,1)} %get-tuple-element.173.g_ref, bf16[1280,1408]{1,0:T(8,128)(2,1)S(1)} %get-tuple-element.182.hidden_ref, ...), custom_call_target="tpu_custom_call" | custom-call | flops 1638400 | bytes 1280 | tf_op jit(solution)/shard_map/ffn_weight_grads/pallas_call | solution.py:550
  468.5 6.3 collective-permute-done.28
  482.3 4.8 multiply_reduce_fusion.1
  488.4 5.6 convolution_convert_fusion.10
  501.3 7.5 convolution_convert_fusion.2
  516.7 40.0 %attn_bwd.1 = bf16[17,64,1280]{2,1,0:T(8,128)(2,1)} custom-call(s32[11]{0:T(128)S(1)} %pad_add_fusion.3.kvmap, bf16[4,7,64,320]{3,2,1,0:T(8,128)(2,1)} %pad_maximum_fusion.1.refs_0_.refs_1_.refs_2_.refs_3_, bf16[4,7,64,320]{3,2,1,0:T(8,128)(2,1)} %pad_maximum_fusion.1.refs_0_.refs_1_.refs_2_.refs_3_, ...), custom_call_target="tpu_custom_call" | custom-call | flops 1638400 | bytes 81920 | tf_op jit(solution)/shard_map/attn_bwd/pallas_call | solution.py:242
  568.4 13.9 %convolution_convert_fusion.7 = bf16[832,1600]{1,0:T(8,128)(2,1)} fusion(s32[832]{0:T(1024)S(1)} %copy-done.59, bf16[832,1280]{1,0:T(8,128)(2,1)S(1)} %copy-done.6, bf16[1280,1600]{1,0:T(8,128)(2,1)} %bitcast.70), kind=kOutput, calls=%fused_computation.39 | convolution fusion | flops 5626343424 | bytes 8891648 | tf_op jit(solution)/shard_map/dot_general | solution.py:64
  582.3 9.3 %fusion.132.up_ref = f32[832,1280]{1,0:T(8,128)} fusion(bf16[832,1600]{1,0:T(8,128)(2,1)} %copy-done.68, bf16[1280,1600]{1,0:T(8,128)(2,1)} %bitcast.70), kind=kOutput, calls=%fused_computation.327 | convolution fusion | flops 3407872000 | bytes 11018240 | tf_op jit(solution)/shard_map/dot_general | solution.py:64
  591.6 26.6 %ssm_bwd.1 = (bf16[1728,1280]{1,0:T(8,128)(2,1)}, f32[48,128]{1,0:T(8,128)S(1)}) custom-call(f32[1728,1280]{1,0:T(8,128)} %fusion.131.p_ref, f32[16,1]{1,0:T(8,128)S(1)} %copy.94.bias, f32[16,1]{1,0:T(8,128)S(1)} %copy.95.decay, f32[8,1280]{1,0:T(8,128)S(1)} %pad_convert_fusion.marks, f32[1280,1]{1,0:T(8,128)S(1)} %reshape_convert_fusion.seg_col, ...), custom_call_target="tpu_custom_call" | custom-call | flops 1638400 | bytes 81920 | tf_op jit(solution)/shard_map/ssm_bwd/pallas_call | solution.py:466
  618.2 5.9 reduce-scatter.5.cloned.1.call-done
  624.2 19.2 %convolution_convert_fusion = bf16[1600,2816]{1,0:T(8,128)(2,1)} fusion(bf16[1280,1600]{1,0:T(8,128)(2,1)} %bitcast.17, bf16[1728,1280]{1,0:T(8,128)(2,1)} %get-tuple-element.216, bf16[1088,1280]{1,0:T(8,128)(2,1)} %bitcast.262), kind=kOutput, calls=%fused_computation | convolution fusion | flops 11553259520 | bytes 20316160 | tf_op jit(solution)/shard_map/dot_general | solution.py:64
  647.6 10.9 %fusion.133 = f32[1280,1600]{1,0:T(8,128)} fusion(bf16[1088,1280]{1,0:T(8,128)(2,1)S(1)} %bitcast.263, bf16[1600,1088]{1,0:T(8,128)(2,1)} %all-gather.7.cloned.1.call-done), kind=kOutput, calls=%fused_computation.328 | convolution fusion | flops 4456448000 | bytes 14458880 | tf_op jit(solution)/shard_map/dot_general | solution.py:64
  658.5 13.9 %fusion.9 = bf16[1280,1600]{1,0:T(8,128)(2,1)S(1)} fusion(f32[1280,1600]{1,0:T(8,128)} %fusion.133, bf16[1728,1280]{1,0:T(8,128)(2,1)} %get-tuple-element.216, bf16[1600,1728]{1,0:T(8,128)(2,1)} %all-gather.9.cloned.1.call-done), kind=kOutput, calls=%fused_computation.15 | convolution fusion | flops 7081984000 | bytes 22241280 | tf_op jit(solution)/shard_map/dot_general | solution.py:64
  675.6 6.4 fusion.26
  682.0 21.0 %collective-permute-done.39 = bf16[400,1600]{1,0:T(8,128)(2,1)S(1)} collective-permute-done((bf16[400,1600]{1,0:T(8,128)(2,1)}, bf16[400,1600]{1,0:T(8,128)(2,1)S(1)}, u32[]{:S(2)}, u32[]{:S(2)}) %collective-permute-start.39) | collective-permute-done | bytes 1280032 | tf_op jit(solution)/shard_map/ppermute | solution.py:600
  710.2 4.4 fusion.19
  714.7 16.7 %collective-permute-done.41 = bf16[320,1600]{1,0:T(8,128)(2,1)S(1)} collective-permute-done((bf16[320,1600]{1,0:T(8,128)(2,1)}, bf16[320,1600]{1,0:T(8,128)(2,1)S(1)}, u32[]{:S(2)}, u32[]{:S(2)}) %collective-permute-start.41) | collective-permute-done | bytes 1024032 | tf_op jit(solution)/shard_map/ppermute | solution.py:600
  731.4 6.3 reduce-scatter.9.cloned.1.call-done
  737.7 12.2 %collective-permute-done.43 = bf16[320,1600]{1,0:T(8,128)(2,1)} collective-permute-done((bf16[320,1600]{1,0:T(8,128)(2,1)}, bf16[320,1600]{1,0:T(8,128)(2,1)}, u32[]{:S(2)}, u32[]{:S(2)}) %collective-permute-start.43) | collective-permute-done | bytes 1024032 | tf_op jit(solution)/shard_map/ppermute | solution.py:600
  751.3 4.3 fusion.43
  770.8 5.6 collective-permute-start.50
  781.5 8.3 %fusion.2 = f32[320,1600]{1,0:T(8,128)} fusion(s32[1600]{0:T(1024)S(1)} %copy-done.55, f32[320,1600]{1,0:T(8,128)S(1)} %copy-done.19, f32[320,1600]{1,0:T(8,128)} %get-tuple-element.251, f32[320]{0:T(512)S(1)} %broadcast_multiply_fusion.2, f32[1600]{0:T(1024)S(1)} %copy-done.45, f32[320]{0:T(512)S(1)} %copy-done.53, bf16[640,1600]{1,0:T(8,128)(2,1)S(1)} %copy-done.17), kind=kOutput, calls=%fused_computation.5 | convolution fusion | flops 4922368000 | bytes 7311360 | tf_op jit(solution)/shard_map/dot_general | solution.py:64
  (484 shorter events, 239.3 us)
Async XLA Ops:
  7.2 90.0 %all-gather.15.cloned.1.call-start = ((), (), s32[]{:S(2)}) async-start(), calls=%async_computation.12 | async-start | bytes 4792320 | tf_op jit(solution)/shard_map/all_gather | solution.py:787
  15.8 94.4 %all-gather.7.cloned.1.call-start = ((), (), s32[]{:S(2)}) async-start(), calls=%async_computation.4 | async-start | bytes 4147200 | tf_op jit(solution)/shard_map/all_gather | solution.py:743
  40.3 131.1 %all-gather.9.cloned.1.call-start = ((), (), s32[]{:S(2)}) async-start(), calls=%async_computation.5 | async-start | bytes 6451200 | tf_op jit(solution)/shard_map/all_gather | solution.py:743
  44.0 255.7 %all-gather.11.cloned.1.call-start = ((), (), s32[]{:S(2)}) async-start(), calls=%async_computation.6 | async-start | bytes 5271552 | tf_op jit(solution)/shard_map/all_gather | solution.py:880
  44.0 25.3 %collective-permute-start.4 = (bf16[320,1600]{1,0:T(8,128)(2,1)S(1)}, bf16[320,1600]{1,0:T(8,128)(2,1)}, u32[]{:S(2)}, u32[]{:S(2)}) collective-permute-start(bf16[320,1600]{1,0:T(8,128)(2,1)S(1)} %fusion.34), channel_id=1, source_target_pairs={{0,16},{8,24},{16,0},{24,8},{1,17},{9,25},{17,1},{25,9},{2,18},{10... | collective-permute-start | bytes 3072008 | tf_op jit(solution)/shard_map/ppermute | solution.py:608
  45.4 27.5 %collective-permute-start.3 = (bf16[320,1600]{1,0:T(8,128)(2,1)S(1)}, bf16[320,1600]{1,0:T(8,128)(2,1)}, u32[]{:S(2)}, u32[]{:S(2)}) collective-permute-start(bf16[320,1600]{1,0:T(8,128)(2,1)S(1)} %fusion.34), channel_id=1, source_target_pairs={{0,8},{8,0},{16,24},{24,16},{1,9},{9,1},{17,25},{25,17},{2,10},{10... | collective-permute-start | bytes 3072008 | tf_op jit(solution)/shard_map/ppermute | solution.py:608
  48.1 327.1 %all-gather.13.cloned.1.call-start = ((), (), s32[]{:S(2)}) async-start(), calls=%async_computation.7 | async-start | bytes 10137600 | tf_op jit(solution)/shard_map/all_gather | solution.py:743
  100.2 53.7 %collective-permute-start.9 = (bf16[400,1600]{1,0:T(8,128)(2,1)}, bf16[400,1600]{1,0:T(8,128)(2,1)}, u32[]{:S(2)}, u32[]{:S(2)}) collective-permute-start(bf16[400,1600]{1,0:T(8,128)(2,1)} %reshape.454), channel_id=1, source_target_pairs={{0,24},{8,16},{16,8},{24,0},{1,25},{9,17},{17,9},{25,1},{2,26},{10... | collective-permute-start | bytes 3840008 | tf_op jit(solution)/shard_map/ppermute | solution.py:600
  101.9 57.0 %collective-permute-start.8 = (bf16[400,1600]{1,0:T(8,128)(2,1)}, bf16[400,1600]{1,0:T(8,128)(2,1)}, u32[]{:S(2)}, u32[]{:S(2)}) collective-permute-start(bf16[400,1600]{1,0:T(8,128)(2,1)} %reshape.454), channel_id=1, source_target_pairs={{0,16},{8,24},{16,0},{24,8},{1,17},{9,25},{17,1},{25,9},{2,18},{10... | collective-permute-start | bytes 3840008 | tf_op jit(solution)/shard_map/ppermute | solution.py:600
  102.2 56.7 %collective-permute-start.7 = (bf16[400,1600]{1,0:T(8,128)(2,1)}, bf16[400,1600]{1,0:T(8,128)(2,1)}, u32[]{:S(2)}, u32[]{:S(2)}) collective-permute-start(bf16[400,1600]{1,0:T(8,128)(2,1)} %reshape.454), channel_id=1, source_target_pairs={{0,8},{8,0},{16,24},{24,16},{1,9},{9,1},{17,25},{25,17},{2,10},{10... | collective-permute-start | bytes 3840008 | tf_op jit(solution)/shard_map/ppermute | solution.py:600
  161.2 38.4 %collective-permute-start.12 = (bf16[448,320]{1,0:T(8,128)(2,1)}, bf16[448,320]{1,0:T(8,128)(2,1)}, u32[]{:S(2)}, u32[]{:S(2)}) collective-permute-start(bf16[448,320]{1,0:T(8,128)(2,1)} %get-tuple-element.284), channel_id=1, source_target_pairs={{0,24},{8,16},{16,8},{24,0},{1,25},{9,17},{17,9},{25,1},{2,26},{10... | collective-permute-start | bytes 860168 | tf_op jit(solution)/shard_map/ppermute | solution.py:600
  162.9 36.7 %collective-permute-start.11 = (bf16[448,320]{1,0:T(8,128)(2,1)}, bf16[448,320]{1,0:T(8,128)(2,1)}, u32[]{:S(2)}, u32[]{:S(2)}) collective-permute-start(bf16[448,320]{1,0:T(8,128)(2,1)} %get-tuple-element.285), channel_id=1, source_target_pairs={{0,16},{8,24},{16,0},{24,8},{1,17},{9,25},{17,1},{25,9},{2,18},{10... | collective-permute-start | bytes 860168 | tf_op jit(solution)/shard_map/ppermute | solution.py:600
  163.7 35.9 %collective-permute-start.10 = (bf16[448,320]{1,0:T(8,128)(2,1)S(1)}, bf16[448,320]{1,0:T(8,128)(2,1)}, u32[]{:S(2)}, u32[]{:S(2)}) collective-permute-start(bf16[448,320]{1,0:T(8,128)(2,1)S(1)} %get-tuple-element.286), channel_id=1, source_target_pairs={{0,8},{8,0},{16,24},{24,16},{1,9},{9,1},{17,25},{25,17},{2,10},{10... | collective-permute-start | bytes 860168 | tf_op jit(solution)/shard_map/ppermute | solution.py:600
  201.3 18.0 %collective-permute-start.25 = (bf16[50,2816]{1,0:T(8,128)(2,1)S(1)}, bf16[50,2816]{1,0:T(8,128)(2,1)S(1)}, u32[]{:S(2)}, u32[]{:S(2)}) collective-permute-start(bf16[50,2816]{1,0:T(8,128)(2,1)S(1)} %get-tuple-element.303), channel_id=1, source_target_pairs={{0,24},{8,16},{16,8},{24,0},{1,25},{9,17},{17,9},{25,1},{2,26},{10... | collective-permute-start | bytes 844808 | tf_op jit(solution)/shard_map/ppermute | solution.py:600
  202.8 15.8 %collective-permute-start.24 = (bf16[50,2816]{1,0:T(8,128)(2,1)S(1)}, bf16[50,2816]{1,0:T(8,128)(2,1)S(1)}, u32[]{:S(2)}, u32[]{:S(2)}) collective-permute-start(bf16[50,2816]{1,0:T(8,128)(2,1)S(1)} %get-tuple-element.304), channel_id=1, source_target_pairs={{0,16},{8,24},{16,0},{24,8},{1,17},{9,25},{17,1},{25,9},{2,18},{10... | collective-permute-start | bytes 844808 | tf_op jit(solution)/shard_map/ppermute | solution.py:600
  222.7 395.5 %reduce-scatter.7.cloned.1.call-start = ((), (), s32[]{:S(2)}) async-start(), calls=%async_computation.9 | async-start | bytes 5271552 | tf_op jit(solution)/shard_map/reduce_scatter | solution.py:920
  231.3 27.4 %collective-permute-start.18 = (bf16[320,1600]{1,0:T(8,128)(2,1)S(1)}, bf16[320,1600]{1,0:T(8,128)(2,1)S(1)}, u32[]{:S(2)}, u32[]{:S(2)}) collective-permute-start(bf16[320,1600]{1,0:T(8,128)(2,1)S(1)} %copy-done.27), channel_id=1, source_target_pairs={{0,24},{8,16},{16,8},{24,0},{1,25},{9,17},{17,9},{25,1},{2,26},{10... | collective-permute-start | bytes 3072008 | tf_op jit(solution)/shard_map/ppermute | solution.py:600
  232.8 46.5 %collective-permute-start.17 = (bf16[320,1600]{1,0:T(8,128)(2,1)S(1)}, bf16[320,1600]{1,0:T(8,128)(2,1)S(1)}, u32[]{:S(2)}, u32[]{:S(2)}) collective-permute-start(bf16[320,1600]{1,0:T(8,128)(2,1)S(1)} %copy-done.27), channel_id=1, source_target_pairs={{0,16},{8,24},{16,0},{24,8},{1,17},{9,25},{17,1},{25,9},{2,18},{10... | collective-permute-start | bytes 3072008 | tf_op jit(solution)/shard_map/ppermute | solution.py:600
  234.3 45.1 %collective-permute-start.16 = (bf16[320,1600]{1,0:T(8,128)(2,1)S(1)}, bf16[320,1600]{1,0:T(8,128)(2,1)S(1)}, u32[]{:S(2)}, u32[]{:S(2)}) collective-permute-start(bf16[320,1600]{1,0:T(8,128)(2,1)S(1)} %copy-done.27), channel_id=1, source_target_pairs={{0,8},{8,0},{16,24},{24,16},{1,9},{9,1},{17,25},{25,17},{2,10},{10... | collective-permute-start | bytes 3072008 | tf_op jit(solution)/shard_map/ppermute | solution.py:600
  279.4 39.3 %collective-permute-start.15 = (bf16[320,1600]{1,0:T(8,128)(2,1)}, bf16[320,1600]{1,0:T(8,128)(2,1)}, u32[]{:S(2)}, u32[]{:S(2)}) collective-permute-start(bf16[320,1600]{1,0:T(8,128)(2,1)} %get-tuple-element.274), channel_id=1, source_target_pairs={{0,24},{8,16},{16,8},{24,0},{1,25},{9,17},{17,9},{25,1},{2,26},{10... | collective-permute-start | bytes 3072008 | tf_op jit(solution)/shard_map/ppermute | solution.py:600
  280.9 48.1 %collective-permute-start.14 = (bf16[320,1600]{1,0:T(8,128)(2,1)}, bf16[320,1600]{1,0:T(8,128)(2,1)}, u32[]{:S(2)}, u32[]{:S(2)}) collective-permute-start(bf16[320,1600]{1,0:T(8,128)(2,1)} %get-tuple-element.275), channel_id=1, source_target_pairs={{0,16},{8,24},{16,0},{24,8},{1,17},{9,25},{17,1},{25,9},{2,18},{10... | collective-permute-start | bytes 3072008 | tf_op jit(solution)/shard_map/ppermute | solution.py:600
  281.5 47.6 %collective-permute-start.13 = (bf16[320,1600]{1,0:T(8,128)(2,1)}, bf16[320,1600]{1,0:T(8,128)(2,1)}, u32[]{:S(2)}, u32[]{:S(2)}) collective-permute-start(bf16[320,1600]{1,0:T(8,128)(2,1)} %get-tuple-element.276), channel_id=1, source_target_pairs={{0,8},{8,0},{16,24},{24,16},{1,9},{9,1},{17,25},{25,17},{2,10},{10... | collective-permute-start | bytes 3072008 | tf_op jit(solution)/shard_map/ppermute | solution.py:600
  334.8 25.4 %collective-permute-start.20 = (bf16[320,1600]{1,0:T(8,128)(2,1)S(1)}, bf16[320,1600]{1,0:T(8,128)(2,1)S(1)}, u32[]{:S(2)}, u32[]{:S(2)}) collective-permute-start(bf16[320,1600]{1,0:T(8,128)(2,1)S(1)} %get-tuple-element.254), channel_id=1, source_target_pairs={{0,16},{8,24},{16,0},{24,8},{1,17},{9,25},{17,1},{25,9},{2,18},{10... | collective-permute-start | bytes 3072008 | tf_op jit(solution)/shard_map/ppermute | solution.py:608
  335.4 25.2 %collective-permute-start.19 = (bf16[320,1600]{1,0:T(8,128)(2,1)S(1)}, bf16[320,1600]{1,0:T(8,128)(2,1)S(1)}, u32[]{:S(2)}, u32[]{:S(2)}) collective-permute-start(bf16[320,1600]{1,0:T(8,128)(2,1)S(1)} %get-tuple-element.254), channel_id=1, source_target_pairs={{0,8},{8,0},{16,24},{24,16},{1,9},{9,1},{17,25},{25,17},{2,10},{10... | collective-permute-start | bytes 3072008 | tf_op jit(solution)/shard_map/ppermute | solution.py:608
  427.0 41.4 %collective-permute-start.27 = (bf16[320,1600]{1,0:T(8,128)(2,1)S(1)}, bf16[320,1600]{1,0:T(8,128)(2,1)}, u32[]{:S(2)}, u32[]{:S(2)}) collective-permute-start(bf16[320,1600]{1,0:T(8,128)(2,1)S(1)} %get-tuple-element.270), channel_id=1, source_target_pairs={{0,16},{8,24},{16,0},{24,8},{1,17},{9,25},{17,1},{25,9},{2,18},{10... | collective-permute-start | bytes 3072008 | tf_op jit(solution)/shard_map/ppermute | solution.py:600
  428.1 40.4 %collective-permute-start.26 = (bf16[320,1600]{1,0:T(8,128)(2,1)S(1)}, bf16[320,1600]{1,0:T(8,128)(2,1)}, u32[]{:S(2)}, u32[]{:S(2)}) collective-permute-start(bf16[320,1600]{1,0:T(8,128)(2,1)S(1)} %get-tuple-element.271), channel_id=1, source_target_pairs={{0,8},{8,0},{16,24},{24,16},{1,9},{9,1},{17,25},{25,17},{2,10},{10... | collective-permute-start | bytes 3072008 | tf_op jit(solution)/shard_map/ppermute | solution.py:600
  429.1 45.7 %collective-permute-start.28 = (bf16[320,1600]{1,0:T(8,128)(2,1)S(1)}, bf16[320,1600]{1,0:T(8,128)(2,1)}, u32[]{:S(2)}, u32[]{:S(2)}) collective-permute-start(bf16[320,1600]{1,0:T(8,128)(2,1)S(1)} %get-tuple-element.272), channel_id=1, source_target_pairs={{0,24},{8,16},{16,8},{24,0},{1,25},{9,17},{17,9},{25,1},{2,26},{10... | collective-permute-start | bytes 3072008 | tf_op jit(solution)/shard_map/ppermute | solution.py:600
  474.8 149.3 %reduce-scatter.5.cloned.1.call-start = ((), (), s32[]{:S(2)}) async-start(), calls=%async_computation.8 | async-start | bytes 10137600 | tf_op jit(solution)/shard_map/reduce_scatter | solution.py:920
  475.6 262.1 %reduce-scatter.9.cloned.1.call-start = ((), (), s32[]{:S(2)}) async-start(), calls=%async_computation.10 | async-start | bytes 10137600 | tf_op jit(solution)/shard_map/reduce_scatter | solution.py:920
  494.3 17.3 %collective-permute-start.31 = (bf16[7,64,320]{2,1,0:T(8,128)(2,1)S(1)}, bf16[7,64,320]{2,1,0:T(8,128)(2,1)S(1)}, u32[]{:S(2)}, u32[]{:S(2)}) collective-permute-start(bf16[7,64,320]{2,1,0:T(8,128)(2,1)S(1)} %get-tuple-element.280), channel_id=1, source_target_pairs={{0,24},{8,16},{16,8},{24,0},{1,25},{9,17},{17,9},{25,1},{2,26},{10... | collective-permute-start | bytes 860168 | tf_op jit(solution)/shard_map/ppermute | solution.py:600
  495.9 15.7 %collective-permute-start.30 = (bf16[7,64,320]{2,1,0:T(8,128)(2,1)S(1)}, bf16[7,64,320]{2,1,0:T(8,128)(2,1)S(1)}, u32[]{:S(2)}, u32[]{:S(2)}) collective-permute-start(bf16[7,64,320]{2,1,0:T(8,128)(2,1)S(1)} %get-tuple-element.281), channel_id=1, source_target_pairs={{0,16},{8,24},{16,0},{24,8},{1,17},{9,25},{17,1},{25,9},{2,18},{10... | collective-permute-start | bytes 860168 | tf_op jit(solution)/shard_map/ppermute | solution.py:600
  511.7 45.1 %collective-permute-start.34 = (bf16[320,1600]{1,0:T(8,128)(2,1)S(1)}, bf16[320,1600]{1,0:T(8,128)(2,1)S(1)}, u32[]{:S(2)}, u32[]{:S(2)}) collective-permute-start(bf16[320,1600]{1,0:T(8,128)(2,1)S(1)} %get-tuple-element.186), channel_id=1, source_target_pairs={{0,24},{8,16},{16,8},{24,0},{1,25},{9,17},{17,9},{25,1},{2,26},{10... | collective-permute-start | bytes 3072008 | tf_op jit(solution)/shard_map/ppermute | solution.py:600
  513.2 44.5 %collective-permute-start.33 = (bf16[320,1600]{1,0:T(8,128)(2,1)S(1)}, bf16[320,1600]{1,0:T(8,128)(2,1)S(1)}, u32[]{:S(2)}, u32[]{:S(2)}) collective-permute-start(bf16[320,1600]{1,0:T(8,128)(2,1)S(1)} %get-tuple-element.186), channel_id=1, source_target_pairs={{0,16},{8,24},{16,0},{24,8},{1,17},{9,25},{17,1},{25,9},{2,18},{10... | collective-permute-start | bytes 3072008 | tf_op jit(solution)/shard_map/ppermute | solution.py:600
  514.0 43.8 %collective-permute-start.32 = (bf16[320,1600]{1,0:T(8,128)(2,1)S(1)}, bf16[320,1600]{1,0:T(8,128)(2,1)S(1)}, u32[]{:S(2)}, u32[]{:S(2)}) collective-permute-start(bf16[320,1600]{1,0:T(8,128)(2,1)S(1)} %get-tuple-element.186), channel_id=1, source_target_pairs={{0,8},{8,0},{16,24},{24,16},{1,9},{9,1},{17,25},{25,17},{2,10},{10... | collective-permute-start | bytes 3072008 | tf_op jit(solution)/shard_map/ppermute | solution.py:600
  559.5 58.7 %collective-permute-start.37 = (bf16[320,1600]{1,0:T(8,128)(2,1)}, bf16[320,1600]{1,0:T(8,128)(2,1)}, u32[]{:S(2)}, u32[]{:S(2)}) collective-permute-start(bf16[320,1600]{1,0:T(8,128)(2,1)} %get-tuple-element.266), channel_id=1, source_target_pairs={{0,24},{8,16},{16,8},{24,0},{1,25},{9,17},{17,9},{25,1},{2,26},{10... | collective-permute-start | bytes 3072008 | tf_op jit(solution)/shard_map/ppermute | solution.py:600
  561.2 56.9 %collective-permute-start.36 = (bf16[320,1600]{1,0:T(8,128)(2,1)}, bf16[320,1600]{1,0:T(8,128)(2,1)}, u32[]{:S(2)}, u32[]{:S(2)}) collective-permute-start(bf16[320,1600]{1,0:T(8,128)(2,1)} %get-tuple-element.267), channel_id=1, source_target_pairs={{0,16},{8,24},{16,0},{24,8},{1,17},{9,25},{17,1},{25,9},{2,18},{10... | collective-permute-start | bytes 3072008 | tf_op jit(solution)/shard_map/ppermute | solution.py:600
  562.1 56.1 %collective-permute-start.35 = (bf16[320,1600]{1,0:T(8,128)(2,1)}, bf16[320,1600]{1,0:T(8,128)(2,1)}, u32[]{:S(2)}, u32[]{:S(2)}) collective-permute-start(bf16[320,1600]{1,0:T(8,128)(2,1)} %get-tuple-element.268), channel_id=1, source_target_pairs={{0,8},{8,0},{16,24},{24,16},{1,9},{9,1},{17,25},{25,17},{2,10},{10... | collective-permute-start | bytes 3072008 | tf_op jit(solution)/shard_map/ppermute | solution.py:600
  643.4 172.8 %reduce-scatter.11.cloned.1.call-start = ((), (), s32[]{:S(2)}) async-start(), calls=%async_computation.11 | async-start | bytes 4792320 | tf_op jit(solution)/shard_map/reduce_scatter | solution.py:920
  644.1 37.9 %collective-permute-start.38 = (bf16[400,1600]{1,0:T(8,128)(2,1)}, bf16[400,1600]{1,0:T(8,128)(2,1)S(1)}, u32[]{:S(2)}, u32[]{:S(2)}) collective-permute-start(bf16[400,1600]{1,0:T(8,128)(2,1)} %get-tuple-element.217), channel_id=1, source_target_pairs={{0,8},{8,0},{16,24},{24,16},{1,9},{9,1},{17,25},{25,17},{2,10},{10... | collective-permute-start | bytes 3840008 | tf_op jit(solution)/shard_map/ppermute | solution.py:600
  645.7 57.3 %collective-permute-start.39 = (bf16[400,1600]{1,0:T(8,128)(2,1)}, bf16[400,1600]{1,0:T(8,128)(2,1)S(1)}, u32[]{:S(2)}, u32[]{:S(2)}) collective-permute-start(bf16[400,1600]{1,0:T(8,128)(2,1)} %get-tuple-element.218), channel_id=1, source_target_pairs={{0,16},{8,24},{16,0},{24,8},{1,17},{9,25},{17,1},{25,9},{2,18},{10... | collective-permute-start | bytes 3840008 | tf_op jit(solution)/shard_map/ppermute | solution.py:600
  647.1 55.8 %collective-permute-start.40 = (bf16[400,1600]{1,0:T(8,128)(2,1)}, bf16[400,1600]{1,0:T(8,128)(2,1)S(1)}, u32[]{:S(2)}, u32[]{:S(2)}) collective-permute-start(bf16[400,1600]{1,0:T(8,128)(2,1)} %get-tuple-element.219), channel_id=1, source_target_pairs={{0,24},{8,16},{16,8},{24,0},{1,25},{9,17},{17,9},{25,1},{2,26},{10... | collective-permute-start | bytes 3840008 | tf_op jit(solution)/shard_map/ppermute | solution.py:600
  704.7 26.7 %collective-permute-start.41 = (bf16[320,1600]{1,0:T(8,128)(2,1)}, bf16[320,1600]{1,0:T(8,128)(2,1)S(1)}, u32[]{:S(2)}, u32[]{:S(2)}) collective-permute-start(bf16[320,1600]{1,0:T(8,128)(2,1)} %get-tuple-element.263), channel_id=1, source_target_pairs={{0,8},{8,0},{16,24},{24,16},{1,9},{9,1},{17,25},{25,17},{2,10},{10... | collective-permute-start | bytes 3072008 | tf_op jit(solution)/shard_map/ppermute | solution.py:600
  705.9 44.0 %collective-permute-start.43 = (bf16[320,1600]{1,0:T(8,128)(2,1)}, bf16[320,1600]{1,0:T(8,128)(2,1)}, u32[]{:S(2)}, u32[]{:S(2)}) collective-permute-start(bf16[320,1600]{1,0:T(8,128)(2,1)} %get-tuple-element.264), channel_id=1, source_target_pairs={{0,24},{8,16},{16,8},{24,0},{1,25},{9,17},{17,9},{25,1},{2,26},{10... | collective-permute-start | bytes 3072008 | tf_op jit(solution)/shard_map/ppermute | solution.py:600
  707.6 43.6 %collective-permute-start.42 = (bf16[320,1600]{1,0:T(8,128)(2,1)}, bf16[320,1600]{1,0:T(8,128)(2,1)}, u32[]{:S(2)}, u32[]{:S(2)}) collective-permute-start(bf16[320,1600]{1,0:T(8,128)(2,1)} %get-tuple-element.265), channel_id=1, source_target_pairs={{0,16},{8,24},{16,0},{24,8},{1,17},{9,25},{17,1},{25,9},{2,18},{10... | collective-permute-start | bytes 3072008 | tf_op jit(solution)/shard_map/ppermute | solution.py:600
  765.6 28.2 %collective-permute-start.46 = (bf16[50,2816]{1,0:T(8,128)(2,1)}, bf16[50,2816]{1,0:T(8,128)(2,1)}, u32[]{:S(2)}, u32[]{:S(2)}) collective-permute-start(bf16[50,2816]{1,0:T(8,128)(2,1)} %get-tuple-element.299), channel_id=1, source_target_pairs={{0,24},{8,16},{16,8},{24,0},{1,25},{9,17},{17,9},{25,1},{2,26},{10... | collective-permute-start | bytes 844808 | tf_op jit(solution)/shard_map/ppermute | solution.py:600
  767.1 25.7 %collective-permute-start.45 = (bf16[50,2816]{1,0:T(8,128)(2,1)}, bf16[50,2816]{1,0:T(8,128)(2,1)}, u32[]{:S(2)}, u32[]{:S(2)}) collective-permute-start(bf16[50,2816]{1,0:T(8,128)(2,1)} %get-tuple-element.300), channel_id=1, source_target_pairs={{0,16},{8,24},{16,0},{24,8},{1,17},{9,25},{17,1},{25,9},{2,18},{10... | collective-permute-start | bytes 844808 | tf_op jit(solution)/shard_map/ppermute | solution.py:600
  767.6 23.6 %collective-permute-start.44 = (bf16[50,2816]{1,0:T(8,128)(2,1)}, bf16[50,2816]{1,0:T(8,128)(2,1)}, u32[]{:S(2)}, u32[]{:S(2)}) collective-permute-start(bf16[50,2816]{1,0:T(8,128)(2,1)} %get-tuple-element.301), channel_id=1, source_target_pairs={{0,8},{8,0},{16,24},{24,16},{1,9},{9,1},{17,25},{25,17},{2,10},{10... | collective-permute-start | bytes 844808 | tf_op jit(solution)/shard_map/ppermute | solution.py:600
  777.5 30.2 %collective-permute-start.54 = (bf16[50,2816]{1,0:T(8,128)(2,1)}, bf16[50,2816]{1,0:T(8,128)(2,1)S(1)}, u32[]{:S(2)}, u32[]{:S(2)}) collective-permute-start(bf16[50,2816]{1,0:T(8,128)(2,1)} %get-tuple-element.287), channel_id=1, source_target_pairs={{0,24},{8,16},{16,8},{24,0},{1,25},{9,17},{17,9},{25,1},{2,26},{10... | collective-permute-start | bytes 844808 | tf_op jit(solution)/shard_map/ppermute | solution.py:600
  (87 other events, 933.7 us)
Sparse Core Ops, SparseCore 0:
  16.0 50.4 all-gather.14
  68.7 41.4 all-gather.6
  112.4 59.0 all-gather.8
  173.5 50.1 all-gather.10
  225.2 86.0 all-gather.12
  474.9 52.6 reduce-scatter.6
  530.0 94.1 reduce-scatter.4
  643.6 94.0 reduce-scatter.8
  760.1 54.6 reduce-scatter.10

commit v3 on v2

--- a/solution.py
+++ b/solution.py
@@ -858,6 +858,7 @@
     w_m = dot(spread_m, w_m_part, 1, 0).astype(bf16)
 
     proj_ssm = dot(w_ssm, normed, 0, 1)
+    proj_ssm, cot_parts = tie(proj_ssm, cot_parts)
 
     def own_heads(v):
         v = jnp.pad(v, (0, STEP_ROWS))
@@ -875,16 +876,17 @@
     attn_got, gate_up, mixed_t = tie(attn_got, gate_up, mixed_t)
     gate_up = take_blocks(gate_up)
     gate_up_got = send_to_peers(gate_up[1:])
+    mamba_parts = take_blocks(row_blocks(row_major(dot(mixed_t, w_m, 0, 0).astype(bf16))))
+    mamba_got = send_to_peers(mamba_parts[1:])
+
+    gate_up_got, mamba_parts[0] = tie(gate_up_got, mamba_parts[0])
     w_gu = collect(place_blocks(gate_up[0], gate_up_got))
     if aligned:
         w_down = lax.all_gather(down_late, "rep", axis=0, tiled=True)
     else:
         w_down = rep_gather(down_late, D)
 
-    mamba_parts = take_blocks(row_blocks(row_major(dot(mixed_t, w_m, 0, 0).astype(bf16))))
-    mamba_got = send_to_peers(mamba_parts[1:])
-
-    cot_parts, w_o_got, attn_got, mamba_parts[0] = tie(cot_parts, w_o_got, attn_got, mamba_parts[0])
+    w_o_got, attn_got, mamba_parts[0] = tie(w_o_got, attn_got, mamba_parts[0])
     w_o = row_major(place_blocks(w_o_sent, w_o_got)).reshape(D, D)
     attn_tok = row_major(place_blocks(attn_parts[0], attn_got)).reshape(F * width_q, rows)[:D]
     attn_proj = dot(attn_tok, w_o, 0, 0)
@@ -966,8 +968,7 @@
     g_att, g_ssm, grad_in = tie(g_att, g_ssm, grad_in)
     in_part = over_rep(grad_in)
     g_normed = dot(g_att, w_att, 0, 1) + dot(g_ssm, w_ssm, 0, 1)
-    g_normed, grad_o_got = tie(row_major(g_normed.astype(bf16)), grad_o_got)
-    g_normed = take_blocks(row_blocks(g_normed))
+    g_normed = take_blocks(row_blocks(row_major(g_normed.astype(bf16))))
     g_normed_got = send_to_peers(g_normed[1:])
     grad_o = add_up(grad_o[0], grad_o_got).astype(bf16)
     if aligned:

time: 836 us -> 795 us (0.951)
  waiting for transfers between devices: 215 us -> 189 us
  local copies, waits for them, and re-layouts: 130 us -> 119 us
    ppermute x42, waiting for transfers between devices: 134 us -> 96 us  [send_to_peers(): lax.ppermute(parts[k - 1], 'fsdp', peers(devices, k))]
  transfers between devices with their start and end apart: 64 -> 64, of which waited for: 26 -> 23; matrix products, arithmetic and copies ran while one was open for 36% -> 36% of each run, Pallas kernels for 16% -> 17%
where the time goes in v3:
time: 795 us; the launch traced here: 789 us
  matrix products  207 us (26%)
  waiting for transfers between devices  189 us (24%)
  Pallas kernels  148 us (19%)
  local copies, waits for them, and re-layouts  119 us (15%)
  starting transfers between devices  68.4 us (9%)
  other arithmetic  40.6 us (5%)
  between operations  16.2 us (2%)
    dot_general x24, matrix products, dot(): lax.dot_general(a, b, (((ca,), (cb,)), ((), ())), precision=precision, pr...  207 us
    ppermute x42, waiting for transfers between devices, send_to_peers(): lax.ppermute(parts[k - 1], 'fsdp', peers(devices, k))  96 us
    ppermute x42, starting transfers between devices, send_to_peers(): lax.ppermute(parts[k - 1], 'fsdp', peers(devices, k))  52.4 us
    ppermute x4, waiting for transfers between devices, gather_start(): one, two = (lax.ppermute(part, 'fsdp', peers(devices, k)) for k in (1, 2))  43.1 us
    pallas_call x1, Pallas kernels, attn_bwd(): pl.pallas_call(functools.partial(attn_bwd_kernel, blocks=group // QUERY_B...  39.8 us
    pallas_call x1, Pallas kernels, ffn_weight_grads(): pl.pallas_call(functools.partial(weight_grads_kernel, wide_steps=wide_ste...  30.3 us
    pallas_call x1, Pallas kernels, ssm_bwd(): pl.pallas_call(functools.partial(ssm_bwd_kernel, heads=heads), out_shape=...  27 us
    pallas_call x1, Pallas kernels, attn_fwd(): pl.pallas_call(functools.partial(attn_fwd_kernel, blocks=group // QUERY_B...  25.8 us
  transfers between devices with their start and end apart: 64, of which 23 were waited for; matrix products, arithmetic and copies ran while one was open for 36% of the time, Pallas kernels for 17%

profile of v3, /device:TPU:0, one launch (start us, length us, event | category | flops | bytes accessed | tf_op | source)
XLA Modules:
  0.0 789.1 jit_solution(16415169206862431004)
XLA Ops:
  19.5 4.0 collective-permute-start.2
  25.0 6.1 fusion.22
  31.9 5.8 collective-permute-done.1
  47.4 19.8 %collective-permute-done.4 = bf16[320,1600]{1,0:T(8,128)(2,1)S(1)} collective-permute-done((bf16[320,1600]{1,0:T(8,128)(2,1)S(1)}, bf16[320,1600]{1,0:T(8,128)(2,1)S(1)}, u32[]{:S(2)}, u32[]{:S(2)}) %collective-permute-start.4) | collective-permute-done | bytes 1024032 | tf_op jit(solution)/shard_map/ppermute | solution.py:608
  71.2 9.3 %collective-permute-done.5 = bf16[160,1600]{1,0:T(8,128)(2,1)S(1)} collective-permute-done((bf16[160,1600]{1,0:T(8,128)(2,1)S(1)}, bf16[160,1600]{1,0:T(8,128)(2,1)S(1)}, u32[]{:S(2)}, u32[]{:S(2)}) %collective-permute-start.5) | collective-permute-done | bytes 512032 | tf_op jit(solution)/shard_map/ppermute | solution.py:609
  101.3 8.8 %all-gather.7.cloned.1.call-done = bf16[1600,1088]{1,0:T(8,128)(2,1)} async-done(((bf16[200,1088]{1,0:T(8,128)(2,1)}), bf16[1600,1088]{1,0:T(8,128)(2,1)}) %all-gather.7.cloned.1.call-update) | async-done | bytes 3481616 | tf_op jit(solution)/shard_map/all_gather | solution.py:743
  110.2 6.3 copy.89
  116.4 10.2 %fusion.130.kv_ref.q_ref = f32[17,64,1280]{2,1,0:T(8,128)} fusion(bf16[17,64,1600]{2,1,0:T(8,128)(2,1)} %bitcast.267, bf16[1280,1600,1]{1,0,2:T(8,128)(2,1)} %bitcast.18), kind=kOutput, calls=%fused_computation.325 | convolution fusion | flops 4456448000 | bytes 13148160 | tf_op jit(solution)/shard_map/dot_general | solution.py:64
  126.7 25.8 %attn_fwd.1 = (bf16[4,7,64,320]{3,2,1,0:T(8,128)(2,1)}, bf16[7,64,1280]{2,1,0:T(8,128)(2,1)S(1)}, bf16[5,64,1280]{2,1,0:T(8,128)(2,1)S(1)}, bf16[5,1280,64]{2,1,0:T(8,128)(2,1)}, bf16[5,1280,64]{2,1,0:T(8,128)(2,1)}) custom-call(s32[11]{0:T(128)S(1)} %pad_add_fusion.3.kvmap, f32[17,64,1280]{2,1,0:T(8,128)} %fusion.130.kv_ref.q_ref, ...), custom_call_target="tpu_custom_call" | custom-call | flops 1638400 | bytes 81920 | tf_op jit(solution)/shard_map/attn_fwd/pallas_call | solution.py:153
  160.2 3.9 reshape.456
  164.1 4.5 fusion.23
  173.0 4.8 convolution_convert_fusion.9
  184.1 13.9 %fusion.131.p_ref = f32[1728,1280]{1,0:T(8,128)} fusion(bf16[1600,1728]{1,0:T(8,128)(2,1)} %all-gather.9.cloned.1.call-done, bf16[1280,1600]{1,0:T(8,128)(2,1)} %bitcast.17), kind=kOutput, calls=%fused_computation.326 | convolution fusion | flops 7077888000 | bytes 18472960 | tf_op jit(solution)/shard_map/dot_general | solution.py:64
  198.0 8.0 %collective-permute-done.14 = bf16[320,1600]{1,0:T(8,128)(2,1)} collective-permute-done((bf16[320,1600]{1,0:T(8,128)(2,1)}, bf16[320,1600]{1,0:T(8,128)(2,1)}, u32[]{:S(2)}, u32[]{:S(2)}) %collective-permute-start.14) | collective-permute-done | bytes 1024032 | tf_op jit(solution)/shard_map/ppermute | solution.py:600
  206.1 14.1 %ssm_fwd.1 = (f32[832,1280]{1,0:T(8,128)}, bf16[832,1280]{1,0:T(8,128)(2,1)S(1)}, f32[10,832,16]{2,1,0:T(8,128)}) custom-call(f32[1728,1280]{1,0:T(8,128)} %fusion.131.p_ref, f32[16,1]{1,0:T(8,128)S(1)} %copy.94.bias, f32[16,1]{1,0:T(8,128)S(1)} %copy.95.decay, f32[8,1280]{1,0:T(8,128)S(1)} %pad_convert_fusion.marks, ...), custom_call_target="tpu_custom_call" | custom-call | flops 1638400 | bytes 81920 | tf_op jit(solution)/shard_map/ssm_fwd/pallas_call | solution.py:338
  223.9 7.1 convolution_convert_fusion.6
  233.1 4.1 collective-permute-done.20
  247.2 12.4 %convolution_convert_fusion.5.g_ref = bf16[1280,1408]{1,0:T(8,128)(2,1)} fusion(bf16[1408,1600]{1,0:T(8,128)(2,1)} %all-gather.11.cloned.1.call-done, bf16[320,1600]{1,0:T(8,128)(2,1)} %collective-permute-done.15, bf16[320,1600]{1,0:T(8,128)(2,1)} %collective-permute-done.14, bf16[320,1600]{1,0:T(8,128)(2,1)} %collective-permute-done.13, ...), kind=kOutput, calls=%fused_computation.19 | convolution fusion | flops 5785354240 | bytes 12206080 | tf_op jit(solution)/shard_map/dot_general | solution.py:64
  271.8 21.4 %collective-permute-done.17 = bf16[320,1600]{1,0:T(8,128)(2,1)} collective-permute-done((bf16[320,1600]{1,0:T(8,128)(2,1)}, bf16[320,1600]{1,0:T(8,128)(2,1)}, u32[]{:S(2)}, u32[]{:S(2)}) %collective-permute-start.17) | collective-permute-done | bytes 1024032 | tf_op jit(solution)/shard_map/ppermute | solution.py:600
  301.2 23.3 %collective-permute-done.23 = bf16[320,1600]{1,0:T(8,128)(2,1)S(1)} collective-permute-done((bf16[320,1600]{1,0:T(8,128)(2,1)S(1)}, bf16[320,1600]{1,0:T(8,128)(2,1)S(1)}, u32[]{:S(2)}, u32[]{:S(2)}) %collective-permute-start.23) | collective-permute-done | bytes 1024032 | tf_op jit(solution)/shard_map/ppermute | solution.py:608
  329.1 8.8 %collective-permute-done.24 = bf16[160,1600]{1,0:T(8,128)(2,1)S(1)} collective-permute-done((bf16[160,1600]{1,0:T(8,128)(2,1)S(1)}, bf16[160,1600]{1,0:T(8,128)(2,1)S(1)}, u32[]{:S(2)}, u32[]{:S(2)}) %collective-permute-start.24) | collective-permute-done | bytes 512032 | tf_op jit(solution)/shard_map/ppermute | solution.py:609
  339.5 19.4 %convolution_convert_fusion.1.gate_up_ref = bf16[1280,2816]{1,0:T(8,128)(2,1)} fusion(bf16[1280,1600]{1,0:T(8,128)(2,1)} %constant_dynamic-update-slice_fusion.rows_ref, bf16[1600,2816]{1,0:T(8,128)(2,1)} %all-gather.13.cloned.1.call-done), kind=kOutput, calls=%fused_computation.1 | convolution fusion | flops 11537940480 | bytes 20316160 | tf_op jit(solution)/shard_map/dot_general | solution.py:64
  359.0 11.5 %ffn_middle.1 = (bf16[1280,1408]{1,0:T(8,128)(2,1)S(1)}, bf16[1280,2816]{1,0:T(8,128)(2,1)}) custom-call(bf16[1280,2816]{1,0:T(8,128)(2,1)} %convolution_convert_fusion.1.gate_up_ref, bf16[1280,1408]{1,0:T(8,128)(2,1)} %convolution_convert_fusion.5.g_ref), custom_call_target="tpu_custom_call" | custom-call | tf_op jit(solution)/shard_map/ffn_middle/pallas_call | solution.py:506
  370.5 19.4 %convolution_convert_fusion.4 = bf16[1280,1600]{1,0:T(8,128)(2,1)S(1)} fusion(bf16[1280,2816]{1,0:T(8,128)(2,1)} %get-tuple-element.179.g_ref, bf16[1600,2816]{1,0:T(8,128)(2,1)} %all-gather.13.cloned.1.call-done), kind=kOutput, calls=%fused_computation.18 | convolution fusion | flops 11536384000 | bytes 20316160 | tf_op jit(solution)/shard_map/dot_general | solution.py:64
  394.6 7.8 pad_maximum_fusion.cot_ref
  402.4 30.3 %ffn_weight_grads.1 = (bf16[1600,2816]{1,0:T(8,128)(2,1)}, bf16[1408,1600]{1,0:T(8,128)(2,1)}) custom-call(bf16[1280,1600]{1,0:T(8,128)(2,1)} %constant_dynamic-update-slice_fusion.rows_ref, bf16[1280,2816]{1,0:T(8,128)(2,1)} %get-tuple-element.179.g_ref, bf16[1280,1408]{1,0:T(8,128)(2,1)S(1)} %get-tuple-element.188.hidden_ref, ...), custom_call_target="tpu_custom_call" | custom-call | flops 1638400 | bytes 1280 | tf_op jit(solution)/shard_map/ffn_weight_grads/pallas_call | solution.py:550
  432.7 6.3 collective-permute-done.28
  441.4 4.5 multiply_reduce_fusion
  445.9 5.8 multiply_reduce_fusion.1
  460.0 3.3 convolution_convert_fusion.3
  463.4 7.5 convolution_convert_fusion.2
  478.7 39.8 %attn_bwd.1 = bf16[17,64,1280]{2,1,0:T(8,128)(2,1)} custom-call(s32[11]{0:T(128)S(1)} %pad_add_fusion.3.kvmap, bf16[4,7,64,320]{3,2,1,0:T(8,128)(2,1)} %pad_maximum_fusion.1.refs_0_.refs_1_.refs_2_.refs_3_, bf16[4,7,64,320]{3,2,1,0:T(8,128)(2,1)} %pad_maximum_fusion.1.refs_0_.refs_1_.refs_2_.refs_3_, ...), custom_call_target="tpu_custom_call" | custom-call | flops 1638400 | bytes 81920 | tf_op jit(solution)/shard_map/attn_bwd/pallas_call | solution.py:242
  531.1 13.8 %convolution_convert_fusion.7 = bf16[832,1600]{1,0:T(8,128)(2,1)} fusion(s32[832]{0:T(1024)S(1)} %copy-done.54, bf16[832,1280]{1,0:T(8,128)(2,1)S(1)} %copy-done.5, bf16[1280,1600]{1,0:T(8,128)(2,1)} %bitcast.70), kind=kOutput, calls=%fused_computation.39 | convolution fusion | flops 5626343424 | bytes 8891648 | tf_op jit(solution)/shard_map/dot_general | solution.py:64
  544.9 9.3 %fusion.132.up_ref = f32[832,1280]{1,0:T(8,128)} fusion(bf16[832,1600]{1,0:T(8,128)(2,1)} %convolution_convert_fusion.9, bf16[1280,1600]{1,0:T(8,128)(2,1)} %bitcast.70), kind=kOutput, calls=%fused_computation.327 | convolution fusion | flops 3407872000 | bytes 11018240 | tf_op jit(solution)/shard_map/dot_general | solution.py:64
  554.2 27.0 %ssm_bwd.1 = (bf16[1728,1280]{1,0:T(8,128)(2,1)}, f32[48,128]{1,0:T(8,128)S(1)}) custom-call(f32[1728,1280]{1,0:T(8,128)} %fusion.131.p_ref, f32[16,1]{1,0:T(8,128)S(1)} %copy.94.bias, f32[16,1]{1,0:T(8,128)S(1)} %copy.95.decay, f32[8,1280]{1,0:T(8,128)S(1)} %pad_convert_fusion.marks, f32[1280,1]{1,0:T(8,128)S(1)} %reshape_convert_fusion.seg_col, ...), custom_call_target="tpu_custom_call" | custom-call | flops 1638400 | bytes 81920 | tf_op jit(solution)/shard_map/ssm_bwd/pallas_call | solution.py:466
  581.2 7.3 reduce-scatter.5.cloned.1.call-done
  588.5 19.3 %convolution_convert_fusion = bf16[1600,2816]{1,0:T(8,128)(2,1)} fusion(bf16[1280,1600]{1,0:T(8,128)(2,1)} %bitcast.17, bf16[1728,1280]{1,0:T(8,128)(2,1)} %get-tuple-element.222, bf16[1088,1280]{1,0:T(8,128)(2,1)} %bitcast.268), kind=kOutput, calls=%fused_computation | convolution fusion | flops 11553259520 | bytes 20316160 | tf_op jit(solution)/shard_map/dot_general | solution.py:64
  612.0 10.9 %fusion.133 = f32[1280,1600]{1,0:T(8,128)} fusion(bf16[1088,1280]{1,0:T(8,128)(2,1)S(1)} %bitcast.269, bf16[1600,1088]{1,0:T(8,128)(2,1)} %all-gather.7.cloned.1.call-done), kind=kOutput, calls=%fused_computation.328 | convolution fusion | flops 4456448000 | bytes 14458880 | tf_op jit(solution)/shard_map/dot_general | solution.py:64
  622.8 13.3 %fusion.9 = bf16[1280,1600]{1,0:T(8,128)(2,1)S(1)} fusion(f32[1280,1600]{1,0:T(8,128)} %fusion.133, bf16[1728,1280]{1,0:T(8,128)(2,1)S(1)} %bitcast.291, bf16[1600,1728]{1,0:T(8,128)(2,1)} %all-gather.9.cloned.1.call-done), kind=kOutput, calls=%fused_computation.15 | convolution fusion | flops 7081984000 | bytes 22241280 | tf_op jit(solution)/shard_map/dot_general | solution.py:64
  645.5 6.5 fusion.26
  652.3 13.8 %collective-permute-done.40 = bf16[400,1600]{1,0:T(8,128)(2,1)S(1)} collective-permute-done((bf16[400,1600]{1,0:T(8,128)(2,1)}, bf16[400,1600]{1,0:T(8,128)(2,1)S(1)}, u32[]{:S(2)}, u32[]{:S(2)}) %collective-permute-start.40) | collective-permute-done | bytes 1280032 | tf_op jit(solution)/shard_map/ppermute | solution.py:600
  666.0 4.4 collective-permute-done.41
  672.5 4.2 fusion.19
  676.7 15.6 %collective-permute-done.38 = bf16[320,1600]{1,0:T(8,128)(2,1)S(1)} collective-permute-done((bf16[320,1600]{1,0:T(8,128)(2,1)}, bf16[320,1600]{1,0:T(8,128)(2,1)S(1)}, u32[]{:S(2)}, u32[]{:S(2)}) %collective-permute-start.38) | collective-permute-done | bytes 1024032 | tf_op jit(solution)/shard_map/ppermute | solution.py:600
  692.2 9.9 %reduce-scatter.9.cloned.1.call-done = bf16[200,2816]{1,0:T(8,128)(2,1)} async-done(((bf16[1600,2816]{1,0:T(8,128)(2,1)}), bf16[200,2816]{1,0:T(8,128)(2,1)}) %reduce-scatter.9.cloned.1.call-update) | async-done | bytes 1126416 | tf_op jit(solution)/shard_map/reduce_scatter | solution.py:922
  702.1 10.8 %collective-permute-done.43 = bf16[320,1600]{1,0:T(8,128)(2,1)} collective-permute-done((bf16[320,1600]{1,0:T(8,128)(2,1)}, bf16[320,1600]{1,0:T(8,128)(2,1)}, u32[]{:S(2)}, u32[]{:S(2)}) %collective-permute-start.43) | collective-permute-done | bytes 1024032 | tf_op jit(solution)/shard_map/ppermute | solution.py:600
  713.1 4.2 fusion.43
  739.9 8.3 %fusion.2 = f32[320,1600]{1,0:T(8,128)} fusion(s32[1600]{0:T(1024)S(1)} %copy-done.50, f32[320,1600]{1,0:T(8,128)S(1)} %copy-done.18, f32[320,1600]{1,0:T(8,128)} %get-tuple-element.253, f32[320]{0:T(512)S(1)} %broadcast_multiply_fusion.2, f32[1600]{0:T(1024)S(1)} %copy-done.39, f32[320]{0:T(512)S(1)} %copy-done.47, bf16[640,1600]{1,0:T(8,128)(2,1)S(1)} %copy-done.15), kind=kOutput, calls=%fused_computation.5 | convolution fusion | flops 4922368000 | bytes 7311360 | tf_op jit(solution)/shard_map/dot_general | solution.py:64
  (482 shorter events, 216.5 us)
Async XLA Ops:
  7.2 82.7 %all-gather.15.cloned.1.call-start = ((), (), s32[]{:S(2)}) async-start(), calls=%async_computation.12 | async-start | bytes 4792320 | tf_op jit(solution)/shard_map/all_gather | solution.py:787
  15.8 94.4 %all-gather.7.cloned.1.call-start = ((), (), s32[]{:S(2)}) async-start(), calls=%async_computation.4 | async-start | bytes 4147200 | tf_op jit(solution)/shard_map/all_gather | solution.py:743
  40.3 143.8 %all-gather.9.cloned.1.call-start = ((), (), s32[]{:S(2)}) async-start(), calls=%async_computation.5 | async-start | bytes 6451200 | tf_op jit(solution)/shard_map/all_gather | solution.py:743
  41.9 205.3 %all-gather.11.cloned.1.call-start = ((), (), s32[]{:S(2)}) async-start(), calls=%async_computation.6 | async-start | bytes 5271552 | tf_op jit(solution)/shard_map/all_gather | solution.py:885
  42.0 25.2 %collective-permute-start.4 = (bf16[320,1600]{1,0:T(8,128)(2,1)S(1)}, bf16[320,1600]{1,0:T(8,128)(2,1)S(1)}, u32[]{:S(2)}, u32[]{:S(2)}) collective-permute-start(bf16[320,1600]{1,0:T(8,128)(2,1)S(1)} %fusion.34), channel_id=1, source_target_pairs={{0,16},{8,24},{16,0},{24,8},{1,17},{9,25},{17,1},{25,9},{2,18},{10... | collective-permute-start | bytes 3072008 | tf_op jit(solution)/shard_map/ppermute | solution.py:608
  43.4 25.6 %collective-permute-start.3 = (bf16[320,1600]{1,0:T(8,128)(2,1)S(1)}, bf16[320,1600]{1,0:T(8,128)(2,1)}, u32[]{:S(2)}, u32[]{:S(2)}) collective-permute-start(bf16[320,1600]{1,0:T(8,128)(2,1)S(1)} %fusion.34), channel_id=1, source_target_pairs={{0,8},{8,0},{16,24},{24,16},{1,9},{9,1},{17,25},{25,17},{2,10},{10... | collective-permute-start | bytes 3072008 | tf_op jit(solution)/shard_map/ppermute | solution.py:608
  46.0 293.6 %all-gather.13.cloned.1.call-start = ((), (), s32[]{:S(2)}) async-start(), calls=%async_computation.7 | async-start | bytes 10137600 | tf_op jit(solution)/shard_map/all_gather | solution.py:743
  93.1 59.4 %collective-permute-start.9 = (bf16[400,1600]{1,0:T(8,128)(2,1)}, bf16[400,1600]{1,0:T(8,128)(2,1)}, u32[]{:S(2)}, u32[]{:S(2)}) collective-permute-start(bf16[400,1600]{1,0:T(8,128)(2,1)} %reshape.454), channel_id=1, source_target_pairs={{0,24},{8,16},{16,8},{24,0},{1,25},{9,17},{17,9},{25,1},{2,26},{10... | collective-permute-start | bytes 3840008 | tf_op jit(solution)/shard_map/ppermute | solution.py:600
  94.8 57.7 %collective-permute-start.8 = (bf16[400,1600]{1,0:T(8,128)(2,1)}, bf16[400,1600]{1,0:T(8,128)(2,1)}, u32[]{:S(2)}, u32[]{:S(2)}) collective-permute-start(bf16[400,1600]{1,0:T(8,128)(2,1)} %reshape.454), channel_id=1, source_target_pairs={{0,16},{8,24},{16,0},{24,8},{1,17},{9,25},{17,1},{25,9},{2,18},{10... | collective-permute-start | bytes 3840008 | tf_op jit(solution)/shard_map/ppermute | solution.py:600
  95.0 57.5 %collective-permute-start.7 = (bf16[400,1600]{1,0:T(8,128)(2,1)}, bf16[400,1600]{1,0:T(8,128)(2,1)}, u32[]{:S(2)}, u32[]{:S(2)}) collective-permute-start(bf16[400,1600]{1,0:T(8,128)(2,1)} %reshape.454), channel_id=1, source_target_pairs={{0,8},{8,0},{16,24},{24,16},{1,9},{9,1},{17,25},{25,17},{2,10},{10... | collective-permute-start | bytes 3840008 | tf_op jit(solution)/shard_map/ppermute | solution.py:600
  155.2 27.0 %collective-permute-start.15 = (bf16[320,1600]{1,0:T(8,128)(2,1)}, bf16[320,1600]{1,0:T(8,128)(2,1)}, u32[]{:S(2)}, u32[]{:S(2)}) collective-permute-start(bf16[320,1600]{1,0:T(8,128)(2,1)} %slice.404), channel_id=1, source_target_pairs={{0,24},{8,16},{16,8},{24,0},{1,25},{9,17},{17,9},{25,1},{2,26},{10... | collective-permute-start | bytes 3072008 | tf_op jit(solution)/shard_map/ppermute | solution.py:600
  177.8 28.3 %collective-permute-start.14 = (bf16[320,1600]{1,0:T(8,128)(2,1)}, bf16[320,1600]{1,0:T(8,128)(2,1)}, u32[]{:S(2)}, u32[]{:S(2)}) collective-permute-start(bf16[320,1600]{1,0:T(8,128)(2,1)} %slice.404), channel_id=1, source_target_pairs={{0,16},{8,24},{16,0},{24,8},{1,17},{9,25},{17,1},{25,9},{2,18},{10... | collective-permute-start | bytes 3072008 | tf_op jit(solution)/shard_map/ppermute | solution.py:600
  178.4 27.7 %collective-permute-start.13 = (bf16[320,1600]{1,0:T(8,128)(2,1)}, bf16[320,1600]{1,0:T(8,128)(2,1)}, u32[]{:S(2)}, u32[]{:S(2)}) collective-permute-start(bf16[320,1600]{1,0:T(8,128)(2,1)} %slice.404), channel_id=1, source_target_pairs={{0,8},{8,0},{16,24},{24,16},{1,9},{9,1},{17,25},{25,17},{2,10},{10... | collective-permute-start | bytes 3072008 | tf_op jit(solution)/shard_map/ppermute | solution.py:600
  179.0 41.2 %collective-permute-start.12 = (bf16[448,320]{1,0:T(8,128)(2,1)}, bf16[448,320]{1,0:T(8,128)(2,1)}, u32[]{:S(2)}, u32[]{:S(2)}) collective-permute-start(bf16[448,320]{1,0:T(8,128)(2,1)} %get-tuple-element.286), channel_id=1, source_target_pairs={{0,24},{8,16},{16,8},{24,0},{1,25},{9,17},{17,9},{25,1},{2,26},{10... | collective-permute-start | bytes 860168 | tf_op jit(solution)/shard_map/ppermute | solution.py:600
  181.3 38.9 %collective-permute-start.11 = (bf16[448,320]{1,0:T(8,128)(2,1)S(1)}, bf16[448,320]{1,0:T(8,128)(2,1)}, u32[]{:S(2)}, u32[]{:S(2)}) collective-permute-start(bf16[448,320]{1,0:T(8,128)(2,1)S(1)} %copy-done.34), channel_id=1, source_target_pairs={{0,16},{8,24},{16,0},{24,8},{1,17},{9,25},{17,1},{25,9},{2,18},{10... | collective-permute-start | bytes 860168 | tf_op jit(solution)/shard_map/ppermute | solution.py:600
  182.2 38.0 %collective-permute-start.10 = (bf16[448,320]{1,0:T(8,128)(2,1)S(1)}, bf16[448,320]{1,0:T(8,128)(2,1)}, u32[]{:S(2)}, u32[]{:S(2)}) collective-permute-start(bf16[448,320]{1,0:T(8,128)(2,1)S(1)} %copy-done.33), channel_id=1, source_target_pairs={{0,8},{8,0},{16,24},{24,16},{1,9},{9,1},{17,25},{25,17},{2,10},{10... | collective-permute-start | bytes 860168 | tf_op jit(solution)/shard_map/ppermute | solution.py:600
  222.3 14.9 %collective-permute-start.20 = (bf16[50,2816]{1,0:T(8,128)(2,1)S(1)}, bf16[50,2816]{1,0:T(8,128)(2,1)S(1)}, u32[]{:S(2)}, u32[]{:S(2)}) collective-permute-start(bf16[50,2816]{1,0:T(8,128)(2,1)S(1)} %get-tuple-element.307), channel_id=1, source_target_pairs={{0,16},{8,24},{16,0},{24,8},{1,17},{9,25},{17,1},{25,9},{2,18},{10... | collective-permute-start | bytes 844808 | tf_op jit(solution)/shard_map/ppermute | solution.py:600
  243.3 337.9 %reduce-scatter.7.cloned.1.call-start = ((), (), s32[]{:S(2)}) async-start(), calls=%async_computation.9 | async-start | bytes 5271552 | tf_op jit(solution)/shard_map/reduce_scatter | solution.py:922
  243.7 28.1 %collective-permute-start.18 = (bf16[320,1600]{1,0:T(8,128)(2,1)}, bf16[320,1600]{1,0:T(8,128)(2,1)}, u32[]{:S(2)}, u32[]{:S(2)}) collective-permute-start(bf16[320,1600]{1,0:T(8,128)(2,1)} %get-tuple-element.276), channel_id=1, source_target_pairs={{0,24},{8,16},{16,8},{24,0},{1,25},{9,17},{17,9},{25,1},{2,26},{10... | collective-permute-start | bytes 3072008 | tf_op jit(solution)/shard_map/ppermute | solution.py:600
  245.5 47.7 %collective-permute-start.17 = (bf16[320,1600]{1,0:T(8,128)(2,1)}, bf16[320,1600]{1,0:T(8,128)(2,1)}, u32[]{:S(2)}, u32[]{:S(2)}) collective-permute-start(bf16[320,1600]{1,0:T(8,128)(2,1)} %get-tuple-element.277), channel_id=1, source_target_pairs={{0,16},{8,24},{16,0},{24,8},{1,17},{9,25},{17,1},{25,9},{2,18},{10... | collective-permute-start | bytes 3072008 | tf_op jit(solution)/shard_map/ppermute | solution.py:600
  246.2 47.0 %collective-permute-start.16 = (bf16[320,1600]{1,0:T(8,128)(2,1)}, bf16[320,1600]{1,0:T(8,128)(2,1)}, u32[]{:S(2)}, u32[]{:S(2)}) collective-permute-start(bf16[320,1600]{1,0:T(8,128)(2,1)} %get-tuple-element.278), channel_id=1, source_target_pairs={{0,8},{8,0},{16,24},{24,16},{1,9},{9,1},{17,25},{25,17},{2,10},{10... | collective-permute-start | bytes 3072008 | tf_op jit(solution)/shard_map/ppermute | solution.py:600
  299.0 25.4 %collective-permute-start.23 = (bf16[320,1600]{1,0:T(8,128)(2,1)S(1)}, bf16[320,1600]{1,0:T(8,128)(2,1)S(1)}, u32[]{:S(2)}, u32[]{:S(2)}) collective-permute-start(bf16[320,1600]{1,0:T(8,128)(2,1)S(1)} %get-tuple-element.256), channel_id=1, source_target_pairs={{0,16},{8,24},{16,0},{24,8},{1,17},{9,25},{17,1},{25,9},{2,18},{10... | collective-permute-start | bytes 3072008 | tf_op jit(solution)/shard_map/ppermute | solution.py:608
  300.0 25.5 %collective-permute-start.22 = (bf16[320,1600]{1,0:T(8,128)(2,1)S(1)}, bf16[320,1600]{1,0:T(8,128)(2,1)S(1)}, u32[]{:S(2)}, u32[]{:S(2)}) collective-permute-start(bf16[320,1600]{1,0:T(8,128)(2,1)S(1)} %get-tuple-element.256), channel_id=1, source_target_pairs={{0,8},{8,0},{16,24},{24,16},{1,9},{9,1},{17,25},{25,17},{2,10},{10... | collective-permute-start | bytes 3072008 | tf_op jit(solution)/shard_map/ppermute | solution.py:608
  391.1 41.5 %collective-permute-start.27 = (bf16[320,1600]{1,0:T(8,128)(2,1)S(1)}, bf16[320,1600]{1,0:T(8,128)(2,1)}, u32[]{:S(2)}, u32[]{:S(2)}) collective-permute-start(bf16[320,1600]{1,0:T(8,128)(2,1)S(1)} %get-tuple-element.272), channel_id=1, source_target_pairs={{0,16},{8,24},{16,0},{24,8},{1,17},{9,25},{17,1},{25,9},{2,18},{10... | collective-permute-start | bytes 3072008 | tf_op jit(solution)/shard_map/ppermute | solution.py:600
  392.3 40.3 %collective-permute-start.26 = (bf16[320,1600]{1,0:T(8,128)(2,1)S(1)}, bf16[320,1600]{1,0:T(8,128)(2,1)}, u32[]{:S(2)}, u32[]{:S(2)}) collective-permute-start(bf16[320,1600]{1,0:T(8,128)(2,1)S(1)} %get-tuple-element.273), channel_id=1, source_target_pairs={{0,8},{8,0},{16,24},{24,16},{1,9},{9,1},{17,25},{25,17},{2,10},{10... | collective-permute-start | bytes 3072008 | tf_op jit(solution)/shard_map/ppermute | solution.py:600
  393.3 45.7 %collective-permute-start.28 = (bf16[320,1600]{1,0:T(8,128)(2,1)S(1)}, bf16[320,1600]{1,0:T(8,128)(2,1)}, u32[]{:S(2)}, u32[]{:S(2)}) collective-permute-start(bf16[320,1600]{1,0:T(8,128)(2,1)S(1)} %get-tuple-element.274), channel_id=1, source_target_pairs={{0,24},{8,16},{16,8},{24,0},{1,25},{9,17},{17,9},{25,1},{2,26},{10... | collective-permute-start | bytes 3072008 | tf_op jit(solution)/shard_map/ppermute | solution.py:600
  439.0 149.5 %reduce-scatter.5.cloned.1.call-start = ((), (), s32[]{:S(2)}) async-start(), calls=%async_computation.8 | async-start | bytes 10137600 | tf_op jit(solution)/shard_map/reduce_scatter | solution.py:922
  439.8 262.3 %reduce-scatter.9.cloned.1.call-start = ((), (), s32[]{:S(2)}) async-start(), calls=%async_computation.10 | async-start | bytes 10137600 | tf_op jit(solution)/shard_map/reduce_scatter | solution.py:922
  456.4 17.2 %collective-permute-start.31 = (bf16[7,64,320]{2,1,0:T(8,128)(2,1)S(1)}, bf16[7,64,320]{2,1,0:T(8,128)(2,1)S(1)}, u32[]{:S(2)}, u32[]{:S(2)}) collective-permute-start(bf16[7,64,320]{2,1,0:T(8,128)(2,1)S(1)} %get-tuple-element.282), channel_id=1, source_target_pairs={{0,24},{8,16},{16,8},{24,0},{1,25},{9,17},{17,9},{25,1},{2,26},{10... | collective-permute-start | bytes 860168 | tf_op jit(solution)/shard_map/ppermute | solution.py:600
  458.0 15.7 %collective-permute-start.30 = (bf16[7,64,320]{2,1,0:T(8,128)(2,1)S(1)}, bf16[7,64,320]{2,1,0:T(8,128)(2,1)S(1)}, u32[]{:S(2)}, u32[]{:S(2)}) collective-permute-start(bf16[7,64,320]{2,1,0:T(8,128)(2,1)S(1)} %get-tuple-element.283), channel_id=1, source_target_pairs={{0,16},{8,24},{16,0},{24,8},{1,17},{9,25},{17,1},{25,9},{2,18},{10... | collective-permute-start | bytes 860168 | tf_op jit(solution)/shard_map/ppermute | solution.py:600
  458.9 14.8 %collective-permute-start.29 = (bf16[7,64,320]{2,1,0:T(8,128)(2,1)S(1)}, bf16[7,64,320]{2,1,0:T(8,128)(2,1)S(1)}, u32[]{:S(2)}, u32[]{:S(2)}) collective-permute-start(bf16[7,64,320]{2,1,0:T(8,128)(2,1)S(1)} %get-tuple-element.284), channel_id=1, source_target_pairs={{0,8},{8,0},{16,24},{24,16},{1,9},{9,1},{17,25},{25,17},{2,10},{10... | collective-permute-start | bytes 860168 | tf_op jit(solution)/shard_map/ppermute | solution.py:600
  473.7 44.8 %collective-permute-start.34 = (bf16[320,1600]{1,0:T(8,128)(2,1)S(1)}, bf16[320,1600]{1,0:T(8,128)(2,1)S(1)}, u32[]{:S(2)}, u32[]{:S(2)}) collective-permute-start(bf16[320,1600]{1,0:T(8,128)(2,1)S(1)} %get-tuple-element.192), channel_id=1, source_target_pairs={{0,24},{8,16},{16,8},{24,0},{1,25},{9,17},{17,9},{25,1},{2,26},{10... | collective-permute-start | bytes 3072008 | tf_op jit(solution)/shard_map/ppermute | solution.py:600
  475.2 45.1 %collective-permute-start.33 = (bf16[320,1600]{1,0:T(8,128)(2,1)S(1)}, bf16[320,1600]{1,0:T(8,128)(2,1)S(1)}, u32[]{:S(2)}, u32[]{:S(2)}) collective-permute-start(bf16[320,1600]{1,0:T(8,128)(2,1)S(1)} %get-tuple-element.192), channel_id=1, source_target_pairs={{0,16},{8,24},{16,0},{24,8},{1,17},{9,25},{17,1},{25,9},{2,18},{10... | collective-permute-start | bytes 3072008 | tf_op jit(solution)/shard_map/ppermute | solution.py:600
  476.1 44.2 %collective-permute-start.32 = (bf16[320,1600]{1,0:T(8,128)(2,1)S(1)}, bf16[320,1600]{1,0:T(8,128)(2,1)S(1)}, u32[]{:S(2)}, u32[]{:S(2)}) collective-permute-start(bf16[320,1600]{1,0:T(8,128)(2,1)S(1)} %get-tuple-element.192), channel_id=1, source_target_pairs={{0,8},{8,0},{16,24},{24,16},{1,9},{9,1},{17,25},{25,17},{2,10},{10... | collective-permute-start | bytes 3072008 | tf_op jit(solution)/shard_map/ppermute | solution.py:600
  522.1 59.0 %collective-permute-start.37 = (bf16[320,1600]{1,0:T(8,128)(2,1)}, bf16[320,1600]{1,0:T(8,128)(2,1)}, u32[]{:S(2)}, u32[]{:S(2)}) collective-permute-start(bf16[320,1600]{1,0:T(8,128)(2,1)} %get-tuple-element.268), channel_id=1, source_target_pairs={{0,24},{8,16},{16,8},{24,0},{1,25},{9,17},{17,9},{25,1},{2,26},{10... | collective-permute-start | bytes 3072008 | tf_op jit(solution)/shard_map/ppermute | solution.py:600
  523.9 57.3 %collective-permute-start.36 = (bf16[320,1600]{1,0:T(8,128)(2,1)}, bf16[320,1600]{1,0:T(8,128)(2,1)}, u32[]{:S(2)}, u32[]{:S(2)}) collective-permute-start(bf16[320,1600]{1,0:T(8,128)(2,1)} %get-tuple-element.269), channel_id=1, source_target_pairs={{0,16},{8,24},{16,0},{24,8},{1,17},{9,25},{17,1},{25,9},{2,18},{10... | collective-permute-start | bytes 3072008 | tf_op jit(solution)/shard_map/ppermute | solution.py:600
  524.8 56.3 %collective-permute-start.35 = (bf16[320,1600]{1,0:T(8,128)(2,1)}, bf16[320,1600]{1,0:T(8,128)(2,1)}, u32[]{:S(2)}, u32[]{:S(2)}) collective-permute-start(bf16[320,1600]{1,0:T(8,128)(2,1)} %get-tuple-element.270), channel_id=1, source_target_pairs={{0,8},{8,0},{16,24},{24,16},{1,9},{9,1},{17,25},{25,17},{2,10},{10... | collective-permute-start | bytes 3072008 | tf_op jit(solution)/shard_map/ppermute | solution.py:600
  607.8 167.2 %reduce-scatter.11.cloned.1.call-start = ((), (), s32[]{:S(2)}) async-start(), calls=%async_computation.11 | async-start | bytes 4792320 | tf_op jit(solution)/shard_map/reduce_scatter | solution.py:922
  608.5 43.5 %collective-permute-start.39 = (bf16[400,1600]{1,0:T(8,128)(2,1)}, bf16[400,1600]{1,0:T(8,128)(2,1)S(1)}, u32[]{:S(2)}, u32[]{:S(2)}) collective-permute-start(bf16[400,1600]{1,0:T(8,128)(2,1)} %get-tuple-element.226), channel_id=1, source_target_pairs={{0,8},{8,0},{16,24},{24,16},{1,9},{9,1},{17,25},{25,17},{2,10},{10... | collective-permute-start | bytes 3840008 | tf_op jit(solution)/shard_map/ppermute | solution.py:600
  610.0 56.0 %collective-permute-start.40 = (bf16[400,1600]{1,0:T(8,128)(2,1)}, bf16[400,1600]{1,0:T(8,128)(2,1)S(1)}, u32[]{:S(2)}, u32[]{:S(2)}) collective-permute-start(bf16[400,1600]{1,0:T(8,128)(2,1)} %get-tuple-element.227), channel_id=1, source_target_pairs={{0,16},{8,24},{16,0},{24,8},{1,17},{9,25},{17,1},{25,9},{2,18},{10... | collective-permute-start | bytes 3840008 | tf_op jit(solution)/shard_map/ppermute | solution.py:600
  611.5 58.9 %collective-permute-start.41 = (bf16[400,1600]{1,0:T(8,128)(2,1)}, bf16[400,1600]{1,0:T(8,128)(2,1)S(1)}, u32[]{:S(2)}, u32[]{:S(2)}) collective-permute-start(bf16[400,1600]{1,0:T(8,128)(2,1)} %get-tuple-element.228), channel_id=1, source_target_pairs={{0,24},{8,16},{16,8},{24,0},{1,25},{9,17},{17,9},{25,1},{2,26},{10... | collective-permute-start | bytes 3840008 | tf_op jit(solution)/shard_map/ppermute | solution.py:600
  639.2 53.1 %collective-permute-start.38 = (bf16[320,1600]{1,0:T(8,128)(2,1)}, bf16[320,1600]{1,0:T(8,128)(2,1)S(1)}, u32[]{:S(2)}, u32[]{:S(2)}) collective-permute-start(bf16[320,1600]{1,0:T(8,128)(2,1)} %get-tuple-element.265), channel_id=1, source_target_pairs={{0,8},{8,0},{16,24},{24,16},{1,9},{9,1},{17,25},{25,17},{2,10},{10... | collective-permute-start | bytes 3072008 | tf_op jit(solution)/shard_map/ppermute | solution.py:600
  640.9 72.0 %collective-permute-start.43 = (bf16[320,1600]{1,0:T(8,128)(2,1)}, bf16[320,1600]{1,0:T(8,128)(2,1)}, u32[]{:S(2)}, u32[]{:S(2)}) collective-permute-start(bf16[320,1600]{1,0:T(8,128)(2,1)} %get-tuple-element.266), channel_id=1, source_target_pairs={{0,24},{8,16},{16,8},{24,0},{1,25},{9,17},{17,9},{25,1},{2,26},{10... | collective-permute-start | bytes 3072008 | tf_op jit(solution)/shard_map/ppermute | solution.py:600
  652.0 61.1 %collective-permute-start.42 = (bf16[320,1600]{1,0:T(8,128)(2,1)}, bf16[320,1600]{1,0:T(8,128)(2,1)}, u32[]{:S(2)}, u32[]{:S(2)}) collective-permute-start(bf16[320,1600]{1,0:T(8,128)(2,1)} %get-tuple-element.267), channel_id=1, source_target_pairs={{0,16},{8,24},{16,0},{24,8},{1,17},{9,25},{17,1},{25,9},{2,18},{10... | collective-permute-start | bytes 3072008 | tf_op jit(solution)/shard_map/ppermute | solution.py:600
  727.0 25.7 %collective-permute-start.46 = (bf16[50,2816]{1,0:T(8,128)(2,1)}, bf16[50,2816]{1,0:T(8,128)(2,1)}, u32[]{:S(2)}, u32[]{:S(2)}) collective-permute-start(bf16[50,2816]{1,0:T(8,128)(2,1)} %get-tuple-element.301), channel_id=1, source_target_pairs={{0,24},{8,16},{16,8},{24,0},{1,25},{9,17},{17,9},{25,1},{2,26},{10... | collective-permute-start | bytes 844808 | tf_op jit(solution)/shard_map/ppermute | solution.py:600
  728.8 22.9 %collective-permute-start.45 = (bf16[50,2816]{1,0:T(8,128)(2,1)}, bf16[50,2816]{1,0:T(8,128)(2,1)}, u32[]{:S(2)}, u32[]{:S(2)}) collective-permute-start(bf16[50,2816]{1,0:T(8,128)(2,1)} %get-tuple-element.302), channel_id=1, source_target_pairs={{0,16},{8,24},{16,0},{24,8},{1,17},{9,25},{17,1},{25,9},{2,18},{10... | collective-permute-start | bytes 844808 | tf_op jit(solution)/shard_map/ppermute | solution.py:600
  729.4 19.7 %collective-permute-start.44 = (bf16[50,2816]{1,0:T(8,128)(2,1)}, bf16[50,2816]{1,0:T(8,128)(2,1)}, u32[]{:S(2)}, u32[]{:S(2)}) collective-permute-start(bf16[50,2816]{1,0:T(8,128)(2,1)} %get-tuple-element.303), channel_id=1, source_target_pairs={{0,8},{8,0},{16,24},{24,16},{1,9},{9,1},{17,25},{25,17},{2,10},{10... | collective-permute-start | bytes 844808 | tf_op jit(solution)/shard_map/ppermute | solution.py:600
  735.2 31.3 %collective-permute-start.54 = (bf16[50,2816]{1,0:T(8,128)(2,1)}, bf16[50,2816]{1,0:T(8,128)(2,1)S(1)}, u32[]{:S(2)}, u32[]{:S(2)}) collective-permute-start(bf16[50,2816]{1,0:T(8,128)(2,1)} %get-tuple-element.289), channel_id=1, source_target_pairs={{0,24},{8,16},{16,8},{24,0},{1,25},{9,17},{17,9},{25,1},{2,26},{10... | collective-permute-start | bytes 844808 | tf_op jit(solution)/shard_map/ppermute | solution.py:600
  (85 other events, 1009.8 us)
Sparse Core Ops, SparseCore 0:
  15.9 50.4 all-gather.14
  68.7 41.4 all-gather.6
  112.4 59.0 all-gather.8
  173.5 50.1 all-gather.10
  243.4 87.0 all-gather.12
  439.2 52.8 reduce-scatter.6
  494.3 94.1 reduce-scatter.4
  607.9 94.0 reduce-scatter.8
  721.5 51.6 reduce-scatter.10

commit v4 on v3

--- a/solution.py
+++ b/solution.py
@@ -974,7 +974,7 @@
     if aligned:
         grad_o = jnp.pad(grad_o.reshape(R, rows_o, D), ((0, 0), (0, pad_o - rows_o), (0, 0)))
         joined = jnp.concatenate([grad_o, grad_m.reshape(R, pad_m, D)], axis=1)
-        g_normed_got[0], gu_part, in_part, joined = tie(g_normed_got[0], gu_part, in_part, joined)
+        g_normed_got[0], gu_part, in_part = tie(g_normed_got[0], gu_part, in_part)
         joined = over_rep(joined.reshape(R * (pad_o + pad_m), D))
     g_normed = add_up(g_normed[0], g_normed_got)
     gu_back = to_owners(gu_part).reshape(F, depth, 2, width_f)

time: 795 us -> 834 us (1.049)
  waiting for transfers between devices: 189 us -> 222 us
    ppermute x42, waiting for transfers between devices: 96 us -> 140 us  [send_to_peers(): lax.ppermute(parts[k - 1], 'fsdp', peers(devices, k))]
    reduce_scatter x4, waiting for transfers between devices: 17.2 us -> 7.26 us  [over_rep(): return lax.psum_scatter(grad, 'rep', scatter_dimension=0, tiled=True)]
  transfers between devices with their start and end apart: 64 -> 64, of which waited for: 23 -> 22; matrix products, arithmetic and copies ran while one was open for 36% -> 35% of each run, Pallas kernels for 17% -> 17%
where the time goes in v4:
time: 834 us; the launch traced here: 828 us
  waiting for transfers between devices  222 us (27%)
  matrix products  207 us (25%)
  Pallas kernels  148 us (18%)
  local copies, waits for them, and re-layouts  123 us (15%)
  starting transfers between devices  71.6 us (9%)
  other arithmetic  41.1 us (5%)
  between operations  16.2 us (2%)
    dot_general x24, matrix products, dot(): lax.dot_general(a, b, (((ca,), (cb,)), ((), ())), precision=precision, pr...  207 us
    ppermute x42, waiting for transfers between devices, send_to_peers(): lax.ppermute(parts[k - 1], 'fsdp', peers(devices, k))  140 us
    ppermute x42, starting transfers between devices, send_to_peers(): lax.ppermute(parts[k - 1], 'fsdp', peers(devices, k))  51.6 us
    ppermute x4, waiting for transfers between devices, gather_start(): one, two = (lax.ppermute(part, 'fsdp', peers(devices, k)) for k in (1, 2))  43 us
    pallas_call x1, Pallas kernels, attn_bwd(): pl.pallas_call(functools.partial(attn_bwd_kernel, blocks=group // QUERY_B...  39.7 us
    pallas_call x1, Pallas kernels, ffn_weight_grads(): pl.pallas_call(functools.partial(weight_grads_kernel, wide_steps=wide_ste...  30.3 us
    pallas_call x1, Pallas kernels, ssm_bwd(): pl.pallas_call(functools.partial(ssm_bwd_kernel, heads=heads), out_shape=...  26.9 us
    pallas_call x1, Pallas kernels, attn_fwd(): pl.pallas_call(functools.partial(attn_fwd_kernel, blocks=group // QUERY_B...  25.8 us
  transfers between devices with their start and end apart: 64, of which 22 were waited for; matrix products, arithmetic and copies ran while one was open for 35% of the time, Pallas kernels for 17%

profile of v4, /device:TPU:0, one launch (start us, length us, event | category | flops | bytes accessed | tf_op | source)
XLA Modules:
  0.0 827.8 jit_solution(5543554244718281902)
XLA Ops:
  19.5 4.0 collective-permute-start.2
  25.0 6.1 fusion.22
  31.9 5.8 collective-permute-done.1
  47.4 19.8 %collective-permute-done.4 = bf16[320,1600]{1,0:T(8,128)(2,1)S(1)} collective-permute-done((bf16[320,1600]{1,0:T(8,128)(2,1)S(1)}, bf16[320,1600]{1,0:T(8,128)(2,1)S(1)}, u32[]{:S(2)}, u32[]{:S(2)}) %collective-permute-start.4) | collective-permute-done | bytes 1024032 | tf_op jit(solution)/shard_map/ppermute | solution.py:608
  71.2 9.3 %collective-permute-done.5 = bf16[160,1600]{1,0:T(8,128)(2,1)S(1)} collective-permute-done((bf16[160,1600]{1,0:T(8,128)(2,1)S(1)}, bf16[160,1600]{1,0:T(8,128)(2,1)S(1)}, u32[]{:S(2)}, u32[]{:S(2)}) %collective-permute-start.5) | collective-permute-done | bytes 512032 | tf_op jit(solution)/shard_map/ppermute | solution.py:609
  101.3 8.8 %all-gather.7.cloned.1.call-done = bf16[1600,1088]{1,0:T(8,128)(2,1)} async-done(((bf16[200,1088]{1,0:T(8,128)(2,1)}), bf16[1600,1088]{1,0:T(8,128)(2,1)}) %all-gather.7.cloned.1.call-update) | async-done | bytes 3481616 | tf_op jit(solution)/shard_map/all_gather | solution.py:743
  110.2 6.3 copy.89
  116.5 10.2 %fusion.130.kv_ref.q_ref = f32[17,64,1280]{2,1,0:T(8,128)} fusion(bf16[17,64,1600]{2,1,0:T(8,128)(2,1)} %bitcast.267, bf16[1280,1600,1]{1,0,2:T(8,128)(2,1)} %bitcast.18), kind=kOutput, calls=%fused_computation.325 | convolution fusion | flops 4456448000 | bytes 13148160 | tf_op jit(solution)/shard_map/dot_general | solution.py:64
  126.7 25.8 %attn_fwd.1 = (bf16[4,7,64,320]{3,2,1,0:T(8,128)(2,1)}, bf16[7,64,1280]{2,1,0:T(8,128)(2,1)S(1)}, bf16[5,64,1280]{2,1,0:T(8,128)(2,1)S(1)}, bf16[5,1280,64]{2,1,0:T(8,128)(2,1)}, bf16[5,1280,64]{2,1,0:T(8,128)(2,1)}) custom-call(s32[11]{0:T(128)S(1)} %pad_add_fusion.3.kvmap, f32[17,64,1280]{2,1,0:T(8,128)} %fusion.130.kv_ref.q_ref, ...), custom_call_target="tpu_custom_call" | custom-call | flops 1638400 | bytes 81920 | tf_op jit(solution)/shard_map/attn_fwd/pallas_call | solution.py:153
  160.3 3.9 reshape.456
  164.2 4.5 fusion.23
  173.1 4.7 convolution_convert_fusion.9
  184.2 13.9 %fusion.131.p_ref = f32[1728,1280]{1,0:T(8,128)} fusion(bf16[1600,1728]{1,0:T(8,128)(2,1)} %all-gather.9.cloned.1.call-done, bf16[1280,1600]{1,0:T(8,128)(2,1)} %bitcast.17), kind=kOutput, calls=%fused_computation.326 | convolution fusion | flops 7077888000 | bytes 18472960 | tf_op jit(solution)/shard_map/dot_general | solution.py:64
  198.1 8.0 collective-permute-done.14
  206.2 14.1 %ssm_fwd.1 = (f32[832,1280]{1,0:T(8,128)}, bf16[832,1280]{1,0:T(8,128)(2,1)S(1)}, f32[10,832,16]{2,1,0:T(8,128)}) custom-call(f32[1728,1280]{1,0:T(8,128)} %fusion.131.p_ref, f32[16,1]{1,0:T(8,128)S(1)} %copy.94.bias, f32[16,1]{1,0:T(8,128)S(1)} %copy.95.decay, f32[8,1280]{1,0:T(8,128)S(1)} %pad_convert_fusion.marks, ...), custom_call_target="tpu_custom_call" | custom-call | flops 1638400 | bytes 81920 | tf_op jit(solution)/shard_map/ssm_fwd/pallas_call | solution.py:338
  224.0 7.1 convolution_convert_fusion.6
  233.2 4.2 collective-permute-done.20
  247.3 12.4 %convolution_convert_fusion.5.g_ref = bf16[1280,1408]{1,0:T(8,128)(2,1)} fusion(bf16[1408,1600]{1,0:T(8,128)(2,1)} %all-gather.11.cloned.1.call-done, bf16[320,1600]{1,0:T(8,128)(2,1)} %collective-permute-done.15, bf16[320,1600]{1,0:T(8,128)(2,1)} %collective-permute-done.14, bf16[320,1600]{1,0:T(8,128)(2,1)} %collective-permute-done.13, ...), kind=kOutput, calls=%fused_computation.19 | convolution fusion | flops 5785354240 | bytes 12206080 | tf_op jit(solution)/shard_map/dot_general | solution.py:64
  271.9 21.4 %collective-permute-done.17 = bf16[320,1600]{1,0:T(8,128)(2,1)} collective-permute-done((bf16[320,1600]{1,0:T(8,128)(2,1)}, bf16[320,1600]{1,0:T(8,128)(2,1)}, u32[]{:S(2)}, u32[]{:S(2)}) %collective-permute-start.17) | collective-permute-done | bytes 1024032 | tf_op jit(solution)/shard_map/ppermute | solution.py:600
  301.3 23.2 %collective-permute-done.23 = bf16[320,1600]{1,0:T(8,128)(2,1)S(1)} collective-permute-done((bf16[320,1600]{1,0:T(8,128)(2,1)S(1)}, bf16[320,1600]{1,0:T(8,128)(2,1)S(1)}, u32[]{:S(2)}, u32[]{:S(2)}) %collective-permute-start.23) | collective-permute-done | bytes 1024032 | tf_op jit(solution)/shard_map/ppermute | solution.py:608
  329.1 8.8 %collective-permute-done.24 = bf16[160,1600]{1,0:T(8,128)(2,1)S(1)} collective-permute-done((bf16[160,1600]{1,0:T(8,128)(2,1)S(1)}, bf16[160,1600]{1,0:T(8,128)(2,1)S(1)}, u32[]{:S(2)}, u32[]{:S(2)}) %collective-permute-start.24) | collective-permute-done | bytes 512032 | tf_op jit(solution)/shard_map/ppermute | solution.py:609
  339.6 19.4 %convolution_convert_fusion.1.gate_up_ref = bf16[1280,2816]{1,0:T(8,128)(2,1)} fusion(bf16[1280,1600]{1,0:T(8,128)(2,1)} %constant_dynamic-update-slice_fusion.rows_ref, bf16[1600,2816]{1,0:T(8,128)(2,1)} %all-gather.13.cloned.1.call-done), kind=kOutput, calls=%fused_computation.1 | convolution fusion | flops 11537940480 | bytes 20316160 | tf_op jit(solution)/shard_map/dot_general | solution.py:64
  359.1 11.5 %ffn_middle.1 = (bf16[1280,1408]{1,0:T(8,128)(2,1)S(1)}, bf16[1280,2816]{1,0:T(8,128)(2,1)}) custom-call(bf16[1280,2816]{1,0:T(8,128)(2,1)} %convolution_convert_fusion.1.gate_up_ref, bf16[1280,1408]{1,0:T(8,128)(2,1)} %convolution_convert_fusion.5.g_ref), custom_call_target="tpu_custom_call" | custom-call | tf_op jit(solution)/shard_map/ffn_middle/pallas_call | solution.py:506
  370.6 19.4 %convolution_convert_fusion.4 = bf16[1280,1600]{1,0:T(8,128)(2,1)S(1)} fusion(bf16[1280,2816]{1,0:T(8,128)(2,1)} %get-tuple-element.178.g_ref, bf16[1600,2816]{1,0:T(8,128)(2,1)} %all-gather.13.cloned.1.call-done), kind=kOutput, calls=%fused_computation.18 | convolution fusion | flops 11536384000 | bytes 20316160 | tf_op jit(solution)/shard_map/dot_general | solution.py:64
  394.7 7.8 pad_maximum_fusion.cot_ref
  402.5 30.3 %ffn_weight_grads.1 = (bf16[1600,2816]{1,0:T(8,128)(2,1)}, bf16[1408,1600]{1,0:T(8,128)(2,1)}) custom-call(bf16[1280,1600]{1,0:T(8,128)(2,1)} %constant_dynamic-update-slice_fusion.rows_ref, bf16[1280,2816]{1,0:T(8,128)(2,1)} %get-tuple-element.178.g_ref, bf16[1280,1408]{1,0:T(8,128)(2,1)S(1)} %get-tuple-element.187.hidden_ref, ...), custom_call_target="tpu_custom_call" | custom-call | flops 1638400 | bytes 1280 | tf_op jit(solution)/shard_map/ffn_weight_grads/pallas_call | solution.py:550
  432.8 6.4 collective-permute-done.28
  441.6 4.5 multiply_reduce_fusion
  446.1 5.8 multiply_reduce_fusion.1
  460.1 3.3 convolution_convert_fusion.3
  463.5 7.5 convolution_convert_fusion.2
  478.9 39.7 %attn_bwd.1 = bf16[17,64,1280]{2,1,0:T(8,128)(2,1)} custom-call(s32[11]{0:T(128)S(1)} %pad_add_fusion.3.kvmap, bf16[4,7,64,320]{3,2,1,0:T(8,128)(2,1)} %pad_maximum_fusion.1.refs_0_.refs_1_.refs_2_.refs_3_, bf16[4,7,64,320]{3,2,1,0:T(8,128)(2,1)} %pad_maximum_fusion.1.refs_0_.refs_1_.refs_2_.refs_3_, ...), custom_call_target="tpu_custom_call" | custom-call | flops 1638400 | bytes 81920 | tf_op jit(solution)/shard_map/attn_bwd/pallas_call | solution.py:242
  531.2 13.8 %convolution_convert_fusion.7 = bf16[832,1600]{1,0:T(8,128)(2,1)} fusion(s32[832]{0:T(1024)S(1)} %copy-done.55, bf16[832,1280]{1,0:T(8,128)(2,1)S(1)} %copy-done.5, bf16[1280,1600]{1,0:T(8,128)(2,1)} %bitcast.70), kind=kOutput, calls=%fused_computation.39 | convolution fusion | flops 5626343424 | bytes 8891648 | tf_op jit(solution)/shard_map/dot_general | solution.py:64
  545.0 9.3 %fusion.132.up_ref = f32[832,1280]{1,0:T(8,128)} fusion(bf16[832,1600]{1,0:T(8,128)(2,1)} %convolution_convert_fusion.9, bf16[1280,1600]{1,0:T(8,128)(2,1)} %bitcast.70), kind=kOutput, calls=%fused_computation.327 | convolution fusion | flops 3407872000 | bytes 11018240 | tf_op jit(solution)/shard_map/dot_general | solution.py:64
  554.3 26.9 %ssm_bwd.1 = (bf16[1728,1280]{1,0:T(8,128)(2,1)}, f32[48,128]{1,0:T(8,128)S(1)}) custom-call(f32[1728,1280]{1,0:T(8,128)} %fusion.131.p_ref, f32[16,1]{1,0:T(8,128)S(1)} %copy.94.bias, f32[16,1]{1,0:T(8,128)S(1)} %copy.95.decay, f32[8,1280]{1,0:T(8,128)S(1)} %pad_convert_fusion.marks, f32[1280,1]{1,0:T(8,128)S(1)} %reshape_convert_fusion.seg_col, ...), custom_call_target="tpu_custom_call" | custom-call | flops 1638400 | bytes 81920 | tf_op jit(solution)/shard_map/ssm_bwd/pallas_call | solution.py:466
  581.2 7.2 reduce-scatter.5.cloned.1.call-done
  588.5 19.3 %convolution_convert_fusion = bf16[1600,2816]{1,0:T(8,128)(2,1)} fusion(bf16[1280,1600]{1,0:T(8,128)(2,1)} %bitcast.17, bf16[1728,1280]{1,0:T(8,128)(2,1)} %get-tuple-element.221, bf16[1088,1280]{1,0:T(8,128)(2,1)} %bitcast.268), kind=kOutput, calls=%fused_computation | convolution fusion | flops 11553259520 | bytes 20316160 | tf_op jit(solution)/shard_map/dot_general | solution.py:64
  611.5 28.8 %collective-permute-done.44 = bf16[400,1600]{1,0:T(8,128)(2,1)S(1)} collective-permute-done((bf16[400,1600]{1,0:T(8,128)(2,1)}, bf16[400,1600]{1,0:T(8,128)(2,1)S(1)}, u32[]{:S(2)}, u32[]{:S(2)}) %collective-permute-start.44) | collective-permute-done | bytes 1280032 | tf_op jit(solution)/shard_map/ppermute | solution.py:600
  640.3 26.4 %collective-permute-done.45 = bf16[400,1600]{1,0:T(8,128)(2,1)S(1)} collective-permute-done((bf16[400,1600]{1,0:T(8,128)(2,1)}, bf16[400,1600]{1,0:T(8,128)(2,1)S(1)}, u32[]{:S(2)}, u32[]{:S(2)}) %collective-permute-start.45) | collective-permute-done | bytes 1280032 | tf_op jit(solution)/shard_map/ppermute | solution.py:600
  670.2 3.6 fusion.19
  675.6 10.6 %fusion.133 = f32[1280,1600]{1,0:T(8,128)} fusion(bf16[1088,1280]{1,0:T(8,128)(2,1)S(1)} %bitcast.269, bf16[1600,1088]{1,0:T(8,128)(2,1)} %all-gather.7.cloned.1.call-done), kind=kOutput, calls=%fused_computation.328 | convolution fusion | flops 4456448000 | bytes 14458880 | tf_op jit(solution)/shard_map/dot_general | solution.py:64
  686.3 13.1 %fusion.9 = bf16[1280,1600]{1,0:T(8,128)(2,1)S(1)} fusion(f32[1280,1600]{1,0:T(8,128)} %fusion.133, bf16[1728,1280]{1,0:T(8,128)(2,1)S(1)} %bitcast.291, bf16[1600,1728]{1,0:T(8,128)(2,1)} %all-gather.9.cloned.1.call-done), kind=kOutput, calls=%fused_computation.15 | convolution fusion | flops 7081984000 | bytes 22241280 | tf_op jit(solution)/shard_map/dot_general | solution.py:64
  709.6 6.5 fusion.26
  716.1 13.0 %collective-permute-done.38 = bf16[320,1600]{1,0:T(8,128)(2,1)S(1)} collective-permute-done((bf16[320,1600]{1,0:T(8,128)(2,1)}, bf16[320,1600]{1,0:T(8,128)(2,1)S(1)}, u32[]{:S(2)}, u32[]{:S(2)}) %collective-permute-start.38) | collective-permute-done | bytes 1024032 | tf_op jit(solution)/shard_map/ppermute | solution.py:600
  729.0 18.6 %collective-permute-done.40 = bf16[320,1600]{1,0:T(8,128)(2,1)} collective-permute-done((bf16[320,1600]{1,0:T(8,128)(2,1)}, bf16[320,1600]{1,0:T(8,128)(2,1)}, u32[]{:S(2)}, u32[]{:S(2)}) %collective-permute-start.40) | collective-permute-done | bytes 1024032 | tf_op jit(solution)/shard_map/ppermute | solution.py:600
  749.0 4.2 fusion.43
  768.5 5.6 collective-permute-start.50
  778.3 8.6 %fusion.2 = f32[320,1600]{1,0:T(8,128)} fusion(s32[1600]{0:T(1024)S(1)} %copy-done.50, f32[320,1600]{1,0:T(8,128)S(1)} %copy-done.18, f32[320,1600]{1,0:T(8,128)} %get-tuple-element.251, f32[320]{0:T(512)S(1)} %broadcast_multiply_fusion.2, f32[1600]{0:T(1024)S(1)} %copy-done.40, f32[320]{0:T(512)S(1)} %copy-done.48, bf16[640,1600]{1,0:T(8,128)(2,1)S(1)} %copy-done.15), kind=kOutput, calls=%fused_computation.5 | convolution fusion | flops 4922368000 | bytes 7311360 | tf_op jit(solution)/shard_map/dot_general | solution.py:64
  (484 shorter events, 218.1 us)
Async XLA Ops:
  7.2 82.7 %all-gather.15.cloned.1.call-start = ((), (), s32[]{:S(2)}) async-start(), calls=%async_computation.12 | async-start | bytes 4792320 | tf_op jit(solution)/shard_map/all_gather | solution.py:787
  15.8 94.4 %all-gather.7.cloned.1.call-start = ((), (), s32[]{:S(2)}) async-start(), calls=%async_computation.4 | async-start | bytes 4147200 | tf_op jit(solution)/shard_map/all_gather | solution.py:743
  40.3 143.9 %all-gather.9.cloned.1.call-start = ((), (), s32[]{:S(2)}) async-start(), calls=%async_computation.5 | async-start | bytes 6451200 | tf_op jit(solution)/shard_map/all_gather | solution.py:743
  41.9 205.4 %all-gather.11.cloned.1.call-start = ((), (), s32[]{:S(2)}) async-start(), calls=%async_computation.6 | async-start | bytes 5271552 | tf_op jit(solution)/shard_map/all_gather | solution.py:885
  42.0 25.2 %collective-permute-start.4 = (bf16[320,1600]{1,0:T(8,128)(2,1)S(1)}, bf16[320,1600]{1,0:T(8,128)(2,1)S(1)}, u32[]{:S(2)}, u32[]{:S(2)}) collective-permute-start(bf16[320,1600]{1,0:T(8,128)(2,1)S(1)} %fusion.34), channel_id=1, source_target_pairs={{0,16},{8,24},{16,0},{24,8},{1,17},{9,25},{17,1},{25,9},{2,18},{10... | collective-permute-start | bytes 3072008 | tf_op jit(solution)/shard_map/ppermute | solution.py:608
  43.4 25.6 %collective-permute-start.3 = (bf16[320,1600]{1,0:T(8,128)(2,1)S(1)}, bf16[320,1600]{1,0:T(8,128)(2,1)}, u32[]{:S(2)}, u32[]{:S(2)}) collective-permute-start(bf16[320,1600]{1,0:T(8,128)(2,1)S(1)} %fusion.34), channel_id=1, source_target_pairs={{0,8},{8,0},{16,24},{24,16},{1,9},{9,1},{17,25},{25,17},{2,10},{10... | collective-permute-start | bytes 3072008 | tf_op jit(solution)/shard_map/ppermute | solution.py:608
  46.0 293.6 %all-gather.13.cloned.1.call-start = ((), (), s32[]{:S(2)}) async-start(), calls=%async_computation.7 | async-start | bytes 10137600 | tf_op jit(solution)/shard_map/all_gather | solution.py:743
  93.1 59.5 %collective-permute-start.9 = (bf16[400,1600]{1,0:T(8,128)(2,1)}, bf16[400,1600]{1,0:T(8,128)(2,1)}, u32[]{:S(2)}, u32[]{:S(2)}) collective-permute-start(bf16[400,1600]{1,0:T(8,128)(2,1)} %reshape.454), channel_id=1, source_target_pairs={{0,24},{8,16},{16,8},{24,0},{1,25},{9,17},{17,9},{25,1},{2,26},{10... | collective-permute-start | bytes 3840008 | tf_op jit(solution)/shard_map/ppermute | solution.py:600
  94.8 57.8 %collective-permute-start.8 = (bf16[400,1600]{1,0:T(8,128)(2,1)}, bf16[400,1600]{1,0:T(8,128)(2,1)}, u32[]{:S(2)}, u32[]{:S(2)}) collective-permute-start(bf16[400,1600]{1,0:T(8,128)(2,1)} %reshape.454), channel_id=1, source_target_pairs={{0,16},{8,24},{16,0},{24,8},{1,17},{9,25},{17,1},{25,9},{2,18},{10... | collective-permute-start | bytes 3840008 | tf_op jit(solution)/shard_map/ppermute | solution.py:600
  95.0 57.6 %collective-permute-start.7 = (bf16[400,1600]{1,0:T(8,128)(2,1)}, bf16[400,1600]{1,0:T(8,128)(2,1)}, u32[]{:S(2)}, u32[]{:S(2)}) collective-permute-start(bf16[400,1600]{1,0:T(8,128)(2,1)} %reshape.454), channel_id=1, source_target_pairs={{0,8},{8,0},{16,24},{24,16},{1,9},{9,1},{17,25},{25,17},{2,10},{10... | collective-permute-start | bytes 3840008 | tf_op jit(solution)/shard_map/ppermute | solution.py:600
  155.3 27.0 %collective-permute-start.15 = (bf16[320,1600]{1,0:T(8,128)(2,1)}, bf16[320,1600]{1,0:T(8,128)(2,1)}, u32[]{:S(2)}, u32[]{:S(2)}) collective-permute-start(bf16[320,1600]{1,0:T(8,128)(2,1)} %slice.404), channel_id=1, source_target_pairs={{0,24},{8,16},{16,8},{24,0},{1,25},{9,17},{17,9},{25,1},{2,26},{10... | collective-permute-start | bytes 3072008 | tf_op jit(solution)/shard_map/ppermute | solution.py:600
  177.8 28.3 %collective-permute-start.14 = (bf16[320,1600]{1,0:T(8,128)(2,1)}, bf16[320,1600]{1,0:T(8,128)(2,1)}, u32[]{:S(2)}, u32[]{:S(2)}) collective-permute-start(bf16[320,1600]{1,0:T(8,128)(2,1)} %slice.404), channel_id=1, source_target_pairs={{0,16},{8,24},{16,0},{24,8},{1,17},{9,25},{17,1},{25,9},{2,18},{10... | collective-permute-start | bytes 3072008 | tf_op jit(solution)/shard_map/ppermute | solution.py:600
  178.5 27.7 %collective-permute-start.13 = (bf16[320,1600]{1,0:T(8,128)(2,1)}, bf16[320,1600]{1,0:T(8,128)(2,1)}, u32[]{:S(2)}, u32[]{:S(2)}) collective-permute-start(bf16[320,1600]{1,0:T(8,128)(2,1)} %slice.404), channel_id=1, source_target_pairs={{0,8},{8,0},{16,24},{24,16},{1,9},{9,1},{17,25},{25,17},{2,10},{10... | collective-permute-start | bytes 3072008 | tf_op jit(solution)/shard_map/ppermute | solution.py:600
  179.1 41.2 %collective-permute-start.12 = (bf16[448,320]{1,0:T(8,128)(2,1)}, bf16[448,320]{1,0:T(8,128)(2,1)}, u32[]{:S(2)}, u32[]{:S(2)}) collective-permute-start(bf16[448,320]{1,0:T(8,128)(2,1)} %get-tuple-element.284), channel_id=1, source_target_pairs={{0,24},{8,16},{16,8},{24,0},{1,25},{9,17},{17,9},{25,1},{2,26},{10... | collective-permute-start | bytes 860168 | tf_op jit(solution)/shard_map/ppermute | solution.py:600
  181.3 38.9 %collective-permute-start.11 = (bf16[448,320]{1,0:T(8,128)(2,1)S(1)}, bf16[448,320]{1,0:T(8,128)(2,1)}, u32[]{:S(2)}, u32[]{:S(2)}) collective-permute-start(bf16[448,320]{1,0:T(8,128)(2,1)S(1)} %copy-done.35), channel_id=1, source_target_pairs={{0,16},{8,24},{16,0},{24,8},{1,17},{9,25},{17,1},{25,9},{2,18},{10... | collective-permute-start | bytes 860168 | tf_op jit(solution)/shard_map/ppermute | solution.py:600
  182.3 38.0 %collective-permute-start.10 = (bf16[448,320]{1,0:T(8,128)(2,1)S(1)}, bf16[448,320]{1,0:T(8,128)(2,1)}, u32[]{:S(2)}, u32[]{:S(2)}) collective-permute-start(bf16[448,320]{1,0:T(8,128)(2,1)S(1)} %copy-done.34), channel_id=1, source_target_pairs={{0,8},{8,0},{16,24},{24,16},{1,9},{9,1},{17,25},{25,17},{2,10},{10... | collective-permute-start | bytes 860168 | tf_op jit(solution)/shard_map/ppermute | solution.py:600
  243.3 337.9 %reduce-scatter.7.cloned.1.call-start = ((), (), s32[]{:S(2)}) async-start(), calls=%async_computation.9 | async-start | bytes 5271552 | tf_op jit(solution)/shard_map/reduce_scatter | solution.py:922
  243.7 28.1 %collective-permute-start.18 = (bf16[320,1600]{1,0:T(8,128)(2,1)}, bf16[320,1600]{1,0:T(8,128)(2,1)}, u32[]{:S(2)}, u32[]{:S(2)}) collective-permute-start(bf16[320,1600]{1,0:T(8,128)(2,1)} %get-tuple-element.274), channel_id=1, source_target_pairs={{0,24},{8,16},{16,8},{24,0},{1,25},{9,17},{17,9},{25,1},{2,26},{10... | collective-permute-start | bytes 3072008 | tf_op jit(solution)/shard_map/ppermute | solution.py:600
  245.6 47.7 %collective-permute-start.17 = (bf16[320,1600]{1,0:T(8,128)(2,1)}, bf16[320,1600]{1,0:T(8,128)(2,1)}, u32[]{:S(2)}, u32[]{:S(2)}) collective-permute-start(bf16[320,1600]{1,0:T(8,128)(2,1)} %get-tuple-element.275), channel_id=1, source_target_pairs={{0,16},{8,24},{16,0},{24,8},{1,17},{9,25},{17,1},{25,9},{2,18},{10... | collective-permute-start | bytes 3072008 | tf_op jit(solution)/shard_map/ppermute | solution.py:600
  246.3 47.0 %collective-permute-start.16 = (bf16[320,1600]{1,0:T(8,128)(2,1)}, bf16[320,1600]{1,0:T(8,128)(2,1)}, u32[]{:S(2)}, u32[]{:S(2)}) collective-permute-start(bf16[320,1600]{1,0:T(8,128)(2,1)} %get-tuple-element.276), channel_id=1, source_target_pairs={{0,8},{8,0},{16,24},{24,16},{1,9},{9,1},{17,25},{25,17},{2,10},{10... | collective-permute-start | bytes 3072008 | tf_op jit(solution)/shard_map/ppermute | solution.py:600
  299.0 25.5 %collective-permute-start.23 = (bf16[320,1600]{1,0:T(8,128)(2,1)S(1)}, bf16[320,1600]{1,0:T(8,128)(2,1)S(1)}, u32[]{:S(2)}, u32[]{:S(2)}) collective-permute-start(bf16[320,1600]{1,0:T(8,128)(2,1)S(1)} %get-tuple-element.254), channel_id=1, source_target_pairs={{0,16},{8,24},{16,0},{24,8},{1,17},{9,25},{17,1},{25,9},{2,18},{10... | collective-permute-start | bytes 3072008 | tf_op jit(solution)/shard_map/ppermute | solution.py:608
  300.0 25.5 %collective-permute-start.22 = (bf16[320,1600]{1,0:T(8,128)(2,1)S(1)}, bf16[320,1600]{1,0:T(8,128)(2,1)S(1)}, u32[]{:S(2)}, u32[]{:S(2)}) collective-permute-start(bf16[320,1600]{1,0:T(8,128)(2,1)S(1)} %get-tuple-element.254), channel_id=1, source_target_pairs={{0,8},{8,0},{16,24},{24,16},{1,9},{9,1},{17,25},{25,17},{2,10},{10... | collective-permute-start | bytes 3072008 | tf_op jit(solution)/shard_map/ppermute | solution.py:608
  391.2 41.5 %collective-permute-start.27 = (bf16[320,1600]{1,0:T(8,128)(2,1)S(1)}, bf16[320,1600]{1,0:T(8,128)(2,1)}, u32[]{:S(2)}, u32[]{:S(2)}) collective-permute-start(bf16[320,1600]{1,0:T(8,128)(2,1)S(1)} %get-tuple-element.270), channel_id=1, source_target_pairs={{0,16},{8,24},{16,0},{24,8},{1,17},{9,25},{17,1},{25,9},{2,18},{10... | collective-permute-start | bytes 3072008 | tf_op jit(solution)/shard_map/ppermute | solution.py:600
  392.4 40.3 %collective-permute-start.26 = (bf16[320,1600]{1,0:T(8,128)(2,1)S(1)}, bf16[320,1600]{1,0:T(8,128)(2,1)}, u32[]{:S(2)}, u32[]{:S(2)}) collective-permute-start(bf16[320,1600]{1,0:T(8,128)(2,1)S(1)} %get-tuple-element.271), channel_id=1, source_target_pairs={{0,8},{8,0},{16,24},{24,16},{1,9},{9,1},{17,25},{25,17},{2,10},{10... | collective-permute-start | bytes 3072008 | tf_op jit(solution)/shard_map/ppermute | solution.py:600
  393.4 45.7 %collective-permute-start.28 = (bf16[320,1600]{1,0:T(8,128)(2,1)S(1)}, bf16[320,1600]{1,0:T(8,128)(2,1)}, u32[]{:S(2)}, u32[]{:S(2)}) collective-permute-start(bf16[320,1600]{1,0:T(8,128)(2,1)S(1)} %get-tuple-element.272), channel_id=1, source_target_pairs={{0,24},{8,16},{16,8},{24,0},{1,25},{9,17},{17,9},{25,1},{2,26},{10... | collective-permute-start | bytes 3072008 | tf_op jit(solution)/shard_map/ppermute | solution.py:600
  439.2 149.3 %reduce-scatter.5.cloned.1.call-start = ((), (), s32[]{:S(2)}) async-start(), calls=%async_computation.8 | async-start | bytes 10137600 | tf_op jit(solution)/shard_map/reduce_scatter | solution.py:922
  439.9 289.1 %reduce-scatter.9.cloned.1.call-start = ((), (), s32[]{:S(2)}) async-start(), calls=%async_computation.10 | async-start | bytes 10137600 | tf_op jit(solution)/shard_map/reduce_scatter | solution.py:922
  456.6 17.3 %collective-permute-start.31 = (bf16[7,64,320]{2,1,0:T(8,128)(2,1)S(1)}, bf16[7,64,320]{2,1,0:T(8,128)(2,1)S(1)}, u32[]{:S(2)}, u32[]{:S(2)}) collective-permute-start(bf16[7,64,320]{2,1,0:T(8,128)(2,1)S(1)} %get-tuple-element.280), channel_id=1, source_target_pairs={{0,24},{8,16},{16,8},{24,0},{1,25},{9,17},{17,9},{25,1},{2,26},{10... | collective-permute-start | bytes 860168 | tf_op jit(solution)/shard_map/ppermute | solution.py:600
  458.1 15.8 %collective-permute-start.30 = (bf16[7,64,320]{2,1,0:T(8,128)(2,1)S(1)}, bf16[7,64,320]{2,1,0:T(8,128)(2,1)S(1)}, u32[]{:S(2)}, u32[]{:S(2)}) collective-permute-start(bf16[7,64,320]{2,1,0:T(8,128)(2,1)S(1)} %get-tuple-element.281), channel_id=1, source_target_pairs={{0,16},{8,24},{16,0},{24,8},{1,17},{9,25},{17,1},{25,9},{2,18},{10... | collective-permute-start | bytes 860168 | tf_op jit(solution)/shard_map/ppermute | solution.py:600
  458.8 15.1 %collective-permute-start.29 = (bf16[7,64,320]{2,1,0:T(8,128)(2,1)S(1)}, bf16[7,64,320]{2,1,0:T(8,128)(2,1)S(1)}, u32[]{:S(2)}, u32[]{:S(2)}) collective-permute-start(bf16[7,64,320]{2,1,0:T(8,128)(2,1)S(1)} %get-tuple-element.282), channel_id=1, source_target_pairs={{0,8},{8,0},{16,24},{24,16},{1,9},{9,1},{17,25},{25,17},{2,10},{10... | collective-permute-start | bytes 860168 | tf_op jit(solution)/shard_map/ppermute | solution.py:600
  473.9 44.7 %collective-permute-start.34 = (bf16[320,1600]{1,0:T(8,128)(2,1)S(1)}, bf16[320,1600]{1,0:T(8,128)(2,1)S(1)}, u32[]{:S(2)}, u32[]{:S(2)}) collective-permute-start(bf16[320,1600]{1,0:T(8,128)(2,1)S(1)} %get-tuple-element.191), channel_id=1, source_target_pairs={{0,24},{8,16},{16,8},{24,0},{1,25},{9,17},{17,9},{25,1},{2,26},{10... | collective-permute-start | bytes 3072008 | tf_op jit(solution)/shard_map/ppermute | solution.py:600
  475.4 45.0 %collective-permute-start.33 = (bf16[320,1600]{1,0:T(8,128)(2,1)S(1)}, bf16[320,1600]{1,0:T(8,128)(2,1)S(1)}, u32[]{:S(2)}, u32[]{:S(2)}) collective-permute-start(bf16[320,1600]{1,0:T(8,128)(2,1)S(1)} %get-tuple-element.191), channel_id=1, source_target_pairs={{0,16},{8,24},{16,0},{24,8},{1,17},{9,25},{17,1},{25,9},{2,18},{10... | collective-permute-start | bytes 3072008 | tf_op jit(solution)/shard_map/ppermute | solution.py:600
  476.1 44.3 %collective-permute-start.32 = (bf16[320,1600]{1,0:T(8,128)(2,1)S(1)}, bf16[320,1600]{1,0:T(8,128)(2,1)S(1)}, u32[]{:S(2)}, u32[]{:S(2)}) collective-permute-start(bf16[320,1600]{1,0:T(8,128)(2,1)S(1)} %get-tuple-element.191), channel_id=1, source_target_pairs={{0,8},{8,0},{16,24},{24,16},{1,9},{9,1},{17,25},{25,17},{2,10},{10... | collective-permute-start | bytes 3072008 | tf_op jit(solution)/shard_map/ppermute | solution.py:600
  522.2 59.0 %collective-permute-start.37 = (bf16[320,1600]{1,0:T(8,128)(2,1)}, bf16[320,1600]{1,0:T(8,128)(2,1)}, u32[]{:S(2)}, u32[]{:S(2)}) collective-permute-start(bf16[320,1600]{1,0:T(8,128)(2,1)} %get-tuple-element.266), channel_id=1, source_target_pairs={{0,24},{8,16},{16,8},{24,0},{1,25},{9,17},{17,9},{25,1},{2,26},{10... | collective-permute-start | bytes 3072008 | tf_op jit(solution)/shard_map/ppermute | solution.py:600
  524.0 57.2 %collective-permute-start.36 = (bf16[320,1600]{1,0:T(8,128)(2,1)}, bf16[320,1600]{1,0:T(8,128)(2,1)}, u32[]{:S(2)}, u32[]{:S(2)}) collective-permute-start(bf16[320,1600]{1,0:T(8,128)(2,1)} %get-tuple-element.267), channel_id=1, source_target_pairs={{0,16},{8,24},{16,0},{24,8},{1,17},{9,25},{17,1},{25,9},{2,18},{10... | collective-permute-start | bytes 3072008 | tf_op jit(solution)/shard_map/ppermute | solution.py:600
  524.8 56.4 %collective-permute-start.35 = (bf16[320,1600]{1,0:T(8,128)(2,1)}, bf16[320,1600]{1,0:T(8,128)(2,1)}, u32[]{:S(2)}, u32[]{:S(2)}) collective-permute-start(bf16[320,1600]{1,0:T(8,128)(2,1)} %get-tuple-element.268), channel_id=1, source_target_pairs={{0,8},{8,0},{16,24},{24,16},{1,9},{9,1},{17,25},{25,17},{2,10},{10... | collective-permute-start | bytes 3072008 | tf_op jit(solution)/shard_map/ppermute | solution.py:600
  607.8 180.5 %reduce-scatter.11.cloned.1.call-start = ((), (), s32[]{:S(2)}) async-start(), calls=%async_computation.11 | async-start | bytes 4792320 | tf_op jit(solution)/shard_map/reduce_scatter | solution.py:922
  607.8 32.4 %collective-permute-start.44 = (bf16[400,1600]{1,0:T(8,128)(2,1)}, bf16[400,1600]{1,0:T(8,128)(2,1)S(1)}, u32[]{:S(2)}, u32[]{:S(2)}) collective-permute-start(bf16[400,1600]{1,0:T(8,128)(2,1)} %get-tuple-element.227), channel_id=1, source_target_pairs={{0,8},{8,0},{16,24},{24,16},{1,9},{9,1},{17,25},{25,17},{2,10},{10... | collective-permute-start | bytes 3840008 | tf_op jit(solution)/shard_map/ppermute | solution.py:600
  609.3 57.3 %collective-permute-start.45 = (bf16[400,1600]{1,0:T(8,128)(2,1)}, bf16[400,1600]{1,0:T(8,128)(2,1)S(1)}, u32[]{:S(2)}, u32[]{:S(2)}) collective-permute-start(bf16[400,1600]{1,0:T(8,128)(2,1)} %get-tuple-element.228), channel_id=1, source_target_pairs={{0,16},{8,24},{16,0},{24,8},{1,17},{9,25},{17,1},{25,9},{2,18},{10... | collective-permute-start | bytes 3840008 | tf_op jit(solution)/shard_map/ppermute | solution.py:600
  610.8 55.8 %collective-permute-start.46 = (bf16[400,1600]{1,0:T(8,128)(2,1)S(1)}, bf16[400,1600]{1,0:T(8,128)(2,1)S(1)}, u32[]{:S(2)}, u32[]{:S(2)}) collective-permute-start(bf16[400,1600]{1,0:T(8,128)(2,1)S(1)} %copy-done.28), channel_id=1, source_target_pairs={{0,24},{8,16},{16,8},{24,0},{1,25},{9,17},{17,9},{25,1},{2,26},{10... | collective-permute-start | bytes 3840008 | tf_op jit(solution)/shard_map/ppermute | solution.py:600
  702.4 26.7 %collective-permute-start.38 = (bf16[320,1600]{1,0:T(8,128)(2,1)}, bf16[320,1600]{1,0:T(8,128)(2,1)S(1)}, u32[]{:S(2)}, u32[]{:S(2)}) collective-permute-start(bf16[320,1600]{1,0:T(8,128)(2,1)} %get-tuple-element.263), channel_id=1, source_target_pairs={{0,8},{8,0},{16,24},{24,16},{1,9},{9,1},{17,25},{25,17},{2,10},{10... | collective-permute-start | bytes 3072008 | tf_op jit(solution)/shard_map/ppermute | solution.py:600
  703.6 44.1 %collective-permute-start.40 = (bf16[320,1600]{1,0:T(8,128)(2,1)}, bf16[320,1600]{1,0:T(8,128)(2,1)}, u32[]{:S(2)}, u32[]{:S(2)}) collective-permute-start(bf16[320,1600]{1,0:T(8,128)(2,1)} %get-tuple-element.264), channel_id=1, source_target_pairs={{0,24},{8,16},{16,8},{24,0},{1,25},{9,17},{17,9},{25,1},{2,26},{10... | collective-permute-start | bytes 3072008 | tf_op jit(solution)/shard_map/ppermute | solution.py:600
  705.3 43.7 %collective-permute-start.39 = (bf16[320,1600]{1,0:T(8,128)(2,1)}, bf16[320,1600]{1,0:T(8,128)(2,1)}, u32[]{:S(2)}, u32[]{:S(2)}) collective-permute-start(bf16[320,1600]{1,0:T(8,128)(2,1)} %get-tuple-element.265), channel_id=1, source_target_pairs={{0,16},{8,24},{16,0},{24,8},{1,17},{9,25},{17,1},{25,9},{2,18},{10... | collective-permute-start | bytes 3072008 | tf_op jit(solution)/shard_map/ppermute | solution.py:600
  763.3 34.7 %collective-permute-start.43 = (bf16[50,2816]{1,0:T(8,128)(2,1)}, bf16[50,2816]{1,0:T(8,128)(2,1)}, u32[]{:S(2)}, u32[]{:S(2)}) collective-permute-start(bf16[50,2816]{1,0:T(8,128)(2,1)} %get-tuple-element.299), channel_id=1, source_target_pairs={{0,24},{8,16},{16,8},{24,0},{1,25},{9,17},{17,9},{25,1},{2,26},{10... | collective-permute-start | bytes 844808 | tf_op jit(solution)/shard_map/ppermute | solution.py:600
  764.9 32.1 %collective-permute-start.42 = (bf16[50,2816]{1,0:T(8,128)(2,1)}, bf16[50,2816]{1,0:T(8,128)(2,1)}, u32[]{:S(2)}, u32[]{:S(2)}) collective-permute-start(bf16[50,2816]{1,0:T(8,128)(2,1)} %get-tuple-element.300), channel_id=1, source_target_pairs={{0,16},{8,24},{16,0},{24,8},{1,17},{9,25},{17,1},{25,9},{2,18},{10... | collective-permute-start | bytes 844808 | tf_op jit(solution)/shard_map/ppermute | solution.py:600
  765.3 29.9 %collective-permute-start.41 = (bf16[50,2816]{1,0:T(8,128)(2,1)}, bf16[50,2816]{1,0:T(8,128)(2,1)}, u32[]{:S(2)}, u32[]{:S(2)}) collective-permute-start(bf16[50,2816]{1,0:T(8,128)(2,1)} %get-tuple-element.301), channel_id=1, source_target_pairs={{0,8},{8,0},{16,24},{24,16},{1,9},{9,1},{17,25},{25,17},{2,10},{10... | collective-permute-start | bytes 844808 | tf_op jit(solution)/shard_map/ppermute | solution.py:600
  775.1 37.5 %collective-permute-start.54 = (bf16[50,2816]{1,0:T(8,128)(2,1)}, bf16[50,2816]{1,0:T(8,128)(2,1)S(1)}, u32[]{:S(2)}, u32[]{:S(2)}) collective-permute-start(bf16[50,2816]{1,0:T(8,128)(2,1)} %get-tuple-element.287), channel_id=1, source_target_pairs={{0,24},{8,16},{16,8},{24,0},{1,25},{9,17},{17,9},{25,1},{2,26},{10... | collective-permute-start | bytes 844808 | tf_op jit(solution)/shard_map/ppermute | solution.py:600
  786.9 17.9 %collective-permute-start.53 = (bf16[50,2816]{1,0:T(8,128)(2,1)}, bf16[50,2816]{1,0:T(8,128)(2,1)}, u32[]{:S(2)}, u32[]{:S(2)}) collective-permute-start(bf16[50,2816]{1,0:T(8,128)(2,1)} %get-tuple-element.288), channel_id=1, source_target_pairs={{0,16},{8,24},{16,0},{24,8},{1,17},{9,25},{17,1},{25,9},{2,18},{10... | collective-permute-start | bytes 844808 | tf_op jit(solution)/shard_map/ppermute | solution.py:600
  (86 other events, 1029.7 us)
Sparse Core Ops, SparseCore 0:
  15.9 50.4 all-gather.14
  68.7 41.4 all-gather.6
  112.4 59.0 all-gather.8
  173.5 50.1 all-gather.10
  243.5 86.9 all-gather.12
  439.3 52.6 reduce-scatter.6
  494.3 94.1 reduce-scatter.4
  607.9 94.0 reduce-scatter.8
  704.3 48.9 reduce-scatter.10
